TPU v7x, 1024 devices: a whole 8x8x8 slice. The times are simulated.
1024 devices in a mesh: gx: 8 (over y), gy: 8 (over x), gz: 16 (over z, core).
Axes of the slice: x: 8, y: 8, z: 8, core: 2. Of those that a mesh axis runs over, the one named last changes fastest.
Arguments:
- basis: float32 [27, 64, 64, 2048], P(None, 'gx', 'gy', 'gz'), may hold values from 0.1 to 1
- perm: float32 [3, 64, 64, 2048], P(None, 'gx', 'gy', 'gz'), may hold values from 0.05 to 5
- storage: float32 [64, 64, 2048], P('gx', 'gy', 'gz'), may hold values from 0.05 to 1
- layer: int32 [64, 64, 2048], P('gx', 'gy', 'gz'), may hold values from 0 to 255, as said below
Outputs:
- smoothed_basis: float32 [27, 64, 64, 2048], P(None, 'gx', 'gy', 'gz')
- coarse_operator: float32 [27, 8, 8, 256], P(None, 'gx', 'gy', 'gz')
Inputs may be any that keep to these rules, and one draw needn't show every extreme that they name: A cell at vertical index z has layer z // 8 or z // 8 + 1; within a column ids never fall with z, and every layer holds at least one cell of every column.
All inputs are finite; a program needn't handle non-finite values.
Results may differ from a plain program's by a relative error of at most 0.0003.
Values sent between devices are 32-bit elements; how exact they have to be, the bound alone decides.
No kernel may reach another device: no remote copies, remote signals or barrier semaphores. Data moves between devices by JAX's collectives and lax.ppermute only.
A program may use at most 64 MiB of HBM per device.

v0:
```python
import jax
import jax.numpy as jnp
from jax import lax
from jax.sharding import PartitionSpec as P

BLOCK = 8
ITERS = 2


relax_weight = 2.0 / 3.0


def extended(block, sides, width):
    for axis, dim in sides:
        count = lax.axis_size(axis)
        forward = [(i, i + 1) for i in range(count - 1)]
        backward = [(target, source) for source, target in forward]
        low = lax.ppermute(
            lax.slice_in_dim(block, block.shape[dim] - width, None, axis=dim), axis, forward
        )
        high = lax.ppermute(lax.slice_in_dim(block, 0, width, axis=dim), axis, backward)
        block = jnp.concatenate([low, block, high], axis=dim)
    return block


def shifted(value, axis, steps):
    count = lax.axis_size(axis)
    leading, last = (max(0, -steps), min(count, count - steps))
    return lax.ppermute(value, axis, [(source, source + steps) for source in range(leading, last)])


def harmonic(first, second):
    total = first + second
    return 2.0 * first * second / jnp.where(total > 0.0, total, 1.0)


def apply_operator(values, perm_pad, storage_pad):
    perm_x = perm_pad[0]
    perm_y = perm_pad[1]
    perm_z = perm_pad[2]
    face_x = harmonic(perm_x[:-1, 1:-1, 1:-1], perm_x[1:, 1:-1, 1:-1])
    face_y = harmonic(perm_y[1:-1, :-1, 1:-1], perm_y[1:-1, 1:, 1:-1])
    face_z = harmonic(perm_z[1:-1, 1:-1, :-1], perm_z[1:-1, 1:-1, 1:])
    diagonal = storage_pad[1:-1, 1:-1, 1:-1] + face_x[:-1] + face_x[1:]
    diagonal = diagonal + face_y[:, :-1] + face_y[:, 1:] + face_z[:, :, :-1] + face_z[:, :, 1:]
    beside = face_x[:-1] * values[..., :-2, 1:-1, 1:-1] + face_x[1:] * values[..., 2:, 1:-1, 1:-1]
    beside = (
        beside
        + face_y[:, :-1] * values[..., 1:-1, :-2, 1:-1]
        + face_y[:, 1:] * values[..., 1:-1, 2:, 1:-1]
    )
    beside = (
        beside
        + face_z[:, :, :-1] * values[..., 1:-1, 1:-1, :-2]
        + face_z[:, :, 1:] * values[..., 1:-1, 1:-1, 2:]
    )
    return (diagonal * values[..., 1:-1, 1:-1, 1:-1] - beside, diagonal)


def lateral_cover(coords, total, blocks):
    lower = (coords + BLOCK // 2) // BLOCK - 1
    upper = lower + 1
    residue = jnp.arange(3, dtype=jnp.int32)[:, None]
    inside = (coords >= 0) & (coords < total)
    hit = (lower >= 0) & (lower % 3 == residue) | (upper < blocks) & (upper % 3 == residue)
    return (hit & inside[None, :]).astype(jnp.float32)


def per_device(basis, perm, storage, layer):
    cells_x, cells_y, cells_z = storage.shape
    total_x = cells_x * lax.axis_size("gx")
    total_y = cells_y * lax.axis_size("gy")
    total_z = cells_z * lax.axis_size("gz")
    blocks_x = total_x // BLOCK
    blocks_y = total_y // BLOCK
    anchor_x = lax.axis_index("gx") * cells_x
    anchor_y = lax.axis_index("gy") * cells_y
    anchor_z = lax.axis_index("gz") * cells_z

    def support_of(layer_part, margin):
        coord_x = anchor_x - margin + jnp.arange(layer_part.shape[0], dtype=jnp.int32)
        coord_y = anchor_y - margin + jnp.arange(layer_part.shape[1], dtype=jnp.int32)
        coord_z = anchor_z - margin + jnp.arange(layer_part.shape[2], dtype=jnp.int32)
        cover_x = lateral_cover(coord_x, total_x, blocks_x)
        cover_y = lateral_cover(coord_y, total_y, blocks_y)
        inside_z = (coord_z >= 0) & (coord_z < total_z)
        residue = jnp.arange(3, dtype=jnp.int32)[:, None, None, None]
        vertical = ((layer_part[None] % 3 == residue) & inside_z[None, None, None, :]).astype(
            jnp.float32
        )
        whole = (
            vertical[:, None, None]
            * cover_y[None, :, None, None, :, None]
            * cover_x[None, None, :, :, None, None]
        )
        return whole.reshape((27,) + layer_part.shape)

    values = support_of(layer, 0) * basis
    perm_pad = extended(perm, (("gx", 1), ("gy", 2), ("gz", 3)), 1)
    storage_pad = jnp.pad(storage, 1)
    for sweep in range(ITERS + 1):
        padded = extended(values, (("gx", 1), ("gy", 2), ("gz", 3)), 1)
        if sweep < ITERS:
            relax_image, relax_diagonal = apply_operator(padded, perm_pad, storage_pad)
            support = support_of(layer, 0)
            centre = padded[:, 1:-1, 1:-1, 1:-1]
            updated = centre - relax_weight * support * relax_image / jnp.where(
                relax_diagonal > 0.0, relax_diagonal, 1.0
            )
            total = jnp.sum(updated, axis=0)
            values = updated / jnp.where(total > 0.0, total, 1.0)
    image, diagonal = apply_operator(padded, perm_pad, storage_pad)
    depth = jnp.arange(cells_z, dtype=jnp.int32)
    rows_here = cells_z // BLOCK
    across_x = cells_x // BLOCK
    across_y = cells_y // BLOCK
    lifted = (layer - (anchor_z + depth)[None, None, :] // BLOCK).astype(jnp.float32)
    grouped = (27, across_x, BLOCK, across_y, BLOCK, rows_here, BLOCK)
    lower = (image * (1.0 - lifted)).reshape(grouped).sum(axis=(2, 4, 6))
    upper = (image * lifted).reshape(grouped).sum(axis=(2, 4, 6))
    partial_value = jnp.pad(lower, ((0, 0), (0, 0), (0, 0), (0, 1))) + jnp.pad(
        upper, ((0, 0), (0, 0), (0, 0), (1, 0))
    )
    first_row = anchor_z // BLOCK
    rows = (first_row + jnp.arange(rows_here + 1, dtype=jnp.int32))[None, None, None, :]
    offsets = jnp.arange(27, dtype=jnp.int32)[:, None, None, None]
    block_x = (anchor_x // BLOCK + jnp.arange(across_x, dtype=jnp.int32))[None, :, None, None]
    block_y = (anchor_y // BLOCK + jnp.arange(across_y, dtype=jnp.int32))[None, None, :, None]
    choose = (
        9 * ((rows + offsets // 9 - 1) % 3)
        + 3 * ((block_y + offsets // 3 % 3 - 1) % 3)
        + (block_x + offsets % 3 - 1) % 3
    )
    picked = jnp.take_along_axis(partial_value, choose, axis=0)
    carried = shifted(picked[:, :, :, rows_here:], "gz", 1)
    summed = picked[:, :, :, :rows_here] + jnp.pad(
        carried, ((0, 0), (0, 0), (0, 0), (0, rows_here - 1))
    )
    coarse = summed * (1.0 / (BLOCK * BLOCK))
    return (values, coarse)


def solution(mesh):
    return jax.shard_map(
        per_device,
        mesh=mesh,
        in_specs=(
            P(None, "gx", "gy", "gz"),
            P(None, "gx", "gy", "gz"),
            P("gx", "gy", "gz"),
            P("gx", "gy", "gz"),
        ),
        out_specs=(P(None, "gx", "gy", "gz"), P(None, "gx", "gy", "gz")),
        check_vma=False,
    )
```

profile of v0, /device:TPU:385, one launch (start us, length us, event | category | flops | bytes accessed | tf_op | source)
XLA Modules:
  0.0 195.1 jit_solution(11502425045991201001)
XLA Ops:
  16.9 9.5 %collective-permute-start.4 = (f32[3,10,10,1]{3,2,1,0:T(8,128)S(1)}, f32[3,10,10,1]{3,2,1,0:T(8,128)S(1)}, u32[]{:S(2)}, u32[]{:S(2)}) collective-permute-start(f32[3,10,10,1]{3,2,1,0:T(8,128)S(1)} %get-tuple-element.39), channel_id=1, source_target_pairs={{0,1},{1,2},{2,3},{3,4},{4,5},{5,6},{6,7},{7,8},{8,9},{9,10},{10,1... | collective-permute-start | bytes 3608 | tf_op jit(solution)/shard_map/ppermute | solution.py:18
  28.4 3.3 %collective-permute-start.6 = (f32[27,1,8,128]{3,2,1,0:T(8,128)S(1)}, f32[27,1,8,128]{3,2,1,0:T(8,128)S(1)}, u32[]{:S(2)}, u32[]{:S(2)}) collective-permute-start(f32[27,1,8,128]{3,2,1,0:T(8,128)S(1)} %get-tuple-element.34), channel_id=1, source_target_pairs={{0,128},{128,256},{256,384},{384,512},{512,640},{640,768},{768,896... | collective-permute-start | bytes 331784 | tf_op jit(solution)/shard_map/ppermute | solution.py:18
  44.8 4.1 %collective-permute-done.9 = f32[27,10,1,128]{3,0,2,1:T(8,128)S(1)} collective-permute-done((f32[27,10,1,128]{3,0,2,1:T(8,128)S(1)}, f32[27,10,1,128]{3,0,2,1:T(8,128)S(1)}, u32[]{:S(2)}, u32[]{:S(2)}) %collective-permute-start.9) | collective-permute-done | bytes 138272 | tf_op jit(solution)/shard_map/ppermute | solution.py:21
  52.4 3.6 %copy.35 = f32[27,10,10,1]{0,2,3,1:T(8,128)} copy(f32[27,10,10,1]{3,2,1,0:T(8,128)} %get-tuple-element.22) | data formatting | bytes 21600 | tf_op jit(solution)/shard_map/slice | solution.py:19
  55.9 6.1 %collective-permute-start.10 = (f32[27,10,10,1]{0,2,3,1:T(8,128)}, f32[27,10,10,1]{0,2,3,1:T(8,128)}, u32[]{:S(2)}, u32[]{:S(2)}) collective-permute-start(f32[27,10,10,1]{0,2,3,1:T(8,128)} %copy.35), channel_id=1, source_target_pairs={{0,1},{1,2},{2,3},{3,4},{4,5},{5,6},{6,7},{7,8},{8,9},{9,10},{10,1... | collective-permute-start | bytes 32408 | tf_op jit(solution)/shard_map/ppermute | solution.py:18
  71.4 4.1 %copy.38 = f32[27,10,10,1]{3,2,1,0:T(8,128)} copy(f32[27,10,10,1]{0,2,3,1:T(8,128)} %collective-permute-done.11) | data formatting | bytes 21600 | tf_op jit(solution)/shard_map/ppermute | solution.py:21
  75.5 4.4 %fusion.85 = (f32[8,8,128]{2,1,0:T(8,128)S(1)}, f32[27,8,8,128]{3,2,1,0:T(8,128)S(1)}) fusion(f32[27,8,8,128]{3,2,1,0:T(8,128)S(1)} %fusion.43, f32[8,8,128]{2,1,0:T(8,128)} %get-tuple-element.16, f32[27,10,10,1]{3,2,1,0:T(8,128)} %copy.38, f32[27,10,1,128]{3,2,1,0:T(1,128)} %copy-done.2, f32[27,1,8,128]{3,2,1,0:T(8,128)} %copy-done.7, ...), kind=kLoop, calls=%fused_computation.229 | loop fusion | flops 8175616 | bytes 2879424 | tf_op jit(solution)/shard_map/reduce_sum | solution.py:110
  80.0 4.9 %collective-permute-start.12 = (f32[27,1,8,128]{3,2,1,0:T(8,128)S(1)}, f32[27,1,8,128]{3,2,1,0:T(8,128)S(1)}, u32[]{:S(2)}, u32[]{:S(2)}) collective-permute-start(f32[27,1,8,128]{3,2,1,0:T(8,128)S(1)} %get-tuple-element.32), channel_id=1, source_target_pairs={{0,128},{128,256},{256,384},{384,512},{512,640},{640,768},{768,896... | collective-permute-start | bytes 331784 | tf_op jit(solution)/shard_map/ppermute | solution.py:18
  86.6 4.0 %collective-permute-done.13 = f32[27,1,8,128]{3,2,1,0:T(8,128)S(1)} collective-permute-done((f32[27,1,8,128]{3,2,1,0:T(8,128)S(1)}, f32[27,1,8,128]{3,2,1,0:T(8,128)S(1)}, u32[]{:S(2)}, u32[]{:S(2)}) %collective-permute-start.13) | collective-permute-done | bytes 110624 | tf_op jit(solution)/shard_map/ppermute | solution.py:21
  90.8 4.9 %collective-permute-start.14 = (f32[27,10,1,128]{3,0,2,1:T(8,128)S(1)}, f32[27,10,1,128]{3,0,2,1:T(8,128)S(1)}, u32[]{:S(2)}, u32[]{:S(2)}) collective-permute-start(f32[27,10,1,128]{3,0,2,1:T(8,128)S(1)} %copy.39), channel_id=1, source_target_pairs={{0,16},{16,32},{32,48},{48,64},{64,80},{80,96},{96,112},{1,17},{17... | collective-permute-start | bytes 414728 | tf_op jit(solution)/shard_map/ppermute | solution.py:18
  98.5 4.2 %collective-permute-done.15 = f32[27,10,1,128]{3,0,2,1:T(8,128)S(1)} collective-permute-done((f32[27,10,1,128]{3,0,2,1:T(8,128)S(1)}, f32[27,10,1,128]{3,0,2,1:T(8,128)S(1)}, u32[]{:S(2)}, u32[]{:S(2)}) %collective-permute-start.15) | collective-permute-done | bytes 138272 | tf_op jit(solution)/shard_map/ppermute | solution.py:21
  106.1 3.6 %copy.45 = f32[27,10,10,1]{0,2,3,1:T(8,128)} copy(f32[27,10,10,1]{3,2,1,0:T(8,128)} %get-tuple-element.20) | data formatting | bytes 21600 | tf_op jit(solution)/shard_map/slice | solution.py:19
  109.6 5.8 %collective-permute-start.16 = (f32[27,10,10,1]{0,2,3,1:T(8,128)}, f32[27,10,10,1]{0,2,3,1:T(8,128)}, u32[]{:S(2)}, u32[]{:S(2)}) collective-permute-start(f32[27,10,10,1]{0,2,3,1:T(8,128)} %copy.45), channel_id=1, source_target_pairs={{0,1},{1,2},{2,3},{3,4},{4,5},{5,6},{6,7},{7,8},{8,9},{9,10},{10,1... | collective-permute-start | bytes 32408 | tf_op jit(solution)/shard_map/ppermute | solution.py:18
  124.8 4.1 %copy.48 = f32[27,10,10,1]{3,2,1,0:T(8,128)} copy(f32[27,10,10,1]{0,2,3,1:T(8,128)} %collective-permute-done.17) | data formatting | bytes 21600 | tf_op jit(solution)/shard_map/ppermute | solution.py:21
  128.9 4.4 %fusion.83 = (f32[8,8,128]{2,1,0:T(8,128)S(1)}, f32[27,8,8,128]{3,2,1,0:T(8,128)S(1)}) fusion(f32[27,8,8,128]{3,2,1,0:T(8,128)S(1)} %broadcast_divide_fusion.1, f32[8,8,128]{2,1,0:T(8,128)} %get-tuple-element.16, f32[27,10,10,1]{3,2,1,0:T(8,128)} %copy.48, f32[27,10,1,128]{3,2,1,0:T(1,128)} %copy-done.1, f32[27,1,8,128]{3,2,1,0:T(8,128)} %copy-done.5, ...), kind=kLoop, calls=%fused_computation.228 | loop fusion | flops 8175616 | bytes 2879424 | tf_op jit(solution)/shard_map/reduce_sum | solution.py:110
  133.4 3.6 %collective-permute-start.18 = (f32[27,1,8,128]{3,2,1,0:T(8,128)S(1)}, f32[27,1,8,128]{3,2,1,0:T(8,128)S(1)}, u32[]{:S(2)}, u32[]{:S(2)}) collective-permute-start(f32[27,1,8,128]{3,2,1,0:T(8,128)S(1)} %get-tuple-element.30), channel_id=1, source_target_pairs={{0,128},{128,256},{256,384},{384,512},{512,640},{640,768},{768,896... | collective-permute-start | bytes 331784 | tf_op jit(solution)/shard_map/ppermute | solution.py:18
  138.8 3.8 %collective-permute-done.19 = f32[27,1,8,128]{3,2,1,0:T(8,128)S(1)} collective-permute-done((f32[27,1,8,128]{3,2,1,0:T(8,128)S(1)}, f32[27,1,8,128]{3,2,1,0:T(8,128)S(1)}, u32[]{:S(2)}, u32[]{:S(2)}) %collective-permute-start.19) | collective-permute-done | bytes 110624 | tf_op jit(solution)/shard_map/ppermute | solution.py:21
  142.7 3.6 %collective-permute-start.20 = (f32[27,10,1,128]{3,0,2,1:T(8,128)S(1)}, f32[27,10,1,128]{3,0,2,1:T(8,128)S(1)}, u32[]{:S(2)}, u32[]{:S(2)}) collective-permute-start(f32[27,10,1,128]{3,0,2,1:T(8,128)S(1)} %copy.49), channel_id=1, source_target_pairs={{0,16},{16,32},{32,48},{48,64},{64,80},{80,96},{96,112},{1,17},{17... | collective-permute-start | bytes 414728 | tf_op jit(solution)/shard_map/ppermute | solution.py:18
  149.4 4.0 %collective-permute-done.21 = f32[27,10,1,128]{3,0,2,1:T(8,128)S(1)} collective-permute-done((f32[27,10,1,128]{3,0,2,1:T(8,128)S(1)}, f32[27,10,1,128]{3,0,2,1:T(8,128)S(1)}, u32[]{:S(2)}, u32[]{:S(2)}) %collective-permute-start.21) | collective-permute-done | bytes 138272 | tf_op jit(solution)/shard_map/ppermute | solution.py:21
  156.1 3.6 %copy.55 = f32[27,10,10,1]{0,2,3,1:T(8,128)} copy(f32[27,10,10,1]{3,2,1,0:T(8,128)} %get-tuple-element.18) | data formatting | bytes 21600 | tf_op jit(solution)/shard_map/slice | solution.py:19
  159.7 6.0 %collective-permute-start.22 = (f32[27,10,10,1]{0,2,3,1:T(8,128)}, f32[27,10,10,1]{0,2,3,1:T(8,128)}, u32[]{:S(2)}, u32[]{:S(2)}) collective-permute-start(f32[27,10,10,1]{0,2,3,1:T(8,128)} %copy.55), channel_id=1, source_target_pairs={{0,1},{1,2},{2,3},{3,4},{4,5},{5,6},{6,7},{7,8},{8,9},{9,10},{10,1... | collective-permute-start | bytes 32408 | tf_op jit(solution)/shard_map/ppermute | solution.py:18
  175.1 4.1 %copy.58 = f32[27,10,10,1]{3,2,1,0:T(8,128)} copy(f32[27,10,10,1]{0,2,3,1:T(8,128)} %collective-permute-done.23) | data formatting | bytes 21600 | tf_op jit(solution)/shard_map/ppermute | solution.py:21
  179.1 3.9 %multiply_reduce_fusion.1 = (f32[27,128]{1,0:T(8,128)}, f32[27,128]{1,0:T(8,128)}) fusion(f32[8,8,128]{2,1,0:T(8,128)} %get-tuple-element.10, f32[8,8,128]{2,1,0:T(8,128)} %get-tuple-element.11, f32[27,10,10,1]{3,2,1,0:T(8,128)} %copy.58, f32[27,10,1,128]{3,2,1,0:T(1,128)S(1)} %copy.52, f32[27,1,8,128]{3,2,1,0:T(8,128)} %copy-done.3, ...), kind=kLoop, calls=%fused_computation.104 | loop fusion | flops 7734528 | bytes 1726560 | tf_op jit(solution)/shard_map/reduce_sum | solution.py:119
  185.0 5.5 %gather_fusion = f32[459]{0:T(512)S(1)} fusion(f32[27,17]{1,0:T(8,128)S(1)} %add_bitcast_fusion, s32[459]{0:T(512)S(1)} %reshape.803), kind=kCustom, calls=%fused_computation | custom fusion | bytes 7344 | tf_op jit(solution)/shard_map/jit(take_along_axis)/gather | solution.py:134
  (153 shorter events, 84.7 us)
Async XLA Ops:
  1.4 5.7 %collective-permute-start = (f32[3,1,8,128]{3,2,1,0:T(8,128)S(1)}, f32[3,1,8,128]{3,2,1,0:T(8,128)S(1)}, u32[]{:S(2)}, u32[]{:S(2)}) collective-permute-start(f32[3,1,8,128]{3,2,1,0:T(8,128)S(1)} %get-tuple-element.44), channel_id=1, source_target_pairs={{0,128},{128,256},{256,384},{384,512},{512,640},{640,768},{768,896... | collective-permute-start | bytes 36872 | tf_op jit(solution)/shard_map/ppermute | solution.py:18
  4.7 4.4 %collective-permute-start.1 = (f32[3,1,8,128]{3,2,1,0:T(8,128)S(1)}, f32[3,1,8,128]{3,2,1,0:T(8,128)S(1)}, u32[]{:S(2)}, u32[]{:S(2)}) collective-permute-start(f32[3,1,8,128]{3,2,1,0:T(8,128)S(1)} %get-tuple-element.43), channel_id=1, source_target_pairs={{128,0},{256,128},{384,256},{512,384},{640,512},{768,640},{896,768... | collective-permute-start | bytes 36872 | tf_op jit(solution)/shard_map/ppermute | solution.py:21
  9.1 5.9 %collective-permute-start.2 = (f32[3,10,1,128]{3,2,1,0:T(1,128)S(1)}, f32[3,10,1,128]{3,2,1,0:T(1,128)S(1)}, u32[]{:S(2)}, u32[]{:S(2)}) collective-permute-start(f32[3,10,1,128]{3,2,1,0:T(1,128)S(1)} %get-tuple-element.41), channel_id=1, source_target_pairs={{0,16},{16,32},{32,48},{48,64},{64,80},{80,96},{96,112},{1,17},{17... | collective-permute-start | bytes 46088 | tf_op jit(solution)/shard_map/ppermute | solution.py:18
  12.3 4.5 %collective-permute-start.3 = (f32[3,10,1,128]{3,2,1,0:T(1,128)S(1)}, f32[3,10,1,128]{3,2,1,0:T(1,128)S(1)}, u32[]{:S(2)}, u32[]{:S(2)}) collective-permute-start(f32[3,10,1,128]{3,2,1,0:T(1,128)S(1)} %get-tuple-element.42), channel_id=1, source_target_pairs={{16,0},{32,16},{48,32},{64,48},{80,64},{96,80},{112,96},{17,1},{33... | collective-permute-start | bytes 46088 | tf_op jit(solution)/shard_map/ppermute | solution.py:21
  16.9 16.1 %collective-permute-start.4 = (f32[3,10,10,1]{3,2,1,0:T(8,128)S(1)}, f32[3,10,10,1]{3,2,1,0:T(8,128)S(1)}, u32[]{:S(2)}, u32[]{:S(2)}) collective-permute-start(f32[3,10,10,1]{3,2,1,0:T(8,128)S(1)} %get-tuple-element.39), channel_id=1, source_target_pairs={{0,1},{1,2},{2,3},{3,4},{4,5},{5,6},{6,7},{7,8},{8,9},{9,10},{10,1... | collective-permute-start | bytes 3608 | tf_op jit(solution)/shard_map/ppermute | solution.py:18
  26.5 8.7 %collective-permute-start.5 = (f32[3,10,10,1]{3,2,1,0:T(8,128)S(1)}, f32[3,10,10,1]{3,2,1,0:T(8,128)S(1)}, u32[]{:S(2)}, u32[]{:S(2)}) collective-permute-start(f32[3,10,10,1]{3,2,1,0:T(8,128)S(1)} %get-tuple-element.40), channel_id=1, source_target_pairs={{1,0},{2,1},{3,2},{4,3},{5,4},{6,5},{7,6},{8,7},{9,8},{10,9},{11,1... | collective-permute-start | bytes 3608 | tf_op jit(solution)/shard_map/ppermute | solution.py:21
  28.4 8.7 %collective-permute-start.6 = (f32[27,1,8,128]{3,2,1,0:T(8,128)S(1)}, f32[27,1,8,128]{3,2,1,0:T(8,128)S(1)}, u32[]{:S(2)}, u32[]{:S(2)}) collective-permute-start(f32[27,1,8,128]{3,2,1,0:T(8,128)S(1)} %get-tuple-element.34), channel_id=1, source_target_pairs={{0,128},{128,256},{256,384},{384,512},{512,640},{640,768},{768,896... | collective-permute-start | bytes 331784 | tf_op jit(solution)/shard_map/ppermute | solution.py:18
  31.7 6.3 %collective-permute-start.7 = (f32[27,1,8,128]{3,2,1,0:T(8,128)S(1)}, f32[27,1,8,128]{3,2,1,0:T(8,128)S(1)}, u32[]{:S(2)}, u32[]{:S(2)}) collective-permute-start(f32[27,1,8,128]{3,2,1,0:T(8,128)S(1)} %get-tuple-element.35), channel_id=1, source_target_pairs={{128,0},{256,128},{384,256},{512,384},{640,512},{768,640},{896,768... | collective-permute-start | bytes 331784 | tf_op jit(solution)/shard_map/ppermute | solution.py:21
  38.3 6.4 %collective-permute-start.8 = (f32[27,10,1,128]{3,0,2,1:T(8,128)S(1)}, f32[27,10,1,128]{3,0,2,1:T(8,128)S(1)}, u32[]{:S(2)}, u32[]{:S(2)}) collective-permute-start(f32[27,10,1,128]{3,0,2,1:T(8,128)S(1)} %copy.29), channel_id=1, source_target_pairs={{0,16},{16,32},{32,48},{48,64},{64,80},{80,96},{96,112},{1,17},{17... | collective-permute-start | bytes 414728 | tf_op jit(solution)/shard_map/ppermute | solution.py:18
  41.4 7.5 %collective-permute-start.9 = (f32[27,10,1,128]{3,0,2,1:T(8,128)S(1)}, f32[27,10,1,128]{3,0,2,1:T(8,128)S(1)}, u32[]{:S(2)}, u32[]{:S(2)}) collective-permute-start(f32[27,10,1,128]{3,0,2,1:T(8,128)S(1)} %copy.31), channel_id=1, source_target_pairs={{16,0},{32,16},{48,32},{64,48},{80,64},{96,80},{112,96},{17,1},{33... | collective-permute-start | bytes 414728 | tf_op jit(solution)/shard_map/ppermute | solution.py:21
  55.9 11.8 %collective-permute-start.10 = (f32[27,10,10,1]{0,2,3,1:T(8,128)}, f32[27,10,10,1]{0,2,3,1:T(8,128)}, u32[]{:S(2)}, u32[]{:S(2)}) collective-permute-start(f32[27,10,10,1]{0,2,3,1:T(8,128)} %copy.35), channel_id=1, source_target_pairs={{0,1},{1,2},{2,3},{3,4},{4,5},{5,6},{6,7},{7,8},{8,9},{9,10},{10,1... | collective-permute-start | bytes 32408 | tf_op jit(solution)/shard_map/ppermute | solution.py:18
  64.2 7.3 %collective-permute-start.11 = (f32[27,10,10,1]{0,2,3,1:T(8,128)}, f32[27,10,10,1]{0,2,3,1:T(8,128)}, u32[]{:S(2)}, u32[]{:S(2)}) collective-permute-start(f32[27,10,10,1]{0,2,3,1:T(8,128)} %copy.37), channel_id=1, source_target_pairs={{1,0},{2,1},{3,2},{4,3},{5,4},{6,5},{7,6},{8,7},{9,8},{10,9},{11,1... | collective-permute-start | bytes 32408 | tf_op jit(solution)/shard_map/ppermute | solution.py:21
  80.0 6.6 %collective-permute-start.12 = (f32[27,1,8,128]{3,2,1,0:T(8,128)S(1)}, f32[27,1,8,128]{3,2,1,0:T(8,128)S(1)}, u32[]{:S(2)}, u32[]{:S(2)}) collective-permute-start(f32[27,1,8,128]{3,2,1,0:T(8,128)S(1)} %get-tuple-element.32), channel_id=1, source_target_pairs={{0,128},{128,256},{256,384},{384,512},{512,640},{640,768},{768,896... | collective-permute-start | bytes 331784 | tf_op jit(solution)/shard_map/ppermute | solution.py:18
  84.9 5.8 %collective-permute-start.13 = (f32[27,1,8,128]{3,2,1,0:T(8,128)S(1)}, f32[27,1,8,128]{3,2,1,0:T(8,128)S(1)}, u32[]{:S(2)}, u32[]{:S(2)}) collective-permute-start(f32[27,1,8,128]{3,2,1,0:T(8,128)S(1)} %get-tuple-element.33), channel_id=1, source_target_pairs={{128,0},{256,128},{384,256},{512,384},{640,512},{768,640},{896,768... | collective-permute-start | bytes 331784 | tf_op jit(solution)/shard_map/ppermute | solution.py:21
  90.8 7.5 %collective-permute-start.14 = (f32[27,10,1,128]{3,0,2,1:T(8,128)S(1)}, f32[27,10,1,128]{3,0,2,1:T(8,128)S(1)}, u32[]{:S(2)}, u32[]{:S(2)}) collective-permute-start(f32[27,10,1,128]{3,0,2,1:T(8,128)S(1)} %copy.39), channel_id=1, source_target_pairs={{0,16},{16,32},{32,48},{48,64},{64,80},{80,96},{96,112},{1,17},{17... | collective-permute-start | bytes 414728 | tf_op jit(solution)/shard_map/ppermute | solution.py:18
  95.7 6.9 %collective-permute-start.15 = (f32[27,10,1,128]{3,0,2,1:T(8,128)S(1)}, f32[27,10,1,128]{3,0,2,1:T(8,128)S(1)}, u32[]{:S(2)}, u32[]{:S(2)}) collective-permute-start(f32[27,10,1,128]{3,0,2,1:T(8,128)S(1)} %copy.41), channel_id=1, source_target_pairs={{16,0},{32,16},{48,32},{64,48},{80,64},{96,80},{112,96},{17,1},{33... | collective-permute-start | bytes 414728 | tf_op jit(solution)/shard_map/ppermute | solution.py:21
  109.6 11.2 %collective-permute-start.16 = (f32[27,10,10,1]{0,2,3,1:T(8,128)}, f32[27,10,10,1]{0,2,3,1:T(8,128)}, u32[]{:S(2)}, u32[]{:S(2)}) collective-permute-start(f32[27,10,10,1]{0,2,3,1:T(8,128)} %copy.45), channel_id=1, source_target_pairs={{0,1},{1,2},{2,3},{3,4},{4,5},{5,6},{6,7},{7,8},{8,9},{9,10},{10,1... | collective-permute-start | bytes 32408 | tf_op jit(solution)/shard_map/ppermute | solution.py:18
  117.5 7.3 %collective-permute-start.17 = (f32[27,10,10,1]{0,2,3,1:T(8,128)}, f32[27,10,10,1]{0,2,3,1:T(8,128)}, u32[]{:S(2)}, u32[]{:S(2)}) collective-permute-start(f32[27,10,10,1]{0,2,3,1:T(8,128)} %copy.47), channel_id=1, source_target_pairs={{1,0},{2,1},{3,2},{4,3},{5,4},{6,5},{7,6},{8,7},{9,8},{10,9},{11,1... | collective-permute-start | bytes 32408 | tf_op jit(solution)/shard_map/ppermute | solution.py:21
  133.4 5.4 %collective-permute-start.18 = (f32[27,1,8,128]{3,2,1,0:T(8,128)S(1)}, f32[27,1,8,128]{3,2,1,0:T(8,128)S(1)}, u32[]{:S(2)}, u32[]{:S(2)}) collective-permute-start(f32[27,1,8,128]{3,2,1,0:T(8,128)S(1)} %get-tuple-element.30), channel_id=1, source_target_pairs={{0,128},{128,256},{256,384},{384,512},{512,640},{640,768},{768,896... | collective-permute-start | bytes 331784 | tf_op jit(solution)/shard_map/ppermute | solution.py:18
  137.0 5.5 %collective-permute-start.19 = (f32[27,1,8,128]{3,2,1,0:T(8,128)S(1)}, f32[27,1,8,128]{3,2,1,0:T(8,128)S(1)}, u32[]{:S(2)}, u32[]{:S(2)}) collective-permute-start(f32[27,1,8,128]{3,2,1,0:T(8,128)S(1)} %get-tuple-element.31), channel_id=1, source_target_pairs={{128,0},{256,128},{384,256},{512,384},{640,512},{768,640},{896,768... | collective-permute-start | bytes 331784 | tf_op jit(solution)/shard_map/ppermute | solution.py:21
  142.7 6.5 %collective-permute-start.20 = (f32[27,10,1,128]{3,0,2,1:T(8,128)S(1)}, f32[27,10,1,128]{3,0,2,1:T(8,128)S(1)}, u32[]{:S(2)}, u32[]{:S(2)}) collective-permute-start(f32[27,10,1,128]{3,0,2,1:T(8,128)S(1)} %copy.49), channel_id=1, source_target_pairs={{0,16},{16,32},{32,48},{48,64},{64,80},{80,96},{96,112},{1,17},{17... | collective-permute-start | bytes 414728 | tf_op jit(solution)/shard_map/ppermute | solution.py:18
  146.4 7.0 %collective-permute-start.21 = (f32[27,10,1,128]{3,0,2,1:T(8,128)S(1)}, f32[27,10,1,128]{3,0,2,1:T(8,128)S(1)}, u32[]{:S(2)}, u32[]{:S(2)}) collective-permute-start(f32[27,10,1,128]{3,0,2,1:T(8,128)S(1)} %copy.51), channel_id=1, source_target_pairs={{16,0},{32,16},{48,32},{64,48},{80,64},{96,80},{112,96},{17,1},{33... | collective-permute-start | bytes 414728 | tf_op jit(solution)/shard_map/ppermute | solution.py:21
  159.7 10.3 %collective-permute-start.22 = (f32[27,10,10,1]{0,2,3,1:T(8,128)}, f32[27,10,10,1]{0,2,3,1:T(8,128)}, u32[]{:S(2)}, u32[]{:S(2)}) collective-permute-start(f32[27,10,10,1]{0,2,3,1:T(8,128)} %copy.55), channel_id=1, source_target_pairs={{0,1},{1,2},{2,3},{3,4},{4,5},{5,6},{6,7},{7,8},{8,9},{9,10},{10,1... | collective-permute-start | bytes 32408 | tf_op jit(solution)/shard_map/ppermute | solution.py:18
  167.8 7.3 %collective-permute-start.23 = (f32[27,10,10,1]{0,2,3,1:T(8,128)}, f32[27,10,10,1]{0,2,3,1:T(8,128)}, u32[]{:S(2)}, u32[]{:S(2)}) collective-permute-start(f32[27,10,10,1]{0,2,3,1:T(8,128)} %copy.57), channel_id=1, source_target_pairs={{1,0},{2,1},{3,2},{4,3},{5,4},{6,5},{7,6},{8,7},{9,8},{10,9},{11,1... | collective-permute-start | bytes 32408 | tf_op jit(solution)/shard_map/ppermute | solution.py:21
  (19 other events, 251.3 us)
where the time goes:
time: 197 us; the launch traced here: 195 us
  starting transfers between devices  78.3 us (40%)
  local copies, waits for them, and re-layouts  56.9 us (29%)
  waiting for transfers between devices  35.4 us (18%)
  other arithmetic  23.1 us (12%)
    ppermute x12, starting transfers between devices, extended(): lax.ppermute(lax.slice_in_dim(block, block.shape[dim] - width, None, axis...  57.4 us
    ppermute x12, waiting for transfers between devices, extended(): lax.ppermute(lax.slice_in_dim(block, 0, width, axis=dim), axis, backward)  29.9 us
    ppermute x12, starting transfers between devices, extended(): lax.ppermute(lax.slice_in_dim(block, 0, width, axis=dim), axis, backward)  18.2 us
    slice x14, local copies, waits for them, and re-layouts, extended(): lax.slice_in_dim(block, block.shape[dim] - width, None, axis=dim)  17.5 us
    ppermute x6, local copies, waits for them, and re-layouts, extended(): lax.ppermute(lax.slice_in_dim(block, 0, width, axis=dim), axis, backward)  12.6 us
    ppermute x6, local copies, waits for them, and re-layouts, extended(): lax.ppermute(lax.slice_in_dim(block, block.shape[dim] - width, None, axis...  9.24 us
    reduce_sum x2, other arithmetic, per_device(): total = jnp.sum(updated, axis=0)  8.7 us
    slice x7, local copies, waits for them, and re-layouts, extended(): lax.slice_in_dim(block, 0, width, axis=dim)  7.03 us
  transfers between devices with their start and end apart: 25, of which 18 were waited for; matrix products, arithmetic and copies ran while one was open for 13% of the time, Pallas kernels for 0%

commit v1 on v0

v1 whole, which is shorter than its diff:
```python
import jax
import jax.numpy as jnp
from jax import lax
from jax.experimental import pallas as pl
from jax.experimental.pallas import tpu as pltpu
from jax.sharding import PartitionSpec as P

BLOCK = 8
FIELDS = 9
PX, PY, PZ, STORAGE, LAYER = 4, 5, 6, 7, 8
ALL = tuple(range(FIELDS))
FIELDS_X = (ALL, ALL, (0, 1, 2, 3, PX, LAYER))
FIELDS_Y = (ALL, ALL, (0, 1, 2, 3, PY, LAYER))
ROWS_Y = 8 * sum(len(f) for f in FIELDS_Y)
ROWS_X = 8 * sum(len(f) for f in FIELDS_X)
F32 = jnp.float32


def iota(shape, dim):
    return lax.broadcasted_iota(jnp.int32, shape, dim)


def roll(value, shift, axis):
    return pltpu.roll(value, shift % value.shape[axis], axis)


def pack_kernel(basis, perm, storage, layer, core, edge):
    gx, gy = lax.axis_index("gx"), lax.axis_index("gy")
    nx, ny = lax.axis_size("gx"), lax.axis_size("gy")
    sub, lane = iota((8, 128), 0), iota((8, 128), 1)
    ids = layer[...].astype(F32)
    residue = ids - 3.0 * jnp.floor((ids + 0.5) * (1.0 / 3.0))
    is_zero, is_one = residue < 0.5, residue < 1.5
    rx_own, rx_low, rx_high = gx % 3, (gx + 2) % 3, (gx + 1) % 3
    ry_own, ry_low, ry_high = gy % 3, (gy + 2) % 3, (gy + 1) % 3
    low_rows = sub < 4
    y_valid = jnp.where(low_rows, (gy > 0).astype(F32), (gy < ny - 1).astype(F32))

    def at(rx, ry, x):
        first, second, third = (basis[9 * rz + 3 * ry + rx, x] for rz in range(3))
        return jnp.where(is_zero[x], first, jnp.where(is_one[x], second, third))

    for x in range(8):
        rx_other = rx_low if x < 4 else rx_high
        x_valid = ((gx > 0) if x < 4 else (gx < nx - 1)).astype(F32)
        for ex, rx in enumerate((rx_own, rx_other)):
            own = at(rx, ry_own, x)
            other = jnp.where(low_rows, at(rx, ry_low, x), at(rx, ry_high, x)) * y_valid
            if ex:
                own, other = own * x_valid, other * x_valid
            core[2 * ex, 8 * x : 8 * x + 8] = own
            core[2 * ex + 1, 8 * x : 8 * x + 8] = other
        for d in range(3):
            core[PX + d, 8 * x : 8 * x + 8] = perm[d, x]
        core[STORAGE, 8 * x : 8 * x + 8] = storage[x]
        core[LAYER, 8 * x : 8 * x + 8] = ids[x]
    for f in ALL:
        packed = jnp.zeros((8, 128), F32)
        for x in range(8):
            value = core[f, 8 * x : 8 * x + 8]
            value = jnp.where(lane < 4, value, roll(value, 16, 1))
            packed = jnp.where(lane // 16 == x, roll(value, 16 * x, 1), packed)
        edge[f] = packed


def y_kernel(core, from_low, from_high, beside_z, to_low, to_high):
    lane = iota((8, 128), 1)
    for f in ALL:
        beside_z[f] = jnp.where(lane % 16 < 4, from_high[f], from_low[f])
    for out, side in ((to_low, 0), (to_high, 1)):
        at = 0
        for d, fields in enumerate(FIELDS_Y):
            y = 7 - d if side else d
            for f in fields:
                out[at : at + 8] = core[f, pl.ds(y, 8, stride=8), :]
                at += 8
        for d in range(3):
            y = 7 - d if side else d
            for f in ALL:
                out[at : at + 1] = beside_z[f, y : y + 1]
                at += 1


def x_kernel(core, beside_z, from_low, from_high, beside_y, corner, to_low, to_high):
    sub, lane = iota((8, 128), 0), iota((8, 128), 1)
    beside_y[...] = jnp.zeros(beside_y.shape, F32)
    corner[...] = jnp.zeros(corner.shape, F32)
    for source, side in ((from_low, 0), (from_high, 1)):
        at = 0
        for d, fields in enumerate(FIELDS_Y):
            row = d if side else 7 - d
            for f in fields:
                into = f ^ 1 if f < 4 else f
                beside_y[into, pl.ds(row, 8, stride=8), :] = source[at : at + 8]
                at += 8
        for d in range(3):
            row = d if side else 7 - d
            for f in ALL:
                into = f ^ 1 if f < 4 else f
                corner[into, row : row + 1] = source[at : at + 1]
                at += 1
    for out, side in ((to_low, 0), (to_high, 1)):
        at = 0
        for d, fields in enumerate(FIELDS_X):
            x = 7 - d if side else d
            for f in fields:
                out[at : at + 8] = core[f, 8 * x : 8 * x + 8]
                at += 8
        first, second = (7, 6) if side else (0, 1)
        for f in ALL:
            out[at : at + 8] = jnp.where(
                (sub == 2) | (sub == 3),
                roll(beside_y[f, 8 * second : 8 * second + 8], 3, 0),
                beside_y[f, 8 * first : 8 * first + 8],
            )
            at += 8
        for f in ALL:
            out[at : at + 8] = jnp.where(
                (lane >= 48) & (lane < 80), roll(corner[f], -48 if side else 48, 1), beside_z[f]
            )
            at += 8


def harmonic(first, second):
    total = first + second
    return 2.0 * first * second / jnp.where(total > 0.0, total, 1.0)


def sweep_kernel(
    core, beside_z, beside_y, corner, from_low, from_high, smoothed, coarse,
    ext, face_x, face_y, face_z, near_x, near_y, near_y_other, near_z, diagonal, weight, once, twice, sums,
):
    gx, gy, gz = lax.axis_index("gx"), lax.axis_index("gy"), lax.axis_index("gz")
    nx, ny = lax.axis_size("gx"), lax.axis_size("gy")
    sub, lane = iota((8, 128), 0), iota((8, 128), 1)
    row = iota((16, 256), 0)
    column = iota((16, 256), 1)

    def unpacked(value, slot):
        value = roll(value, -16 * slot, 1)
        return jnp.where(lane < 3, value, jnp.where(lane >= 117, roll(value, 112, 1), 0.0))

    zero = jnp.zeros((8, 128), F32)
    for f in ALL:
        for x in range(8):
            ext[f, x + 3, 0:8, 0:128] = core[f, 8 * x : 8 * x + 8]
            ext[f, x + 3, 8:16, 0:128] = beside_y[f, 8 * x : 8 * x + 8]
            ext[f, x + 3, 0:8, 128:256] = unpacked(beside_z[f], x)
            ext[f, x + 3, 8:16, 128:256] = unpacked(corner[f], x)
    for source, side in ((from_low, 0), (from_high, 1)):
        at = 0
        for d in range(3):
            plane = 11 + d if side else 2 - d
            for f in ALL:
                into = f ^ 2 if f < 4 else f
                if f in FIELDS_X[d]:
                    ext[into, plane, 0:8, 0:128] = source[at : at + 8]
                    at += 8
                else:
                    ext[into, plane, 0:8, 0:128] = zero
        for f in ALL:
            into = f ^ 2 if f < 4 else f
            rows = source[at : at + 8]
            across = source[at + 72 : at + 80]
            at += 8
            lateral = roll(across, -48 if side else 48, 1)
            for d in range(3):
                plane = 11 + d if side else 2 - d
                slot = d if side else 7 - d
                ext[into, plane, 0:8, 128:256] = unpacked(across, slot)
                if d == 0:
                    ext[into, plane, 8:16, 0:128] = jnp.where((sub < 2) | (sub > 5), rows, 0.0)
                elif d == 1:
                    ext[into, plane, 8:16, 0:128] = jnp.where((sub < 1) | (sub > 6), roll(rows, -3, 0), 0.0)
                else:
                    ext[into, plane, 8:16, 0:128] = zero
                ext[into, plane, 8:16, 128:256] = unpacked(lateral, slot) if d < 2 else zero

    for p in range(13):
        face = harmonic(ext[PX, p], ext[PX, p + 1])
        face_x[p] = face
        near_x[p] = jnp.where(ext[LAYER, p] == ext[LAYER, p + 1], face, 0.0)
    for p in range(1, 13):
        ids = ext[LAYER, p]
        across = ext[PY, p]
        face = harmonic(across, roll(across, -1, 0))
        face_y[p] = face
        near = jnp.where(ids == roll(ids, -1, 0), face, 0.0)
        near_y[p] = near
        near_y_other[p] = jnp.where(row == 3, 0.0, near)
        total = ext[STORAGE, p] + face_x[p - 1] + face_x[p] + face + roll(face, 1, 0)
        across = ext[PZ, p]
        face = harmonic(across, roll(across, -1, 1))
        face_z[p] = face
        near_z[p] = jnp.where(ids == roll(ids, -1, 1), face, 0.0)
        total = total + face + roll(face, 1, 1)
        diagonal[p] = total
        weight[p] = (2.0 / 3.0) / jnp.where(total > 0.0, total, 1.0)

    y_valid = jnp.where((row < 4) | (row >= 12), (gy > 0).astype(F32), (gy < ny - 1).astype(F32))

    def relax(values, p):
        x_valid = ((gx > 0) if p < 7 else (gx < nx - 1)).astype(F32)
        updated = []
        for f in range(4):
            own = values(f, p)
            side_y = near_y_other[p] if f & 1 else near_y[p]
            total = side_y * roll(own, -1, 0) + roll(side_y * own, 1, 0)
            side_z = near_z[p]
            total = total + side_z * roll(own, -1, 1) + roll(side_z * own, 1, 1)
            if not (f & 2 and p == 7):
                total = total + near_x[p - 1] * values(f, p - 1)
            if not (f & 2 and p == 6):
                total = total + near_x[p] * values(f, p + 1)
            scale = weight[p]
            if f & 1:
                scale = scale * y_valid
            if f & 2:
                scale = scale * x_valid
            updated.append(own * (1.0 / 3.0) + scale * total)
        total = (updated[0] + updated[1]) + (updated[2] + updated[3])
        inverse = 1.0 / jnp.where(total > 0.0, total, 1.0)
        return [value * inverse for value in updated]

    for p in range(1, 13):
        for f, value in enumerate(relax(lambda f, p: ext[f, p], p)):
            once[f, p] = value
    for p in range(2, 12):
        for f, value in enumerate(relax(lambda f, p: once[f, p], p)):
            twice[f, p] = value

    rx_own, rx_low, rx_high = gx % 3, (gx + 2) % 3, (gx + 1) % 3
    ry_own, ry_low, ry_high = gy % 3, (gy + 2) % 3, (gy + 1) % 3
    for x in range(8):
        ids = ext[LAYER, x + 3, 0:8, 0:128]
        residue = ids - 3.0 * jnp.floor((ids + 0.5) * (1.0 / 3.0))
        rx_other, rx_none = (rx_low, rx_high) if x < 4 else (rx_high, rx_low)
        for rz in range(3):
            hit = jnp.abs(residue - rz) < 0.5
            for ex, rx in ((0, rx_own), (1, rx_other)):
                own = jnp.where(hit, twice[2 * ex, x + 3, 0:8, 0:128], 0.0)
                other = jnp.where(hit, twice[2 * ex + 1, x + 3, 0:8, 0:128], 0.0)
                smoothed[9 * rz + 3 * ry_own + rx, x] = own
                smoothed[9 * rz + 3 * ry_low + rx, x] = jnp.where(sub < 4, other, 0.0)
                smoothed[9 * rz + 3 * ry_high + rx, x] = jnp.where(sub < 4, 0.0, other)
            for ry in range(3):
                smoothed[9 * rz + 3 * ry + rx_none, x] = zero

    first_octet = gz * (128 // BLOCK)
    octet = (jnp.where(column < 192, column, column - 256) + 256) // BLOCK - 32 + first_octet
    octet = octet.astype(F32)
    sums[...] = jnp.zeros(sums.shape, F32)
    for p in range(2, 12):
        inside = 3 <= p <= 10
        tall = 16 if inside else 8
        ids = ext[LAYER, p, 0:tall]
        lifted = ids > octet[0:tall]
        parts = [jnp.zeros((tall, 256), F32) for _ in range(3)]

        def add(parts, face, step, keep=None):
            if keep is not None:
                face = jnp.where(keep, face, 0.0)
            return [
                parts[0] - jnp.where(step == 1.0, face, 0.0),
                parts[1] - jnp.where(step == 0.0, face, 0.0),
                parts[2] - jnp.where(step == -1.0, face, 0.0),
            ]

        in_block = row[0:tall] < 8
        if p >= 4:
            parts = add(parts, face_x[p - 1, 0:tall], ext[LAYER, p - 1, 0:tall] - ids, in_block)
        if p <= 9:
            parts = add(parts, face_x[p, 0:tall], ext[LAYER, p + 1, 0:tall] - ids, in_block)
        if inside:
            face = face_y[p]
            parts = add(parts, face, roll(ids, -1, 0) - ids, (row < 7) | (row == 15))
            parts = add(parts, roll(face, 1, 0), roll(ids, 1, 0) - ids, (row > 0) & (row < 9))
            face = face_z[p]
            parts = add(parts, face, roll(ids, -1, 1) - ids, in_block)
            parts = add(parts, roll(face, 1, 1), roll(ids, 1, 1) - ids, in_block)
            parts[1] = parts[1] + jnp.where(in_block, diagonal[p], 0.0)
        for oz in range(3):
            upper = jnp.where(lifted, parts[oz], 0.0)
            lower = parts[oz] - upper
            for f in range(4):
                value = twice[f, p, 0:tall]
                ox = 1 if f < 2 else (0 if p < 7 else 2)
                sums[oz, 0, ox, f & 1, 0:tall] += lower * value
                sums[oz, 1, ox, f & 1, 0:tall] += upper * value
    spot = iota((256, 128), 0)
    place = (jnp.where(spot < 192, spot, spot - 256) + 256) // BLOCK - 32
    for oz in range(3):
        total = jnp.zeros((16, 128), F32)
        for lift in range(2):
            rows = []
            for oy in range(3):
                for ox in range(3):
                    if oy == 1:
                        value = sums[oz, lift, ox, 0]
                        value = value[0:8] + value[8:16]
                    else:
                        value = sums[oz, lift, ox, 1]
                        value = value[0:8] + roll(value[8:16], 4, 0)
                        value = value[0:4] if oy == 0 else value[4:8]
                    rows.append(jnp.sum(value, axis=0, keepdims=True))
            rows.append(jnp.zeros((7, 256), F32))
            chosen = (place + lift - (oz - 1) == iota((256, 128), 1)).astype(F32)
            total = total + jnp.dot(
                jnp.concatenate(rows, axis=0), chosen, precision=lax.Precision.HIGHEST, preferred_element_type=F32
            )
        total = total * (1.0 / (BLOCK * BLOCK))
        coarse[9 * oz : 9 * oz + 9] = total[0:9, 0:16]


def call(kernel, shapes, *operands, scratch=()):
    vmem = pl.BlockSpec(memory_space=pltpu.VMEM)
    return pl.pallas_call(
        kernel,
        out_shape=[jax.ShapeDtypeStruct(shape, F32) for shape in shapes],
        in_specs=[vmem] * len(operands),
        out_specs=[vmem] * len(shapes),
        scratch_shapes=[pltpu.VMEM(shape, F32) for shape in scratch],
        compiler_params=pltpu.CompilerParams(vmem_limit_bytes=48 * 1024 * 1024),
    )(*operands)


def exchange(axis, to_low, to_high):
    count = lax.axis_size(axis)
    forward = [(i, i + 1) for i in range(count - 1)]
    backward = [(target, source) for source, target in forward]
    return lax.ppermute(to_high, axis, forward), lax.ppermute(to_low, axis, backward)


def per_device(basis, perm, storage, layer):
    block = (FIELDS, 64, 128)
    side = (FIELDS, 8, 128)
    core, edge = call(pack_kernel, (block, side), basis, perm, storage, layer)
    low, high = exchange("gz", edge, edge)
    rows = (ROWS_Y + 32, 128)
    beside_z, to_low, to_high = call(y_kernel, (side, rows, rows), core, low, high)
    low, high = exchange("gy", to_low, to_high)
    rows = (ROWS_X + 144, 128)
    beside_y, corner, to_low, to_high = call(x_kernel, (block, side, rows, rows), core, beside_z, low, high)
    low, high = exchange("gx", to_low, to_high)
    field = (14, 16, 256)
    smoothed, coarse = call(
        sweep_kernel,
        ((27, 8, 8, 128), (27, 16)),
        core,
        beside_z,
        beside_y,
        corner,
        low,
        high,
        scratch=((FIELDS,) + field,) + (field,) * 9 + ((4,) + field,) * 2 + ((3, 2, 3, 2, 16, 256),),
    )
    return smoothed, coarse.reshape(27, 1, 1, 16)


def solution(mesh):
    return jax.shard_map(
        per_device,
        mesh=mesh,
        in_specs=(
            P(None, "gx", "gy", "gz"),
            P(None, "gx", "gy", "gz"),
            P("gx", "gy", "gz"),
            P("gx", "gy", "gz"),
        ),
        out_specs=(P(None, "gx", "gy", "gz"), P(None, "gx", "gy", "gz")),
        check_vma=False,
    )
```

time: 197 us -> 46.4 us (0.24)
  the two profiles are of different devices: /device:TPU:385 before, /device:TPU:1 now
where the time goes in v1:
time: 46.4 us; the launch traced here: 46 us
  starting transfers between devices  23.2 us (50%)
  waiting for transfers between devices  11.9 us (26%)
  Pallas kernels  5.98 us (13%)
  local copies, waits for them, and re-layouts  4.25 us (9%)
  between operations  0.72 us (2%)
    ppermute x3, starting transfers between devices, exchange(): lax.ppermute(to_low, axis, backward)  18.6 us
    ppermute x3, waiting for transfers between devices, exchange(): lax.ppermute(to_low, axis, backward)  7.7 us
    pallas_call x4, Pallas kernels, call(): pl.pallas_call(kernel, out_shape=[jax.ShapeDtypeStruct(shape, F32) for sh...  5.98 us
    ppermute x3, starting transfers between devices, exchange(): lax.ppermute(to_high, axis, forward)  4.52 us
    unnamed x9, local copies, waits for them, and re-layouts  4.25 us
    ppermute x3, waiting for transfers between devices, exchange(): lax.ppermute(to_high, axis, forward)  4.17 us
  transfers between devices with their start and end apart: 6, of which 5 were waited for; matrix products, arithmetic and copies ran while one was open for 0% of the time, Pallas kernels for 0%

profile of v1, /device:TPU:1, one launch (start us, length us, event | category | flops | bytes accessed | tf_op | source)
XLA Modules:
  0.0 46.0 jit_solution(1890214650487290627)
XLA Ops:
  0.6 0.0 copy-start
  0.6 1.2 %copy-done = f32[27,8,8,128]{3,2,1,0:T(8,128)S(1)} copy-done((f32[27,8,8,128]{3,2,1,0:T(8,128)S(1)}, f32[27,8,8,128]{3,2,1,0:T(8,128)}, u32[]{:S(2)}) %copy-start) | copy-done | bytes 884760
  1.8 0.0 copy-start.1
  1.8 0.9 %copy-done.1 = f32[3,8,8,128]{3,2,1,0:T(8,128)S(1)} copy-done((f32[3,8,8,128]{3,2,1,0:T(8,128)S(1)}, f32[3,8,8,128]{3,2,1,0:T(8,128)}, u32[]{:S(2)}) %copy-start.1) | copy-done | bytes 98328
  2.7 0.0 copy-start.2
  2.7 0.8 %copy-done.2 = f32[8,8,128]{2,1,0:T(8,128)S(1)} copy-done((f32[8,8,128]{2,1,0:T(8,128)S(1)}, f32[8,8,128]{2,1,0:T(8,128)}, u32[]{:S(2)}) %copy-start.2) | copy-done | bytes 32792
  3.5 0.8 %copy-done.3 = s32[8,8,128]{2,1,0:T(8,128)S(1)} copy-done((s32[8,8,128]{2,1,0:T(8,128)S(1)}, s32[8,8,128]{2,1,0:T(8,128)}, u32[]{:S(2)}) %copy-start.3) | copy-done | bytes 32792
  4.2 0.3 shard_map.59
  4.5 16.1 %collective-permute-start.1 = (f32[9,8,128]{2,1,0:T(8,128)S(1)}, f32[9,8,128]{2,1,0:T(8,128)S(1)}, u32[]{:S(2)}, u32[]{:S(2)}) collective-permute-start(f32[9,8,128]{2,1,0:T(8,128)S(1)} %get-tuple-element.14), channel_id=1, source_target_pairs={{1,0},{2,1},{3,2},{4,3},{5,4},{6,5},{7,6},{8,7},{9,8},{10,9},{11,1... | collective-permute-start | bytes 110600 | tf_op jit(solution)/shard_map/ppermute | solution.py:331
  20.6 1.9 %collective-permute-start = (f32[9,8,128]{2,1,0:T(8,128)S(1)}, f32[9,8,128]{2,1,0:T(8,128)S(1)}, u32[]{:S(2)}, u32[]{:S(2)}) collective-permute-start(f32[9,8,128]{2,1,0:T(8,128)S(1)} %get-tuple-element.14), channel_id=1, source_target_pairs={{0,1},{1,2},{2,3},{3,4},{4,5},{5,6},{6,7},{7,8},{8,9},{9,10},{10,1... | collective-permute-start | bytes 110600 | tf_op jit(solution)/shard_map/ppermute | solution.py:331
  22.5 0.0 collective-permute-done.1.from_high
  22.5 1.2 %collective-permute-done.from_low = f32[9,8,128]{2,1,0:T(8,128)S(1)} collective-permute-done((f32[9,8,128]{2,1,0:T(8,128)S(1)}, f32[9,8,128]{2,1,0:T(8,128)S(1)}, u32[]{:S(2)}, u32[]{:S(2)}) %collective-permute-start) | collective-permute-done | bytes 36896 | tf_op jit(solution)/shard_map/ppermute | solution.py:331
  23.7 0.1 shard_map.60
  23.7 1.3 %collective-permute-start.2 = (f32[224,128]{1,0:T(8,128)S(1)}, f32[224,128]{1,0:T(8,128)S(1)}, u32[]{:S(2)}, u32[]{:S(2)}) collective-permute-start(f32[224,128]{1,0:T(8,128)S(1)} %get-tuple-element.16), channel_id=1, source_target_pairs={{0,16},{16,32},{32,48},{48,64},{64,80},{80,96},{96,112},{1,17},{17... | collective-permute-start | bytes 344072 | tf_op jit(solution)/shard_map/ppermute | solution.py:331
  25.0 1.3 %collective-permute-start.3 = (f32[224,128]{1,0:T(8,128)S(1)}, f32[224,128]{1,0:T(8,128)S(1)}, u32[]{:S(2)}, u32[]{:S(2)}) collective-permute-start(f32[224,128]{1,0:T(8,128)S(1)} %get-tuple-element.17), channel_id=1, source_target_pairs={{16,0},{32,16},{48,32},{64,48},{80,64},{96,80},{112,96},{17,1},{33... | collective-permute-start | bytes 344072 | tf_op jit(solution)/shard_map/ppermute | solution.py:331
  26.3 1.3 %collective-permute-done.2.from_low = f32[224,128]{1,0:T(8,128)S(1)} collective-permute-done((f32[224,128]{1,0:T(8,128)S(1)}, f32[224,128]{1,0:T(8,128)S(1)}, u32[]{:S(2)}, u32[]{:S(2)}) %collective-permute-start.2) | collective-permute-done | bytes 114720 | tf_op jit(solution)/shard_map/ppermute | solution.py:331
  27.6 3.9 %collective-permute-done.3.from_high = f32[224,128]{1,0:T(8,128)S(1)} collective-permute-done((f32[224,128]{1,0:T(8,128)S(1)}, f32[224,128]{1,0:T(8,128)S(1)}, u32[]{:S(2)}, u32[]{:S(2)}) %collective-permute-start.3) | collective-permute-done | bytes 114720 | tf_op jit(solution)/shard_map/ppermute | solution.py:331
  31.5 0.1 shard_map.61
  31.7 1.3 %collective-permute-start.4 = (f32[336,128]{1,0:T(8,128)S(1)}, f32[336,128]{1,0:T(8,128)S(1)}, u32[]{:S(2)}, u32[]{:S(2)}) collective-permute-start(f32[336,128]{1,0:T(8,128)S(1)} %get-tuple-element.20), channel_id=1, source_target_pairs={{0,128},{128,256},{256,384},{384,512},{512,640},{640,768},{768,896... | collective-permute-start | bytes 516104 | tf_op jit(solution)/shard_map/ppermute | solution.py:331
  33.0 1.3 %collective-permute-start.5 = (f32[336,128]{1,0:T(8,128)S(1)}, f32[336,128]{1,0:T(8,128)S(1)}, u32[]{:S(2)}, u32[]{:S(2)}) collective-permute-start(f32[336,128]{1,0:T(8,128)S(1)} %get-tuple-element.21), channel_id=1, source_target_pairs={{128,0},{256,128},{384,256},{512,384},{640,512},{768,640},{896,768... | collective-permute-start | bytes 516104 | tf_op jit(solution)/shard_map/ppermute | solution.py:331
  34.3 1.7 %collective-permute-done.4.from_low = f32[336,128]{1,0:T(8,128)S(1)} collective-permute-done((f32[336,128]{1,0:T(8,128)S(1)}, f32[336,128]{1,0:T(8,128)S(1)}, u32[]{:S(2)}, u32[]{:S(2)}) %collective-permute-start.4) | collective-permute-done | bytes 172064 | tf_op jit(solution)/shard_map/ppermute | solution.py:331
  36.0 3.8 %collective-permute-done.5.from_high = f32[336,128]{1,0:T(8,128)S(1)} collective-permute-done((f32[336,128]{1,0:T(8,128)S(1)}, f32[336,128]{1,0:T(8,128)S(1)}, u32[]{:S(2)}, u32[]{:S(2)}) %collective-permute-start.5) | collective-permute-done | bytes 172064 | tf_op jit(solution)/shard_map/ppermute | solution.py:331
  39.8 5.5 %shard_map.62 = (f32[27,8,8,128]{3,2,1,0:T(8,128)}, f32[27,16]{1,0:T(8,128)S(1)}) custom-call(f32[9,64,128]{2,1,0:T(8,128)S(1)} %get-tuple-element.13.core, f32[9,8,128]{2,1,0:T(8,128)S(1)} %get-tuple-element.15.beside_z, f32[9,64,128]{2,1,0:T(8,128)S(1)} %get-tuple-element.18.beside_y, f32[9,8,128]{2,1,0:T(8,128)S(1)} %get-tuple-element.19.corner, ...), custom_call_target="tpu_custom_call" | custom-call | tf_op jit(solution)/shard_map/pallas_call | solution.py:317
  45.3 0.7 %copy.6 = f32[27,1,1,16]{0,3,2,1:T(8,128)} copy(f32[27,1,1,16]{3,0,2,1:T(8,128)S(1)} %bitcast.1) | data formatting | bytes 3456
  (1 shorter events, 0.0 us)
Async XLA Ops:
  0.6 1.2 %copy-start = (f32[27,8,8,128]{3,2,1,0:T(8,128)S(1)}, f32[27,8,8,128]{3,2,1,0:T(8,128)}, u32[]{:S(2)}) copy-start(f32[27,8,8,128]{3,2,1,0:T(8,128)} %basis.1) | copy-start | bytes 2654212
  1.8 0.9 %copy-start.1 = (f32[3,8,8,128]{3,2,1,0:T(8,128)S(1)}, f32[3,8,8,128]{3,2,1,0:T(8,128)}, u32[]{:S(2)}) copy-start(f32[3,8,8,128]{3,2,1,0:T(8,128)} %perm.1) | copy-start | bytes 294916
  2.7 0.8 %copy-start.2 = (f32[8,8,128]{2,1,0:T(8,128)S(1)}, f32[8,8,128]{2,1,0:T(8,128)}, u32[]{:S(2)}) copy-start(f32[8,8,128]{2,1,0:T(8,128)} %storage.1) | copy-start | bytes 98308
  3.5 0.8 %copy-start.3 = (s32[8,8,128]{2,1,0:T(8,128)S(1)}, s32[8,8,128]{2,1,0:T(8,128)}, u32[]{:S(2)}) copy-start(s32[8,8,128]{2,1,0:T(8,128)} %layer.1) | copy-start | bytes 98308
  4.5 18.0 %collective-permute-start.1 = (f32[9,8,128]{2,1,0:T(8,128)S(1)}, f32[9,8,128]{2,1,0:T(8,128)S(1)}, u32[]{:S(2)}, u32[]{:S(2)}) collective-permute-start(f32[9,8,128]{2,1,0:T(8,128)S(1)} %get-tuple-element.14), channel_id=1, source_target_pairs={{1,0},{2,1},{3,2},{4,3},{5,4},{6,5},{7,6},{8,7},{9,8},{10,9},{11,1... | collective-permute-start | bytes 110600 | tf_op jit(solution)/shard_map/ppermute | solution.py:331
  20.6 3.1 %collective-permute-start = (f32[9,8,128]{2,1,0:T(8,128)S(1)}, f32[9,8,128]{2,1,0:T(8,128)S(1)}, u32[]{:S(2)}, u32[]{:S(2)}) collective-permute-start(f32[9,8,128]{2,1,0:T(8,128)S(1)} %get-tuple-element.14), channel_id=1, source_target_pairs={{0,1},{1,2},{2,3},{3,4},{4,5},{5,6},{6,7},{7,8},{8,9},{9,10},{10,1... | collective-permute-start | bytes 110600 | tf_op jit(solution)/shard_map/ppermute | solution.py:331
  23.7 3.9 %collective-permute-start.2 = (f32[224,128]{1,0:T(8,128)S(1)}, f32[224,128]{1,0:T(8,128)S(1)}, u32[]{:S(2)}, u32[]{:S(2)}) collective-permute-start(f32[224,128]{1,0:T(8,128)S(1)} %get-tuple-element.16), channel_id=1, source_target_pairs={{0,16},{16,32},{32,48},{48,64},{64,80},{80,96},{96,112},{1,17},{17... | collective-permute-start | bytes 344072 | tf_op jit(solution)/shard_map/ppermute | solution.py:331
  25.0 6.5 %collective-permute-start.3 = (f32[224,128]{1,0:T(8,128)S(1)}, f32[224,128]{1,0:T(8,128)S(1)}, u32[]{:S(2)}, u32[]{:S(2)}) collective-permute-start(f32[224,128]{1,0:T(8,128)S(1)} %get-tuple-element.17), channel_id=1, source_target_pairs={{16,0},{32,16},{48,32},{64,48},{80,64},{96,80},{112,96},{17,1},{33... | collective-permute-start | bytes 344072 | tf_op jit(solution)/shard_map/ppermute | solution.py:331
  31.7 4.3 %collective-permute-start.4 = (f32[336,128]{1,0:T(8,128)S(1)}, f32[336,128]{1,0:T(8,128)S(1)}, u32[]{:S(2)}, u32[]{:S(2)}) collective-permute-start(f32[336,128]{1,0:T(8,128)S(1)} %get-tuple-element.20), channel_id=1, source_target_pairs={{0,128},{128,256},{256,384},{384,512},{512,640},{640,768},{768,896... | collective-permute-start | bytes 516104 | tf_op jit(solution)/shard_map/ppermute | solution.py:331
  33.0 6.8 %collective-permute-start.5 = (f32[336,128]{1,0:T(8,128)S(1)}, f32[336,128]{1,0:T(8,128)S(1)}, u32[]{:S(2)}, u32[]{:S(2)}) collective-permute-start(f32[336,128]{1,0:T(8,128)S(1)} %get-tuple-element.21), channel_id=1, source_target_pairs={{128,0},{256,128},{384,256},{512,384},{640,512},{768,640},{896,768... | collective-permute-start | bytes 516104 | tf_op jit(solution)/shard_map/ppermute | solution.py:331

commit v2 on v0

v2 whole, which is shorter than its diff:
```python
import jax
import jax.numpy as jnp
from jax import lax
from jax.experimental import pallas as pl
from jax.experimental.pallas import tpu as pltpu
from jax.sharding import PartitionSpec as P

BLOCK = 8
FIELDS = 9
PX, PY, PZ, STORAGE, LAYER = 4, 5, 6, 7, 8
ALL = tuple(range(FIELDS))
FIELDS_X = (ALL, ALL, (0, 1, 2, 3, PX, LAYER))
FIELDS_Y = (ALL, ALL, (0, 1, 2, 3, PY, LAYER))
ROWS_Y = 8 * sum(len(f) for f in FIELDS_Y)
ROWS_X = 8 * sum(len(f) for f in FIELDS_X)
F32 = jnp.float32


def iota(shape, dim):
    return lax.broadcasted_iota(jnp.int32, shape, dim)


def roll(value, shift, axis):
    return pltpu.roll(value, shift % value.shape[axis], axis)


def pack_kernel(basis_hbm, perm_hbm, storage_hbm, layer_hbm, core, edge, basis, layer, sems):
    copies = [
        pltpu.make_async_copy(source, target, sems.at[i])
        for i, (source, target) in enumerate(
            (
                (basis_hbm, basis),
                (layer_hbm, layer),
                (perm_hbm, core.at[PX : PZ + 1]),
                (storage_hbm, core.at[STORAGE]),
            )
        )
    ]
    for copy in copies:
        copy.start()
    gx, gy = lax.axis_index("gx"), lax.axis_index("gy")
    nx, ny = lax.axis_size("gx"), lax.axis_size("gy")
    sub, lane = iota((8, 128), 0), iota((8, 128), 1)
    rx_own, rx_low, rx_high = gx % 3, (gx + 2) % 3, (gx + 1) % 3
    ry_own, ry_low, ry_high = gy % 3, (gy + 2) % 3, (gy + 1) % 3
    low_rows = sub < 4
    y_valid = jnp.where(low_rows, (gy > 0).astype(F32), (gy < ny - 1).astype(F32))
    for copy in copies:
        copy.wait()
    ids = layer[...].astype(F32)
    core[LAYER] = ids
    residue = ids - 3.0 * jnp.floor((ids + 0.5) * (1.0 / 3.0))

    for x in range(8):
        here = residue[8 * x : 8 * x + 8]
        is_zero, is_one = here < 0.5, here < 1.5

        def at(rx, ry):
            first, second, third = (basis[9 * rz + 3 * ry + rx, 8 * x : 8 * x + 8] for rz in range(3))
            return jnp.where(is_zero, first, jnp.where(is_one, second, third))

        rx_other = rx_low if x < 4 else rx_high
        x_valid = ((gx > 0) if x < 4 else (gx < nx - 1)).astype(F32)
        for ex, rx in enumerate((rx_own, rx_other)):
            own = at(rx, ry_own)
            other = jnp.where(low_rows, at(rx, ry_low), at(rx, ry_high)) * y_valid
            if ex:
                own, other = own * x_valid, other * x_valid
            core[2 * ex, 8 * x : 8 * x + 8] = own
            core[2 * ex + 1, 8 * x : 8 * x + 8] = other
    for f in ALL:
        packed = jnp.zeros((8, 128), F32)
        for x in range(8):
            value = core[f, 8 * x : 8 * x + 8]
            value = jnp.where(lane < 4, value, roll(value, 16, 1))
            packed = jnp.where(lane // 16 == x, roll(value, 16 * x, 1), packed)
        edge[f] = packed


def by_side(axis, one, other, body):
    even = lax.axis_index(axis) % 2 == 0
    pl.when(even)(lambda: body(((one, 1), (other, 0))))
    pl.when(jnp.logical_not(even))(lambda: body(((one, 0), (other, 1))))


def y_kernel(core, from_one, from_other, beside_z, to_one, to_other):
    lane = iota((8, 128), 1)
    high = (lane % 16 < 4).astype(jnp.int32)
    odd = lax.axis_index("gz") % 2
    for f in ALL:
        beside_z[f] = jnp.where(high != odd, from_one[f], from_other[f])

    def send(pairs):
        for out, side in pairs:
            at = 0
            for d, fields in enumerate(FIELDS_Y):
                y = 7 - d if side else d
                for f in fields:
                    out[at : at + 8] = core[f, pl.ds(y, 8, stride=8), :]
                    at += 8
            for d in range(3):
                y = 7 - d if side else d
                for f in ALL:
                    out[at : at + 1] = beside_z[f, y : y + 1]
                    at += 1

    by_side("gy", to_one, to_other, send)


def x_kernel(core, beside_z, from_one, from_other, beside_y, corner, to_one, to_other):
    sub, lane = iota((8, 128), 0), iota((8, 128), 1)
    beside_y[...] = jnp.zeros(beside_y.shape, F32)
    corner[...] = jnp.zeros(corner.shape, F32)

    def receive(pairs):
        for source, side in pairs:
            at = 0
            for d, fields in enumerate(FIELDS_Y):
                row = d if side else 7 - d
                for f in fields:
                    into = f ^ 1 if f < 4 else f
                    beside_y[into, pl.ds(row, 8, stride=8), :] = source[at : at + 8]
                    at += 8
            for d in range(3):
                row = d if side else 7 - d
                for f in ALL:
                    into = f ^ 1 if f < 4 else f
                    corner[into, row : row + 1] = source[at : at + 1]
                    at += 1

    by_side("gy", from_one, from_other, receive)

    def send(pairs):
        for out, side in pairs:
            at = 0
            for d, fields in enumerate(FIELDS_X):
                x = 7 - d if side else d
                for f in fields:
                    out[at : at + 8] = core[f, 8 * x : 8 * x + 8]
                    at += 8
            first, second = (7, 6) if side else (0, 1)
            for f in ALL:
                out[at : at + 8] = jnp.where(
                    (sub == 2) | (sub == 3),
                    roll(beside_y[f, 8 * second : 8 * second + 8], 3, 0),
                    beside_y[f, 8 * first : 8 * first + 8],
                )
                at += 8
            for f in ALL:
                out[at : at + 8] = jnp.where(
                    (lane >= 48) & (lane < 80), roll(corner[f], -48 if side else 48, 1), beside_z[f]
                )
                at += 8

    by_side("gx", to_one, to_other, send)


def harmonic(first, second):
    total = first + second
    return 2.0 * first * second / jnp.where(total > 0.0, total, 1.0)


def unpacked(value, slot):
    lane = iota((8, 128), 1)
    value = roll(value, -16 * slot, 1)
    return jnp.where(lane < 3, value, jnp.where(lane >= 117, roll(value, 112, 1), 0.0))


class Planes:
    def __init__(self, inner, outer, first):
        self.inner, self.outer, self.first, self.last = inner, outer, first, 13 - first

    def at(self, p, shift=0):
        if self.first <= p <= self.last - shift:
            return self.inner, p - self.first
        return self.outer, p


def read(planes, p, f=None, tall=16, shift=0):
    ref, p = planes.at(p, shift)
    return ref[p, 0:tall] if f is None else ref[f, p, 0:tall]


def write(planes, value, p, f=None, shift=0):
    ref, p = planes.at(p, shift)
    rows = value.shape[0]
    if f is None:
        ref[p, 0:rows] = value
    else:
        ref[f, p, 0:rows] = value


class Block:
    def __init__(self, inner, outer):
        names = ("ext", "face_x", "near_x", "face_y", "face_z", "near_y", "near_z", "rest", "weight", "once", "twice")
        first = (3, 3, 3, 3, 3, 3, 3, 3, 4, 4, 5)
        for i, name in enumerate(names):
            setattr(self, name, Planes(inner[i], outer[i] if outer else None, first[i]))
        self.row, self.column = iota((16, 256), 0), iota((16, 256), 1)

    def cells(self, f, p, tall=16):
        return read(self.ext, p, f, tall)

    def side_x(self, planes, p, tall=16):
        return read(planes, p, None, tall, 1)

    def faces_x(self, planes):
        for p in planes:
            face = harmonic(self.cells(PX, p), self.cells(PX, p + 1))
            write(self.face_x, face, p, None, 1)
            write(self.near_x, jnp.where(self.cells(LAYER, p) == self.cells(LAYER, p + 1), face, 0.0), p, None, 1)

    def faces(self, planes):
        for p in planes:
            ids = self.cells(LAYER, p)
            total = self.cells(STORAGE, p)
            for f, axis, face_at, near_at in ((PY, 0, self.face_y, self.near_y), (PZ, 1, self.face_z, self.near_z)):
                across = self.cells(f, p)
                face = harmonic(across, roll(across, -1, axis))
                write(face_at, face, p)
                write(near_at, jnp.where(ids == roll(ids, -1, axis), face, 0.0), p)
                total = total + (face + roll(face, 1, axis))
            write(self.rest, total, p)

    def diagonal(self, p):
        return read(self.rest, p) + (self.side_x(self.face_x, p - 1) + self.side_x(self.face_x, p))

    def weights(self, planes):
        for p in planes:
            total = self.diagonal(p)
            write(self.weight, (2.0 / 3.0) / jnp.where(total > 0.0, total, 1.0), p)

    def relax(self, planes, source, target):
        gx, gy = lax.axis_index("gx"), lax.axis_index("gy")
        nx, ny = lax.axis_size("gx"), lax.axis_size("gy")
        row = self.row
        y_valid = jnp.where((row < 4) | (row >= 12), (gy > 0).astype(F32), (gy < ny - 1).astype(F32))
        for p in planes:
            tall = 8 if (source is self.ext and p in (1, 12)) or (source is self.once and p in (2, 11)) else 16
            x_valid = ((gx > 0) if p < 7 else (gx < nx - 1)).astype(F32)
            near_y, near_z = read(self.near_y, p), read(self.near_z, p, None, tall)
            near_y_other = jnp.where(row == 3, 0.0, near_y)
            low, high = self.side_x(self.near_x, p - 1, tall), self.side_x(self.near_x, p, tall)
            scale = read(self.weight, p, None, tall)
            scale_other = scale * y_valid[0:tall]
            updated = []
            for f in range(4):
                whole = read(source, p, f)
                own = whole[0:tall]
                side = near_y_other if f & 1 else near_y
                total = side[0:tall] * roll(whole, -1, 0)[0:tall] + roll(side * whole, 1, 0)[0:tall]
                total = total + (near_z * roll(own, -1, 1) + roll(near_z * own, 1, 1))
                if not (f & 2 and p == 7):
                    total = total + low * read(source, p - 1, f, tall)
                if not (f & 2 and p == 6):
                    total = total + high * read(source, p + 1, f, tall)
                factor = scale_other if f & 1 else scale
                if f & 2:
                    factor = factor * x_valid
                updated.append(own * (1.0 / 3.0) + factor * total)
            total = (updated[0] + updated[1]) + (updated[2] + updated[3])
            inverse = 1.0 / jnp.where(total > 0.0, total, 1.0)
            for f in range(4):
                write(target, updated[f] * inverse, p, f)

    def coarse_parts(self, planes, parts):
        row, column = self.row, self.column
        octet = (jnp.where(column < 192, column, column - 256) + 256) // BLOCK - 32
        octet = (octet + lax.axis_index("gz") * (128 // BLOCK)).astype(F32)
        in_block = row < 8
        for p in planes:
            inside = 3 <= p <= 10
            tall = 16 if inside else 8
            ids = self.cells(LAYER, p, tall)
            lifted = ids > octet[0:tall]
            keep = in_block[0:tall]
            given = []
            if p >= 4:
                given.append((self.side_x(self.face_x, p - 1, tall), self.cells(LAYER, p - 1, tall), keep))
            if p <= 9:
                given.append((self.side_x(self.face_x, p, tall), self.cells(LAYER, p + 1, tall), keep))
            total = [jnp.zeros((tall, 256), F32) for _ in range(3)]
            if inside:
                face = read(self.face_y, p)
                given.append((face, roll(ids, -1, 0), (row < 7) | (row == 15)))
                given.append((roll(face, 1, 0), roll(ids, 1, 0), (row > 0) & (row < 9)))
                face = read(self.face_z, p)
                given.append((face, roll(ids, -1, 1), keep))
                given.append((roll(face, 1, 1), roll(ids, 1, 1), keep))
                total[1] = jnp.where(keep, self.diagonal(p), 0.0)
            for face, beside, kept in given:
                face = jnp.where(kept, face, 0.0)
                step = beside - ids
                total[0] = total[0] - jnp.where(step == 1.0, face, 0.0)
                total[1] = total[1] - jnp.where(step == 0.0, face, 0.0)
                total[2] = total[2] - jnp.where(step == -1.0, face, 0.0)
            for oz in range(3):
                upper = jnp.where(lifted, total[oz], 0.0)
                parts[oz, 0, p, 0:tall] = total[oz] - upper
                parts[oz, 1, p, 0:tall] = upper

    def coarse_sums(self, planes, parts, sums):
        for oz in range(3):
            for lift in range(2):
                for f in range(4):
                    groups = (planes,) if f < 2 else ([p for p in planes if p < 7], [p for p in planes if p >= 7])
                    for i, group in enumerate(groups):
                        top = bottom = None
                        for p in group:
                            value = parts[oz, lift, p, 0:8] * read(self.twice, p, f, 8)
                            top = value if top is None else top + value
                            if 3 <= p <= 10:
                                ref, at = self.twice.at(p)
                                value = parts[oz, lift, p, 8:16] * ref[f, at, 8:16]
                                bottom = value if bottom is None else bottom + value
                        ox = 1 if f < 2 else 2 * i
                        sums[oz, lift, ox, f & 1] = top + (roll(bottom, 4, 0) if f & 1 else bottom)


def inner_kernel(core, beside_z, beside_y, corner, *refs):
    arrays, parts, sums = refs[:11], refs[12], refs[11]
    ext = arrays[0]
    for f in ALL:
        for x in range(8):
            ext[f, x, 0:8, 0:128] = core[f, 8 * x : 8 * x + 8]
            ext[f, x, 8:16, 0:128] = beside_y[f, 8 * x : 8 * x + 8]
            ext[f, x, 0:8, 128:256] = unpacked(beside_z[f], x)
            ext[f, x, 8:16, 128:256] = unpacked(corner[f], x)
    block = Block(arrays, None)
    block.faces_x(range(3, 10))
    block.faces(range(3, 11))
    block.weights(range(4, 10))
    block.relax(range(4, 10), block.ext, block.once)
    block.relax(range(5, 9), block.once, block.twice)
    block.coarse_parts(range(5, 9), parts)
    block.coarse_sums(list(range(5, 9)), parts, sums)


def outer_kernel(from_one, from_other, *refs):
    arrays, inner_sums = refs[:11], refs[11]
    smoothed_hbm, coarse = refs[12:14]
    outer = refs[14:25]
    parts, sums, smoothed, sem = refs[25:]
    ext = outer[0]
    gx, gy = lax.axis_index("gx"), lax.axis_index("gy")
    sub = iota((8, 128), 0)
    zero = jnp.zeros((8, 128), F32)

    def receive(pairs):
        for source, side in pairs:
            at = 0
            for d in range(3):
                plane = 11 + d if side else 2 - d
                for f in ALL:
                    into = f ^ 2 if f < 4 else f
                    if f in FIELDS_X[d]:
                        ext[into, plane, 0:8, 0:128] = source[at : at + 8]
                        at += 8
                    else:
                        ext[into, plane, 0:8, 0:128] = zero
            for f in ALL:
                into = f ^ 2 if f < 4 else f
                rows = source[at : at + 8]
                across = source[at + 72 : at + 80]
                at += 8
                lateral = roll(across, -48 if side else 48, 1)
                for d in range(3):
                    plane = 11 + d if side else 2 - d
                    slot = d if side else 7 - d
                    ext[into, plane, 0:8, 128:256] = unpacked(across, slot)
                    if d == 0:
                        ext[into, plane, 8:16, 0:128] = jnp.where((sub < 2) | (sub > 5), rows, 0.0)
                    elif d == 1:
                        ext[into, plane, 8:16, 0:128] = jnp.where((sub < 1) | (sub > 6), roll(rows, -3, 0), 0.0)
                    else:
                        ext[into, plane, 8:16, 0:128] = zero
                    ext[into, plane, 8:16, 128:256] = unpacked(lateral, slot) if d < 2 else zero

    by_side("gx", from_one, from_other, receive)
    block = Block(arrays, outer)
    block.faces_x((0, 1, 2, 10, 11, 12))
    block.faces((1, 2, 11, 12))
    block.weights((1, 2, 3, 10, 11, 12))
    block.relax((1, 2, 3, 10, 11, 12), block.ext, block.once)
    block.relax((2, 3, 4, 9, 10, 11), block.once, block.twice)

    rx_own, rx_low, rx_high = gx % 3, (gx + 2) % 3, (gx + 1) % 3
    ry_own, ry_low, ry_high = gy % 3, (gy + 2) % 3, (gy + 1) % 3
    for x in range(8):
        ids = block.cells(LAYER, x + 3, 8)[:, 0:128]
        residue = ids - 3.0 * jnp.floor((ids + 0.5) * (1.0 / 3.0))
        rx_other, rx_none = (rx_low, rx_high) if x < 4 else (rx_high, rx_low)
        for ex, rx in ((0, rx_own), (1, rx_other)):
            own = read(block.twice, x + 3, 2 * ex, 8)[:, 0:128]
            other = read(block.twice, x + 3, 2 * ex + 1, 8)[:, 0:128]
            low = jnp.where(sub < 4, other, 0.0)
            high = other - low
            for rz in range(3):
                hit = jnp.abs(residue - rz) < 0.5
                smoothed[9 * rz + 3 * ry_own + rx, x] = jnp.where(hit, own, 0.0)
                smoothed[9 * rz + 3 * ry_low + rx, x] = jnp.where(hit, low, 0.0)
                smoothed[9 * rz + 3 * ry_high + rx, x] = jnp.where(hit, high, 0.0)
        for rz in range(3):
            for ry in range(3):
                smoothed[9 * rz + 3 * ry + rx_none, x] = zero
    copy = pltpu.make_async_copy(smoothed, smoothed_hbm, sem)
    copy.start()

    block.coarse_parts((2, 3, 4, 9, 10, 11), parts)
    block.coarse_sums([2, 3, 4, 9, 10, 11], parts, sums)
    spot = iota((16, 256), 1)
    place = (jnp.where(spot < 192, spot, spot - 256) + 256) // BLOCK - 32
    for oz in range(3):
        total = jnp.zeros((16, 16), F32)
        for lift in range(2):
            rows = []
            for oy in range(3):
                for ox in range(3):
                    ey = 0 if oy == 1 else 1
                    value = sums[oz, lift, ox, ey] + inner_sums[oz, lift, ox, ey]
                    if oy != 1:
                        value = value[0:4] if oy == 0 else value[4:8]
                    rows.append(jnp.sum(value, axis=0, keepdims=True))
            rows.append(jnp.zeros((7, 256), F32))
            chosen = (place + lift - (oz - 1) == iota((16, 256), 0)).astype(F32)
            total = total + lax.dot_general(
                chosen,
                jnp.concatenate(rows, axis=0),
                (((1,), (1,)), ((), ())),
                precision=lax.Precision.HIGHEST,
                preferred_element_type=F32,
            )
        coarse[:, 9 * oz : 9 * oz + 9] = total[:, 0:9] * (1.0 / (BLOCK * BLOCK))
    copy.wait()


VMEM = pl.BlockSpec(memory_space=pltpu.VMEM)
HBM = pl.BlockSpec(memory_space=pltpu.HBM)


def call(kernel, outs, *operands, in_specs=None, out_specs=None, scratch=(), vmem=48 * 1024 * 1024):
    return pl.pallas_call(
        kernel,
        out_shape=[jax.ShapeDtypeStruct(shape, F32) for shape in outs],
        in_specs=in_specs or [VMEM] * len(operands),
        out_specs=out_specs or [VMEM] * len(outs),
        scratch_shapes=scratch,
        compiler_params=pltpu.CompilerParams(vmem_limit_bytes=vmem),
    )(*operands)


def exchange(axis, to_one, to_other):
    count = lax.axis_size(axis)
    one = [(i, i ^ 1) for i in range(count)]
    other = [(i, ((i + 1) ^ 1) - 1) for i in range(1, count - 1)]
    from_other = lax.ppermute(to_other, axis, other)
    return lax.ppermute(to_one, axis, one), from_other


def per_device(basis, perm, storage, layer):
    block = (FIELDS, 64, 128)
    side = (FIELDS, 8, 128)
    core, edge = call(
        pack_kernel,
        (block, side),
        basis.reshape(27, 64, 128),
        perm.reshape(3, 64, 128),
        storage.reshape(64, 128),
        layer.reshape(64, 128),
        in_specs=[HBM] * 4,
        vmem=None,
        scratch=[pltpu.VMEM((27, 64, 128), F32), pltpu.VMEM((64, 128), jnp.int32), pltpu.SemaphoreType.DMA((4,))],
    )
    one, other = exchange("gz", edge, edge)
    rows = (ROWS_Y + 32, 128)
    beside_z, to_one, to_other = call(y_kernel, (side, rows, rows), core, one, other)
    one, other = exchange("gy", to_one, to_other)
    rows = (ROWS_X + 144, 128)
    beside_y, corner, to_one, to_other = call(x_kernel, (block, side, rows, rows), core, beside_z, one, other)
    one, other = exchange("gx", to_one, to_other)

    def arrays(planes):
        return [
            (FIELDS, planes(3), 16, 256),
            (planes(3), 16, 256),
            (planes(3), 16, 256),
            (planes(3), 16, 256),
            (planes(3), 16, 256),
            (planes(3), 16, 256),
            (planes(3), 16, 256),
            (planes(3), 16, 256),
            (planes(4), 16, 256),
            (4, planes(4), 16, 256),
            (4, planes(5), 16, 256),
        ]

    parts = pltpu.VMEM((3, 2, 14, 16, 256), F32)
    sums = (3, 2, 3, 2, 8, 256)
    inner = call(
        inner_kernel, arrays(lambda first: 14 - 2 * first) + [sums], core, beside_z, beside_y, corner, scratch=[parts]
    )
    smoothed, coarse = call(
        outer_kernel,
        ((27, 8, 8, 128), (16, 27)),
        one,
        other,
        *inner,
        out_specs=[HBM, VMEM],
        scratch=[pltpu.VMEM(shape, F32) for shape in arrays(lambda first: 14)]
        + [parts, pltpu.VMEM(sums, F32), pltpu.VMEM((27, 8, 8, 128), F32), pltpu.SemaphoreType.DMA],
    )
    return smoothed, coarse.T.reshape(27, 1, 1, 16)


def solution(mesh):
    return jax.shard_map(
        per_device,
        mesh=mesh,
        in_specs=(
            P(None, "gx", "gy", "gz"),
            P(None, "gx", "gy", "gz"),
            P("gx", "gy", "gz"),
            P("gx", "gy", "gz"),
        ),
        out_specs=(P(None, "gx", "gy", "gz"), P(None, "gx", "gy", "gz")),
        check_vma=False,
    )
```

time: 197 us -> 42.8 us (0.22)
  the two profiles are of different devices: /device:TPU:385 before, /device:TPU:18 now
where the time goes in v2:
time: 42.8 us; the launch traced here: 42.5 us
  starting transfers between devices  25.6 us (60%)
  waiting for transfers between devices  7.88 us (18%)
  Pallas kernels  7.27 us (17%)
  local copies, waits for them, and re-layouts  0.96 us (2%)
  between operations  0.72 us (2%)
    ppermute x3, starting transfers between devices, exchange(): return (lax.ppermute(to_one, axis, one), from_other)  18.7 us
    pallas_call x5, Pallas kernels, call(): pl.pallas_call(kernel, out_shape=[jax.ShapeDtypeStruct(shape, F32) for sh...  7.27 us
    ppermute x3, starting transfers between devices, exchange(): from_other = lax.ppermute(to_other, axis, other)  6.94 us
    ppermute x3, waiting for transfers between devices, exchange(): from_other = lax.ppermute(to_other, axis, other)  6.36 us
    ppermute x3, waiting for transfers between devices, exchange(): return (lax.ppermute(to_one, axis, one), from_other)  1.52 us
    unnamed x2, local copies, waits for them, and re-layouts  0.96 us
  transfers between devices with their start and end apart: 6, of which 4 were waited for; matrix products, arithmetic and copies ran while one was open for 0% of the time, Pallas kernels for 4%

profile of v2, /device:TPU:18, one launch (start us, length us, event | category | flops | bytes accessed | tf_op | source)
XLA Modules:
  0.0 42.5 jit_solution(11231736095148094144)
XLA Ops:
  0.6 2.1 %shard_map.59 = (f32[9,64,128]{2,1,0:T(8,128)}, f32[9,8,128]{2,1,0:T(8,128)}) custom-call(f32[27,64,128]{2,1,0:T(8,128)} %bitcast.7, f32[3,64,128]{2,1,0:T(8,128)} %bitcast.8, f32[64,128]{1,0:T(8,128)} %bitcast.9, s32[64,128]{1,0:T(8,128)} %bitcast.10), custom_call_target="tpu_custom_call" | custom-call | tf_op jit(solution)/shard_map/pallas_call | solution.py:442
  2.7 0.7 %collective-permute-start.1 = (f32[9,8,128]{2,1,0:T(8,128)}, f32[9,8,128]{2,1,0:T(8,128)S(1)}, u32[]{:S(2)}, u32[]{:S(2)}) collective-permute-start(f32[9,8,128]{2,1,0:T(8,128)} %get-tuple-element.26), channel_id=1, source_target_pairs={{1,2},{2,1},{3,4},{4,3},{5,6},{6,5},{7,8},{8,7},{9,10},{10,9},{11,... | collective-permute-start | bytes 110600 | tf_op jit(solution)/shard_map/ppermute | solution.py:456
  3.4 6.5 %collective-permute-start = (f32[9,8,128]{2,1,0:T(8,128)}, f32[9,8,128]{2,1,0:T(8,128)S(1)}, u32[]{:S(2)}, u32[]{:S(2)}) collective-permute-start(f32[9,8,128]{2,1,0:T(8,128)} %get-tuple-element.26), channel_id=1, source_target_pairs={{0,1},{1,0},{2,3},{3,2},{4,5},{5,4},{6,7},{7,6},{8,9},{9,8},{10,11... | collective-permute-start | bytes 110600 | tf_op jit(solution)/shard_map/ppermute | solution.py:457
  10.0 0.0 collective-permute-done.1.from_other
  10.0 1.0 %collective-permute-done.from_one = f32[9,8,128]{2,1,0:T(8,128)S(1)} collective-permute-done((f32[9,8,128]{2,1,0:T(8,128)}, f32[9,8,128]{2,1,0:T(8,128)S(1)}, u32[]{:S(2)}, u32[]{:S(2)}) %collective-permute-start) | collective-permute-done | bytes 36896 | tf_op jit(solution)/shard_map/ppermute | solution.py:457
  11.0 0.0 copy-start
  11.0 1.0 %copy-done = f32[9,64,128]{2,1,0:T(8,128)S(1)} copy-done((f32[9,64,128]{2,1,0:T(8,128)S(1)}, f32[9,64,128]{2,1,0:T(8,128)}, u32[]{:S(2)}) %copy-start) | copy-done | bytes 294936
  12.0 0.1 shard_map.60
  12.1 2.4 %collective-permute-start.2 = (f32[224,128]{1,0:T(8,128)S(1)}, f32[224,128]{1,0:T(8,128)S(1)}, u32[]{:S(2)}, u32[]{:S(2)}) collective-permute-start(f32[224,128]{1,0:T(8,128)S(1)} %get-tuple-element.28), channel_id=1, source_target_pairs={{0,16},{16,0},{32,48},{48,32},{64,80},{80,64},{96,112},{112,96},{1... | collective-permute-start | bytes 344072 | tf_op jit(solution)/shard_map/ppermute | solution.py:457
  14.5 4.4 %collective-permute-start.3 = (f32[224,128]{1,0:T(8,128)S(1)}, f32[224,128]{1,0:T(8,128)S(1)}, u32[]{:S(2)}, u32[]{:S(2)}) collective-permute-start(f32[224,128]{1,0:T(8,128)S(1)} %get-tuple-element.29), channel_id=1, source_target_pairs={{16,32},{32,16},{48,64},{64,48},{80,96},{96,80},{17,33},{33,17},{4... | collective-permute-start | bytes 344072 | tf_op jit(solution)/shard_map/ppermute | solution.py:456
  18.9 0.5 %collective-permute-done.2.from_one = f32[224,128]{1,0:T(8,128)S(1)} collective-permute-done((f32[224,128]{1,0:T(8,128)S(1)}, f32[224,128]{1,0:T(8,128)S(1)}, u32[]{:S(2)}, u32[]{:S(2)}) %collective-permute-start.2) | collective-permute-done | bytes 114720 | tf_op jit(solution)/shard_map/ppermute | solution.py:457
  19.4 2.9 %collective-permute-done.3.from_other = f32[224,128]{1,0:T(8,128)S(1)} collective-permute-done((f32[224,128]{1,0:T(8,128)S(1)}, f32[224,128]{1,0:T(8,128)S(1)}, u32[]{:S(2)}, u32[]{:S(2)}) %collective-permute-start.3) | collective-permute-done | bytes 114720 | tf_op jit(solution)/shard_map/ppermute | solution.py:456
  22.2 0.2 shard_map.61
  22.4 9.7 %collective-permute-start.4 = (f32[336,128]{1,0:T(8,128)S(1)}, f32[336,128]{1,0:T(8,128)S(1)}, u32[]{:S(2)}, u32[]{:S(2)}) collective-permute-start(f32[336,128]{1,0:T(8,128)S(1)} %get-tuple-element.30), channel_id=1, source_target_pairs={{0,128},{128,0},{256,384},{384,256},{512,640},{640,512},{768,896},... | collective-permute-start | bytes 516104 | tf_op jit(solution)/shard_map/ppermute | solution.py:457
  32.1 1.9 %collective-permute-start.5 = (f32[336,128]{1,0:T(8,128)S(1)}, f32[336,128]{1,0:T(8,128)S(1)}, u32[]{:S(2)}, u32[]{:S(2)}) collective-permute-start(f32[336,128]{1,0:T(8,128)S(1)} %get-tuple-element.31), channel_id=1, source_target_pairs={{128,256},{256,128},{384,512},{512,384},{640,768},{768,640},{129,2... | collective-permute-start | bytes 516104 | tf_op jit(solution)/shard_map/ppermute | solution.py:456
  34.1 1.9 %shard_map.62 = (f32[9,8,16,256]{3,2,1,0:T(8,128)S(1)}, f32[8,16,256]{2,1,0:T(8,128)S(1)}, f32[8,16,256]{2,1,0:T(8,128)S(1)}, f32[8,16,256]{2,1,0:T(8,128)S(1)},...) custom-call(f32[9,64,128]{2,1,0:T(8,128)S(1)} %copy-done, ...), custom_call_target="tpu_custom_call" | custom-call | tf_op jit(solution)/shard_map/pallas_call | solution.py:442
  35.9 0.0 collective-permute-done.4.from_one
  36.0 3.5 %collective-permute-done.5.from_other = f32[336,128]{1,0:T(8,128)S(1)} collective-permute-done((f32[336,128]{1,0:T(8,128)S(1)}, f32[336,128]{1,0:T(8,128)S(1)}, u32[]{:S(2)}, u32[]{:S(2)}) %collective-permute-start.5) | collective-permute-done | bytes 172064 | tf_op jit(solution)/shard_map/ppermute | solution.py:456
  39.4 3.0 %shard_map.63 = (f32[27,8,8,128]{3,2,1,0:T(8,128)}, f32[16,27]{1,0:T(8,128)}) custom-call(f32[336,128]{1,0:T(8,128)S(1)} %collective-permute-done.4.from_one, f32[336,128]{1,0:T(8,128)S(1)} %collective-permute-done.5.from_other, f32[9,8,16,256]{3,2,1,0:T(8,128)S(1)} %get-tuple-element.34.refs_0_, f32[8,16,256]{2,1,0:T(8,128)S(1)} %get-tuple-element.35.refs_1_, ...), custom_call_target="tpu_custom_call" | custom-call | tf_op jit(solution)/shard_map/pallas_call | solution.py:442
Async XLA Ops:
  2.7 7.2 %collective-permute-start.1 = (f32[9,8,128]{2,1,0:T(8,128)}, f32[9,8,128]{2,1,0:T(8,128)S(1)}, u32[]{:S(2)}, u32[]{:S(2)}) collective-permute-start(f32[9,8,128]{2,1,0:T(8,128)} %get-tuple-element.26), channel_id=1, source_target_pairs={{1,2},{2,1},{3,4},{4,3},{5,6},{6,5},{7,8},{8,7},{9,10},{10,9},{11,... | collective-permute-start | bytes 110600 | tf_op jit(solution)/shard_map/ppermute | solution.py:456
  3.4 7.6 %collective-permute-start = (f32[9,8,128]{2,1,0:T(8,128)}, f32[9,8,128]{2,1,0:T(8,128)S(1)}, u32[]{:S(2)}, u32[]{:S(2)}) collective-permute-start(f32[9,8,128]{2,1,0:T(8,128)} %get-tuple-element.26), channel_id=1, source_target_pairs={{0,1},{1,0},{2,3},{3,2},{4,5},{5,4},{6,7},{7,6},{8,9},{9,8},{10,11... | collective-permute-start | bytes 110600 | tf_op jit(solution)/shard_map/ppermute | solution.py:457
  11.0 1.0 %copy-start = (f32[9,64,128]{2,1,0:T(8,128)S(1)}, f32[9,64,128]{2,1,0:T(8,128)}, u32[]{:S(2)}) copy-start(f32[9,64,128]{2,1,0:T(8,128)} %get-tuple-element.25.core) | copy-start | bytes 884740
  12.1 7.3 %collective-permute-start.2 = (f32[224,128]{1,0:T(8,128)S(1)}, f32[224,128]{1,0:T(8,128)S(1)}, u32[]{:S(2)}, u32[]{:S(2)}) collective-permute-start(f32[224,128]{1,0:T(8,128)S(1)} %get-tuple-element.28), channel_id=1, source_target_pairs={{0,16},{16,0},{32,48},{48,32},{64,80},{80,64},{96,112},{112,96},{1... | collective-permute-start | bytes 344072 | tf_op jit(solution)/shard_map/ppermute | solution.py:457
  14.5 7.7 %collective-permute-start.3 = (f32[224,128]{1,0:T(8,128)S(1)}, f32[224,128]{1,0:T(8,128)S(1)}, u32[]{:S(2)}, u32[]{:S(2)}) collective-permute-start(f32[224,128]{1,0:T(8,128)S(1)} %get-tuple-element.29), channel_id=1, source_target_pairs={{16,32},{32,16},{48,64},{64,48},{80,96},{96,80},{17,33},{33,17},{4... | collective-permute-start | bytes 344072 | tf_op jit(solution)/shard_map/ppermute | solution.py:456
  22.4 13.5 %collective-permute-start.4 = (f32[336,128]{1,0:T(8,128)S(1)}, f32[336,128]{1,0:T(8,128)S(1)}, u32[]{:S(2)}, u32[]{:S(2)}) collective-permute-start(f32[336,128]{1,0:T(8,128)S(1)} %get-tuple-element.30), channel_id=1, source_target_pairs={{0,128},{128,0},{256,384},{384,256},{512,640},{640,512},{768,896},... | collective-permute-start | bytes 516104 | tf_op jit(solution)/shard_map/ppermute | solution.py:457
  32.1 7.3 %collective-permute-start.5 = (f32[336,128]{1,0:T(8,128)S(1)}, f32[336,128]{1,0:T(8,128)S(1)}, u32[]{:S(2)}, u32[]{:S(2)}) collective-permute-start(f32[336,128]{1,0:T(8,128)S(1)} %get-tuple-element.31), channel_id=1, source_target_pairs={{128,256},{256,128},{384,512},{512,384},{640,768},{768,640},{129,2... | collective-permute-start | bytes 516104 | tf_op jit(solution)/shard_map/ppermute | solution.py:456

commit v3 on v2

--- a/solution.py
+++ b/solution.py
@@ -24,7 +24,7 @@
     return pltpu.roll(value, shift % value.shape[axis], axis)
 
 
-def pack_kernel(basis_hbm, perm_hbm, storage_hbm, layer_hbm, core, edge, basis, layer, sems):
+def pack_kernel(basis_hbm, perm_hbm, storage_hbm, layer_hbm, core_hbm, edge_hbm, core, edge, basis, layer, sems):
     copies = [
         pltpu.make_async_copy(source, target, sems.at[i])
         for i, (source, target) in enumerate(
@@ -68,6 +68,8 @@
                 own, other = own * x_valid, other * x_valid
             core[2 * ex, 8 * x : 8 * x + 8] = own
             core[2 * ex + 1, 8 * x : 8 * x + 8] = other
+    keep = [pltpu.make_async_copy(core, core_hbm, sems.at[4]), pltpu.make_async_copy(edge, edge_hbm, sems.at[5])]
+    keep[0].start()
     for f in ALL:
         packed = jnp.zeros((8, 128), F32)
         for x in range(8):
@@ -75,6 +77,13 @@
             value = jnp.where(lane < 4, value, roll(value, 16, 1))
             packed = jnp.where(lane // 16 == x, roll(value, 16 * x, 1), packed)
         edge[f] = packed
+    keep[1].start()
+    for copy in keep:
+        copy.wait()
+
+
+def load_kernel(core_hbm, core):
+    core[...] = core_hbm[...]
 
 
 def by_side(axis, one, other, body):
@@ -230,43 +239,62 @@
             total = self.diagonal(p)
             write(self.weight, (2.0 / 3.0) / jnp.where(total > 0.0, total, 1.0), p)
 
-    def relax(self, planes, source, target):
+    def height(self, p, source):
+        return 8 if p in ((1, 12) if source is self.ext else (2, 11)) else 16
+
+    def beside(self, p, source, low=True, high=True):
+        tall = self.height(p, source)
+        near_y, near_z = read(self.near_y, p), read(self.near_z, p, None, tall)
+        near_y_other = jnp.where(self.row == 3, 0.0, near_y)
+        totals = []
+        for f in range(4):
+            whole = read(source, p, f)
+            own = whole[0:tall]
+            side = near_y_other if f & 1 else near_y
+            total = side[0:tall] * roll(whole, -1, 0)[0:tall] + roll(side * whole, 1, 0)[0:tall]
+            totals.append(total + (near_z * roll(own, -1, 1) + roll(near_z * own, 1, 1)))
+        return self.beside_x(p, source, totals, low, high)
+
+    def beside_x(self, p, source, totals, low=False, high=False):
+        tall = self.height(p, source)
+        totals = list(totals)
+        if low:
+            face = self.side_x(self.near_x, p - 1, tall)
+            for f in range(2 if p == 7 else 4):
+                totals[f] = totals[f] + face * read(source, p - 1, f, tall)
+        if high:
+            face = self.side_x(self.near_x, p, tall)
+            for f in range(2 if p == 6 else 4):
+                totals[f] = totals[f] + face * read(source, p + 1, f, tall)
+        return totals
+
+    def relax(self, p, source, target, totals):
         gx, gy = lax.axis_index("gx"), lax.axis_index("gy")
         nx, ny = lax.axis_size("gx"), lax.axis_size("gy")
+        tall = self.height(p, source)
+        row = self.row[0:tall]
+        y_valid = jnp.where((row < 4) | (row >= 12), (gy > 0).astype(F32), (gy < ny - 1).astype(F32))
+        x_valid = ((gx > 0) if p < 7 else (gx < nx - 1)).astype(F32)
+        scale = read(self.weight, p, None, tall)
+        scale_other = scale * y_valid
+        updated = []
+        for f in range(4):
+            factor = scale_other if f & 1 else scale
+            if f & 2:
+                factor = factor * x_valid
+            updated.append(read(source, p, f, tall) * (1.0 / 3.0) + factor * totals[f])
+        total = (updated[0] + updated[1]) + (updated[2] + updated[3])
+        inverse = 1.0 / jnp.where(total > 0.0, total, 1.0)
+        for f in range(4):
+            write(target, updated[f] * inverse, p, f)
+
+    def sweep(self, planes, source, target):
+        for p in planes:
+            self.relax(p, source, target, self.beside(p, source))
+
+    def coarse_parts(self, planes, parts):
         row = self.row
-        y_valid = jnp.where((row < 4) | (row >= 12), (gy > 0).astype(F32), (gy < ny - 1).astype(F32))
-        for p in planes:
-            tall = 8 if (source is self.ext and p in (1, 12)) or (source is self.once and p in (2, 11)) else 16
-            x_valid = ((gx > 0) if p < 7 else (gx < nx - 1)).astype(F32)
-            near_y, near_z = read(self.near_y, p), read(self.near_z, p, None, tall)
-            near_y_other = jnp.where(row == 3, 0.0, near_y)
-            low, high = self.side_x(self.near_x, p - 1, tall), self.side_x(self.near_x, p, tall)
-            scale = read(self.weight, p, None, tall)
-            scale_other = scale * y_valid[0:tall]
-            updated = []
-            for f in range(4):
-                whole = read(source, p, f)
-                own = whole[0:tall]
-                side = near_y_other if f & 1 else near_y
-                total = side[0:tall] * roll(whole, -1, 0)[0:tall] + roll(side * whole, 1, 0)[0:tall]
-                total = total + (near_z * roll(own, -1, 1) + roll(near_z * own, 1, 1))
-                if not (f & 2 and p == 7):
-                    total = total + low * read(source, p - 1, f, tall)
-                if not (f & 2 and p == 6):
-                    total = total + high * read(source, p + 1, f, tall)
-                factor = scale_other if f & 1 else scale
-                if f & 2:
-                    factor = factor * x_valid
-                updated.append(own * (1.0 / 3.0) + factor * total)
-            total = (updated[0] + updated[1]) + (updated[2] + updated[3])
-            inverse = 1.0 / jnp.where(total > 0.0, total, 1.0)
-            for f in range(4):
-                write(target, updated[f] * inverse, p, f)
-
-    def coarse_parts(self, planes, parts):
-        row, column = self.row, self.column
-        octet = (jnp.where(column < 192, column, column - 256) + 256) // BLOCK - 32
-        octet = (octet + lax.axis_index("gz") * (128 // BLOCK)).astype(F32)
+        octet = self.octets()
         in_block = row < 8
         for p in planes:
             inside = 3 <= p <= 10
@@ -287,7 +315,12 @@
                 face = read(self.face_z, p)
                 given.append((face, roll(ids, -1, 1), keep))
                 given.append((roll(face, 1, 1), roll(ids, 1, 1), keep))
-                total[1] = jnp.where(keep, self.diagonal(p), 0.0)
+                own = read(self.rest, p)
+                if p >= 4:
+                    own = own + self.side_x(self.face_x, p - 1)
+                if p <= 9:
+                    own = own + self.side_x(self.face_x, p)
+                total[1] = jnp.where(keep, own, 0.0)
             for face, beside, kept in given:
                 face = jnp.where(kept, face, 0.0)
                 step = beside - ids
@@ -296,10 +329,24 @@
                 total[2] = total[2] - jnp.where(step == -1.0, face, 0.0)
             for oz in range(3):
                 upper = jnp.where(lifted, total[oz], 0.0)
-                parts[oz, 0, p, 0:tall] = total[oz] - upper
-                parts[oz, 1, p, 0:tall] = upper
-
-    def coarse_sums(self, planes, parts, sums):
+                ref, at = parts.at(p)
+                ref[oz, 0, at, 0:tall] = total[oz] - upper
+                ref[oz, 1, at, 0:tall] = upper
+
+    def coarse_outer_faces(self, parts, outer_parts):
+        row, octet = self.row, self.octets()
+        for p, face in ((3, 2), (10, 10)):
+            face = jnp.where(row < 8, self.side_x(self.face_x, face), 0.0)
+            upper = jnp.where(self.cells(LAYER, p) > octet, face, 0.0)
+            ref, at = parts.at(p)
+            outer_parts[1, 0, p] = ref[1, 0, at] + (face - upper)
+            outer_parts[1, 1, p] = ref[1, 1, at] + upper
+
+    def octets(self):
+        octet = (jnp.where(self.column < 192, self.column, self.column - 256) + 256) // BLOCK - 32
+        return (octet + lax.axis_index("gz") * (128 // BLOCK)).astype(F32)
+
+    def coarse_sums(self, planes, parts, sums, changed=None):
         for oz in range(3):
             for lift in range(2):
                 for f in range(4):
@@ -307,18 +354,47 @@
                     for i, group in enumerate(groups):
                         top = bottom = None
                         for p in group:
-                            value = parts[oz, lift, p, 0:8] * read(self.twice, p, f, 8)
+                            part, spot = parts.at(p)
+                            if changed is not None and oz == 1 and p in (3, 10):
+                                part, spot = changed, p
+                            value = part[oz, lift, spot, 0:8] * read(self.twice, p, f, 8)
                             top = value if top is None else top + value
                             if 3 <= p <= 10:
                                 ref, at = self.twice.at(p)
-                                value = parts[oz, lift, p, 8:16] * ref[f, at, 8:16]
+                                value = part[oz, lift, spot, 8:16] * ref[f, at, 8:16]
                                 bottom = value if bottom is None else bottom + value
                         ox = 1 if f < 2 else 2 * i
                         sums[oz, lift, ox, f & 1] = top + (roll(bottom, 4, 0) if f & 1 else bottom)
 
 
+def store_slots(block, planes, smoothed):
+    gx, gy = lax.axis_index("gx"), lax.axis_index("gy")
+    rx_own, rx_low, rx_high = gx % 3, (gx + 2) % 3, (gx + 1) % 3
+    ry_own, ry_low, ry_high = gy % 3, (gy + 2) % 3, (gy + 1) % 3
+    sub = iota((8, 128), 0)
+    zero = jnp.zeros((8, 128), F32)
+    for i, x in enumerate(planes):
+        ids = block.cells(LAYER, x + 3, 8)[:, 0:128]
+        residue = ids - 3.0 * jnp.floor((ids + 0.5) * (1.0 / 3.0))
+        rx_other, rx_none = (rx_low, rx_high) if x < 4 else (rx_high, rx_low)
+        for ex, rx in ((0, rx_own), (1, rx_other)):
+            own = read(block.twice, x + 3, 2 * ex, 8)[:, 0:128]
+            other = read(block.twice, x + 3, 2 * ex + 1, 8)[:, 0:128]
+            low = jnp.where(sub < 4, other, 0.0)
+            high = other - low
+            for rz in range(3):
+                hit = jnp.abs(residue - rz) < 0.5
+                smoothed[9 * rz + 3 * ry_own + rx, i] = jnp.where(hit, own, 0.0)
+                smoothed[9 * rz + 3 * ry_low + rx, i] = jnp.where(hit, low, 0.0)
+                smoothed[9 * rz + 3 * ry_high + rx, i] = jnp.where(hit, high, 0.0)
+        for rz in range(3):
+            for ry in range(3):
+                smoothed[9 * rz + 3 * ry + rx_none, i] = zero
+
+
 def inner_kernel(core, beside_z, beside_y, corner, *refs):
-    arrays, parts, sums = refs[:11], refs[12], refs[11]
+    arrays, (sums, parts_ref, held_once, held_twice, smoothed_hbm) = refs[:11], refs[11:16]
+    smoothed, sem = refs[16:]
     ext = arrays[0]
     for f in ALL:
         for x in range(8):
@@ -327,22 +403,30 @@
             ext[f, x, 0:8, 128:256] = unpacked(beside_z[f], x)
             ext[f, x, 8:16, 128:256] = unpacked(corner[f], x)
     block = Block(arrays, None)
+    parts = Planes(parts_ref, None, 3)
     block.faces_x(range(3, 10))
     block.faces(range(3, 11))
     block.weights(range(4, 10))
-    block.relax(range(4, 10), block.ext, block.once)
-    block.relax(range(5, 9), block.once, block.twice)
-    block.coarse_parts(range(5, 9), parts)
+    block.sweep(range(4, 10), block.ext, block.once)
+    block.sweep(range(5, 9), block.once, block.twice)
+    store_slots(block, (2, 3, 4, 5), smoothed)
+    copy = pltpu.make_async_copy(smoothed, smoothed_hbm.at[:, 2:6], sem)
+    copy.start()
+    for held, source, first, last in ((held_once, block.ext, 3, 10), (held_twice, block.once, 4, 9)):
+        for i, p in enumerate((first, last)):
+            for f, total in enumerate(block.beside(p, source, low=i == 1, high=i == 0)):
+                held[f, i] = total
+    block.coarse_parts(range(3, 11), parts)
     block.coarse_sums(list(range(5, 9)), parts, sums)
+    copy.wait()
 
 
 def outer_kernel(from_one, from_other, *refs):
-    arrays, inner_sums = refs[:11], refs[11]
-    smoothed_hbm, coarse = refs[12:14]
-    outer = refs[14:25]
-    parts, sums, smoothed, sem = refs[25:]
+    arrays, (inner_sums, inner_parts, held_once, held_twice, _) = refs[:11], refs[11:16]
+    smoothed_hbm, coarse = refs[16:18]
+    outer = refs[18:29]
+    outer_parts, sums, smoothed, sem = refs[29:]
     ext = outer[0]
-    gx, gy = lax.axis_index("gx"), lax.axis_index("gy")
     sub = iota((8, 128), 0)
     zero = jnp.zeros((8, 128), F32)
 
@@ -381,33 +465,27 @@
     block.faces_x((0, 1, 2, 10, 11, 12))
     block.faces((1, 2, 11, 12))
     block.weights((1, 2, 3, 10, 11, 12))
-    block.relax((1, 2, 3, 10, 11, 12), block.ext, block.once)
-    block.relax((2, 3, 4, 9, 10, 11), block.once, block.twice)
-
-    rx_own, rx_low, rx_high = gx % 3, (gx + 2) % 3, (gx + 1) % 3
-    ry_own, ry_low, ry_high = gy % 3, (gy + 2) % 3, (gy + 1) % 3
-    for x in range(8):
-        ids = block.cells(LAYER, x + 3, 8)[:, 0:128]
-        residue = ids - 3.0 * jnp.floor((ids + 0.5) * (1.0 / 3.0))
-        rx_other, rx_none = (rx_low, rx_high) if x < 4 else (rx_high, rx_low)
-        for ex, rx in ((0, rx_own), (1, rx_other)):
-            own = read(block.twice, x + 3, 2 * ex, 8)[:, 0:128]
-            other = read(block.twice, x + 3, 2 * ex + 1, 8)[:, 0:128]
-            low = jnp.where(sub < 4, other, 0.0)
-            high = other - low
-            for rz in range(3):
-                hit = jnp.abs(residue - rz) < 0.5
-                smoothed[9 * rz + 3 * ry_own + rx, x] = jnp.where(hit, own, 0.0)
-                smoothed[9 * rz + 3 * ry_low + rx, x] = jnp.where(hit, low, 0.0)
-                smoothed[9 * rz + 3 * ry_high + rx, x] = jnp.where(hit, high, 0.0)
-        for rz in range(3):
-            for ry in range(3):
-                smoothed[9 * rz + 3 * ry + rx_none, x] = zero
-    copy = pltpu.make_async_copy(smoothed, smoothed_hbm, sem)
-    copy.start()
-
-    block.coarse_parts((2, 3, 4, 9, 10, 11), parts)
-    block.coarse_sums([2, 3, 4, 9, 10, 11], parts, sums)
+    steps = (
+        (held_once, block.ext, block.once, (1, 2, 11, 12), (3, 10)),
+        (held_twice, block.once, block.twice, (2, 3, 10, 11), (4, 9)),
+    )
+    for held, source, target, whole, begun in steps:
+        block.sweep(whole, source, target)
+        for i, p in enumerate(begun):
+            totals = block.beside_x(p, source, [held[f, i] for f in range(4)], low=i == 0, high=i == 1)
+            block.relax(p, source, target, totals)
+    store_slots(block, (0, 1, 6, 7), smoothed)
+    copies = [
+        pltpu.make_async_copy(smoothed.at[:, 0:2], smoothed_hbm.at[:, 0:2], sem.at[0]),
+        pltpu.make_async_copy(smoothed.at[:, 2:4], smoothed_hbm.at[:, 6:8], sem.at[1]),
+    ]
+    for copy in copies:
+        copy.start()
+
+    parts = Planes(inner_parts, outer_parts, 3)
+    block.coarse_parts((2, 11), parts)
+    block.coarse_outer_faces(parts, outer_parts)
+    block.coarse_sums([2, 3, 4, 9, 10, 11], parts, sums, outer_parts)
     spot = iota((16, 256), 1)
     place = (jnp.where(spot < 192, spot, spot - 256) + 256) // BLOCK - 32
     for oz in range(3):
@@ -431,20 +509,22 @@
                 preferred_element_type=F32,
             )
         coarse[:, 9 * oz : 9 * oz + 9] = total[:, 0:9] * (1.0 / (BLOCK * BLOCK))
-    copy.wait()
+    for copy in copies:
+        copy.wait()
 
 
 VMEM = pl.BlockSpec(memory_space=pltpu.VMEM)
 HBM = pl.BlockSpec(memory_space=pltpu.HBM)
 
 
-def call(kernel, outs, *operands, in_specs=None, out_specs=None, scratch=(), vmem=48 * 1024 * 1024):
+def call(kernel, outs, *operands, in_specs=None, out_specs=None, scratch=(), aliases=None, vmem=48 * 1024 * 1024):
     return pl.pallas_call(
         kernel,
         out_shape=[jax.ShapeDtypeStruct(shape, F32) for shape in outs],
         in_specs=in_specs or [VMEM] * len(operands),
         out_specs=out_specs or [VMEM] * len(outs),
         scratch_shapes=scratch,
+        input_output_aliases=aliases or {},
         compiler_params=pltpu.CompilerParams(vmem_limit_bytes=vmem),
     )(*operands)
 
@@ -468,10 +548,18 @@
         storage.reshape(64, 128),
         layer.reshape(64, 128),
         in_specs=[HBM] * 4,
+        out_specs=[HBM, HBM],
         vmem=None,
-        scratch=[pltpu.VMEM((27, 64, 128), F32), pltpu.VMEM((64, 128), jnp.int32), pltpu.SemaphoreType.DMA((4,))],
+        scratch=[
+            pltpu.VMEM(block, F32),
+            pltpu.VMEM(side, F32),
+            pltpu.VMEM((27, 64, 128), F32),
+            pltpu.VMEM((64, 128), jnp.int32),
+            pltpu.SemaphoreType.DMA((6,)),
+        ],
     )
     one, other = exchange("gz", edge, edge)
+    (core,) = call(load_kernel, (block,), core)
     rows = (ROWS_Y + 32, 128)
     beside_z, to_one, to_other = call(y_kernel, (side, rows, rows), core, one, other)
     one, other = exchange("gy", to_one, to_other)
@@ -494,20 +582,32 @@
             (4, planes(5), 16, 256),
         ]
 
-    parts = pltpu.VMEM((3, 2, 14, 16, 256), F32)
     sums = (3, 2, 3, 2, 8, 256)
+    whole = (27, 8, 8, 128)
+    half = pltpu.VMEM((27, 4, 8, 128), F32)
+    held = (4, 2, 16, 256)
+    outs = arrays(lambda first: 14 - 2 * first) + [sums, (3, 2, 8, 16, 256), held, held, whole]
     inner = call(
-        inner_kernel, arrays(lambda first: 14 - 2 * first) + [sums], core, beside_z, beside_y, corner, scratch=[parts]
+        inner_kernel,
+        outs,
+        core,
+        beside_z,
+        beside_y,
+        corner,
+        out_specs=[VMEM] * 15 + [HBM],
+        scratch=[half, pltpu.SemaphoreType.DMA],
     )
     smoothed, coarse = call(
         outer_kernel,
-        ((27, 8, 8, 128), (16, 27)),
+        (whole, (16, 27)),
         one,
         other,
         *inner,
+        in_specs=[VMEM] * 17 + [HBM],
         out_specs=[HBM, VMEM],
         scratch=[pltpu.VMEM(shape, F32) for shape in arrays(lambda first: 14)]
-        + [parts, pltpu.VMEM(sums, F32), pltpu.VMEM((27, 8, 8, 128), F32), pltpu.SemaphoreType.DMA],
+        + [pltpu.VMEM((3, 2, 14, 16, 256), F32), pltpu.VMEM(sums, F32), half, pltpu.SemaphoreType.DMA((2,))],
+        aliases={17: 0},
     )
     return smoothed, coarse.T.reshape(27, 1, 1, 16)
 

time: 42.8 us -> 41.3 us (0.965)
  waiting for transfers between devices: 7.88 us -> 5.86 us
  Pallas kernels: 7.27 us -> 7.86 us
    ppermute x3, waiting for transfers between devices: 6.36 us -> 5.33 us  [exchange(): from_other = lax.ppermute(to_other, axis, other)]
    ppermute x3, waiting for transfers between devices: 1.52 us -> 0.54 us  [exchange(): return (lax.ppermute(to_one, axis, one), from_other)]
    pallas_call x5 -> x6, Pallas kernels: 7.27 us -> 7.86 us  [call(): pl.pallas_call(kernel, out_shape=[jax.ShapeDtypeStruct(shape, F32) for sh...]
  transfers between devices with their start and end apart: 6 -> 6, of which waited for: 4 -> 4; matrix products, arithmetic and copies ran while one was open for 0% -> 0% of each run, Pallas kernels for 4% -> 7%
where the time goes in v3:
time: 41.3 us; the launch traced here: 41 us
  starting transfers between devices  25.6 us (62%)
  Pallas kernels  7.86 us (19%)
  waiting for transfers between devices  5.86 us (14%)
  local copies, waits for them, and re-layouts  0.96 us (2%)
  between operations  0.73 us (2%)
    ppermute x3, starting transfers between devices, exchange(): return (lax.ppermute(to_one, axis, one), from_other)  18.7 us
    pallas_call x6, Pallas kernels, call(): pl.pallas_call(kernel, out_shape=[jax.ShapeDtypeStruct(shape, F32) for sh...  7.86 us
    ppermute x3, starting transfers between devices, exchange(): from_other = lax.ppermute(to_other, axis, other)  6.94 us
    ppermute x3, waiting for transfers between devices, exchange(): from_other = lax.ppermute(to_other, axis, other)  5.33 us
    unnamed x2, local copies, waits for them, and re-layouts  0.96 us
  transfers between devices with their start and end apart: 6, of which 4 were waited for; matrix products, arithmetic and copies ran while one was open for 0% of the time, Pallas kernels for 7%

profile of v3, /device:TPU:18, one launch (start us, length us, event | category | flops | bytes accessed | tf_op | source)
XLA Modules:
  0.0 41.0 jit_solution(15921647345742595903)
XLA Ops:
  0.6 2.1 %shard_map.59 = (f32[9,64,128]{2,1,0:T(8,128)}, f32[9,8,128]{2,1,0:T(8,128)}) custom-call(f32[27,64,128]{2,1,0:T(8,128)} %bitcast.7, f32[3,64,128]{2,1,0:T(8,128)} %bitcast.8, f32[64,128]{1,0:T(8,128)} %bitcast.9, s32[64,128]{1,0:T(8,128)} %bitcast.10), custom_call_target="tpu_custom_call" | custom-call | tf_op jit(solution)/shard_map/pallas_call | solution.py:521
  2.8 0.7 %collective-permute-start.1 = (f32[9,8,128]{2,1,0:T(8,128)}, f32[9,8,128]{2,1,0:T(8,128)S(1)}, u32[]{:S(2)}, u32[]{:S(2)}) collective-permute-start(f32[9,8,128]{2,1,0:T(8,128)} %get-tuple-element.30), channel_id=1, source_target_pairs={{1,2},{2,1},{3,4},{4,3},{5,6},{6,5},{7,8},{8,7},{9,10},{10,9},{11,... | collective-permute-start | bytes 110600 | tf_op jit(solution)/shard_map/ppermute | solution.py:536
  3.4 6.5 %collective-permute-start = (f32[9,8,128]{2,1,0:T(8,128)}, f32[9,8,128]{2,1,0:T(8,128)S(1)}, u32[]{:S(2)}, u32[]{:S(2)}) collective-permute-start(f32[9,8,128]{2,1,0:T(8,128)} %get-tuple-element.30), channel_id=1, source_target_pairs={{0,1},{1,0},{2,3},{3,2},{4,5},{5,4},{6,7},{7,6},{8,9},{9,8},{10,11... | collective-permute-start | bytes 110600 | tf_op jit(solution)/shard_map/ppermute | solution.py:537
  10.0 0.0 copy-start
  10.0 1.0 %copy-done = f32[9,64,128]{2,1,0:T(8,128)S(1)} copy-done((f32[9,64,128]{2,1,0:T(8,128)S(1)}, f32[9,64,128]{2,1,0:T(8,128)}, u32[]{:S(2)}) %copy-start) | copy-done | bytes 294936
  11.0 0.0 collective-permute-done.1.from_other
  11.0 0.1 collective-permute-done.from_one
  11.0 0.1 shard_map.61
  11.1 2.4 %collective-permute-start.2 = (f32[224,128]{1,0:T(8,128)S(1)}, f32[224,128]{1,0:T(8,128)S(1)}, u32[]{:S(2)}, u32[]{:S(2)}) collective-permute-start(f32[224,128]{1,0:T(8,128)S(1)} %get-tuple-element.32), channel_id=1, source_target_pairs={{0,16},{16,0},{32,48},{48,32},{64,80},{80,64},{96,112},{112,96},{1... | collective-permute-start | bytes 344072 | tf_op jit(solution)/shard_map/ppermute | solution.py:537
  13.6 4.4 %collective-permute-start.3 = (f32[224,128]{1,0:T(8,128)S(1)}, f32[224,128]{1,0:T(8,128)S(1)}, u32[]{:S(2)}, u32[]{:S(2)}) collective-permute-start(f32[224,128]{1,0:T(8,128)S(1)} %get-tuple-element.33), channel_id=1, source_target_pairs={{16,32},{32,16},{48,64},{64,48},{80,96},{96,80},{17,33},{33,17},{4... | collective-permute-start | bytes 344072 | tf_op jit(solution)/shard_map/ppermute | solution.py:536
  17.9 0.5 %collective-permute-done.2.from_one = f32[224,128]{1,0:T(8,128)S(1)} collective-permute-done((f32[224,128]{1,0:T(8,128)S(1)}, f32[224,128]{1,0:T(8,128)S(1)}, u32[]{:S(2)}, u32[]{:S(2)}) %collective-permute-start.2) | collective-permute-done | bytes 114720 | tf_op jit(solution)/shard_map/ppermute | solution.py:537
  18.4 2.9 %collective-permute-done.3.from_other = f32[224,128]{1,0:T(8,128)S(1)} collective-permute-done((f32[224,128]{1,0:T(8,128)S(1)}, f32[224,128]{1,0:T(8,128)S(1)}, u32[]{:S(2)}, u32[]{:S(2)}) %collective-permute-start.3) | collective-permute-done | bytes 114720 | tf_op jit(solution)/shard_map/ppermute | solution.py:536
  21.3 0.2 shard_map.62
  21.5 9.7 %collective-permute-start.4 = (f32[336,128]{1,0:T(8,128)S(1)}, f32[336,128]{1,0:T(8,128)S(1)}, u32[]{:S(2)}, u32[]{:S(2)}) collective-permute-start(f32[336,128]{1,0:T(8,128)S(1)} %get-tuple-element.34), channel_id=1, source_target_pairs={{0,128},{128,0},{256,384},{384,256},{512,640},{640,512},{768,896},... | collective-permute-start | bytes 516104 | tf_op jit(solution)/shard_map/ppermute | solution.py:537
  31.2 1.9 %collective-permute-start.5 = (f32[336,128]{1,0:T(8,128)S(1)}, f32[336,128]{1,0:T(8,128)S(1)}, u32[]{:S(2)}, u32[]{:S(2)}) collective-permute-start(f32[336,128]{1,0:T(8,128)S(1)} %get-tuple-element.35), channel_id=1, source_target_pairs={{128,256},{256,128},{384,512},{512,384},{640,768},{768,640},{129,2... | collective-permute-start | bytes 516104 | tf_op jit(solution)/shard_map/ppermute | solution.py:536
  33.1 2.9 %shard_map.63 = (f32[9,8,16,256]{3,2,1,0:T(8,128)S(1)}, f32[8,16,256]{2,1,0:T(8,128)S(1)}, f32[8,16,256]{2,1,0:T(8,128)S(1)}, f32[8,16,256]{2,1,0:T(8,128)S(1)},...) custom-call(f32[9,64,128]{2,1,0:T(8,128)S(1)} %shard_map.60.core, ...), custom_call_target="tpu_custom_call" | custom-call | tf_op jit(solution)/shard_map/pallas_call | solution.py:521
  36.0 0.0 collective-permute-done.4.from_one
  36.0 2.4 %collective-permute-done.5.from_other = f32[336,128]{1,0:T(8,128)S(1)} collective-permute-done((f32[336,128]{1,0:T(8,128)S(1)}, f32[336,128]{1,0:T(8,128)S(1)}, u32[]{:S(2)}, u32[]{:S(2)}) %collective-permute-start.5) | collective-permute-done | bytes 172064 | tf_op jit(solution)/shard_map/ppermute | solution.py:536
  38.5 2.6 %shard_map.64 = (f32[27,8,8,128]{3,2,1,0:T(8,128)}, f32[16,27]{1,0:T(8,128)}) custom-call(f32[336,128]{1,0:T(8,128)S(1)} %collective-permute-done.4.from_one, f32[336,128]{1,0:T(8,128)S(1)} %collective-permute-done.5.from_other, f32[9,8,16,256]{3,2,1,0:T(8,128)S(1)} %get-tuple-element.38.refs_0_, ...), custom_call_target="tpu_custom_call", output_to_operand_aliasing={{0}: (17, {})} | custom-call | tf_op jit(solution)/shard_map/pallas_call | solution.py:521
  (1 shorter events, 0.0 us)
Async XLA Ops:
  2.8 8.2 %collective-permute-start.1 = (f32[9,8,128]{2,1,0:T(8,128)}, f32[9,8,128]{2,1,0:T(8,128)S(1)}, u32[]{:S(2)}, u32[]{:S(2)}) collective-permute-start(f32[9,8,128]{2,1,0:T(8,128)} %get-tuple-element.30), channel_id=1, source_target_pairs={{1,2},{2,1},{3,4},{4,3},{5,6},{6,5},{7,8},{8,7},{9,10},{10,9},{11,... | collective-permute-start | bytes 110600 | tf_op jit(solution)/shard_map/ppermute | solution.py:536
  3.4 7.6 %collective-permute-start = (f32[9,8,128]{2,1,0:T(8,128)}, f32[9,8,128]{2,1,0:T(8,128)S(1)}, u32[]{:S(2)}, u32[]{:S(2)}) collective-permute-start(f32[9,8,128]{2,1,0:T(8,128)} %get-tuple-element.30), channel_id=1, source_target_pairs={{0,1},{1,0},{2,3},{3,2},{4,5},{5,4},{6,7},{7,6},{8,9},{9,8},{10,11... | collective-permute-start | bytes 110600 | tf_op jit(solution)/shard_map/ppermute | solution.py:537
  10.0 1.0 %copy-start = (f32[9,64,128]{2,1,0:T(8,128)S(1)}, f32[9,64,128]{2,1,0:T(8,128)}, u32[]{:S(2)}) copy-start(f32[9,64,128]{2,1,0:T(8,128)} %get-tuple-element.29.core_hbm) | copy-start | bytes 884740
  11.1 7.3 %collective-permute-start.2 = (f32[224,128]{1,0:T(8,128)S(1)}, f32[224,128]{1,0:T(8,128)S(1)}, u32[]{:S(2)}, u32[]{:S(2)}) collective-permute-start(f32[224,128]{1,0:T(8,128)S(1)} %get-tuple-element.32), channel_id=1, source_target_pairs={{0,16},{16,0},{32,48},{48,32},{64,80},{80,64},{96,112},{112,96},{1... | collective-permute-start | bytes 344072 | tf_op jit(solution)/shard_map/ppermute | solution.py:537
  13.6 7.7 %collective-permute-start.3 = (f32[224,128]{1,0:T(8,128)S(1)}, f32[224,128]{1,0:T(8,128)S(1)}, u32[]{:S(2)}, u32[]{:S(2)}) collective-permute-start(f32[224,128]{1,0:T(8,128)S(1)} %get-tuple-element.33), channel_id=1, source_target_pairs={{16,32},{32,16},{48,64},{64,48},{80,96},{96,80},{17,33},{33,17},{4... | collective-permute-start | bytes 344072 | tf_op jit(solution)/shard_map/ppermute | solution.py:536
  21.5 14.6 %collective-permute-start.4 = (f32[336,128]{1,0:T(8,128)S(1)}, f32[336,128]{1,0:T(8,128)S(1)}, u32[]{:S(2)}, u32[]{:S(2)}) collective-permute-start(f32[336,128]{1,0:T(8,128)S(1)} %get-tuple-element.34), channel_id=1, source_target_pairs={{0,128},{128,0},{256,384},{384,256},{512,640},{640,512},{768,896},... | collective-permute-start | bytes 516104 | tf_op jit(solution)/shard_map/ppermute | solution.py:537
  31.2 7.3 %collective-permute-start.5 = (f32[336,128]{1,0:T(8,128)S(1)}, f32[336,128]{1,0:T(8,128)S(1)}, u32[]{:S(2)}, u32[]{:S(2)}) collective-permute-start(f32[336,128]{1,0:T(8,128)S(1)} %get-tuple-element.35), channel_id=1, source_target_pairs={{128,256},{256,128},{384,512},{512,384},{640,768},{768,640},{129,2... | collective-permute-start | bytes 516104 | tf_op jit(solution)/shard_map/ppermute | solution.py:536

commit v4 on v3

--- a/solution.py
+++ b/solution.py
@@ -13,6 +13,12 @@
 FIELDS_Y = (ALL, ALL, (0, 1, 2, 3, PY, LAYER))
 ROWS_Y = 8 * sum(len(f) for f in FIELDS_Y)
 ROWS_X = 8 * sum(len(f) for f in FIELDS_X)
+FIELDS_XY = (0, 1, 2, 3, PX, PY, LAYER)
+ROWS_XY = (
+    [(0, row, f) for row in (7, 0) for f in ALL]
+    + [(0, row, f) for row in (6, 1) for f in FIELDS_XY]
+    + [(1, row, f) for row in (7, 0) for f in FIELDS_XY]
+)
 F32 = jnp.float32
 
 
@@ -25,18 +31,13 @@
 
 
 def pack_kernel(basis_hbm, perm_hbm, storage_hbm, layer_hbm, core_hbm, edge_hbm, core, edge, basis, layer, sems):
-    copies = [
-        pltpu.make_async_copy(source, target, sems.at[i])
-        for i, (source, target) in enumerate(
-            (
-                (basis_hbm, basis),
-                (layer_hbm, layer),
-                (perm_hbm, core.at[PX : PZ + 1]),
-                (storage_hbm, core.at[STORAGE]),
-            )
-        )
+    rest = [
+        pltpu.make_async_copy(layer_hbm, layer, sems.at[0]),
+        pltpu.make_async_copy(perm_hbm, core.at[PX : PZ + 1], sems.at[1]),
+        pltpu.make_async_copy(storage_hbm, core.at[STORAGE], sems.at[2]),
     ]
-    for copy in copies:
+    arriving = pltpu.make_async_copy(basis_hbm, basis, sems.at[3])
+    for copy in rest + [arriving]:
         copy.start()
     gx, gy = lax.axis_index("gx"), lax.axis_index("gy")
     nx, ny = lax.axis_size("gx"), lax.axis_size("gy")
@@ -45,12 +46,26 @@
     ry_own, ry_low, ry_high = gy % 3, (gy + 2) % 3, (gy + 1) % 3
     low_rows = sub < 4
     y_valid = jnp.where(low_rows, (gy > 0).astype(F32), (gy < ny - 1).astype(F32))
-    for copy in copies:
+
+    def moved(value, x):
+        return roll(jnp.where(lane < 4, value, roll(value, 16, 1)), 16 * x, 1)
+
+    for copy in rest:
         copy.wait()
     ids = layer[...].astype(F32)
     core[LAYER] = ids
+    kept = [pltpu.make_async_copy(core.at[4:9], core_hbm.at[4:9], sems.at[4])]
+    kept[0].start()
     residue = ids - 3.0 * jnp.floor((ids + 0.5) * (1.0 / 3.0))
-
+    strip = lane // 16
+    for f in range(4, FIELDS):
+        packed = jnp.zeros((8, 128), F32)
+        for x in range(8):
+            packed = jnp.where(strip == x, moved(core[f, 8 * x : 8 * x + 8], x), packed)
+        edge[f] = packed
+
+    packed = [jnp.zeros((8, 128), F32) for _ in range(4)]
+    arriving.wait()
     for x in range(8):
         here = residue[8 * x : 8 * x + 8]
         is_zero, is_one = here < 0.5, here < 1.5
@@ -66,19 +81,16 @@
             other = jnp.where(low_rows, at(rx, ry_low), at(rx, ry_high)) * y_valid
             if ex:
                 own, other = own * x_valid, other * x_valid
-            core[2 * ex, 8 * x : 8 * x + 8] = own
-            core[2 * ex + 1, 8 * x : 8 * x + 8] = other
-    keep = [pltpu.make_async_copy(core, core_hbm, sems.at[4]), pltpu.make_async_copy(edge, edge_hbm, sems.at[5])]
-    keep[0].start()
-    for f in ALL:
-        packed = jnp.zeros((8, 128), F32)
-        for x in range(8):
-            value = core[f, 8 * x : 8 * x + 8]
-            value = jnp.where(lane < 4, value, roll(value, 16, 1))
-            packed = jnp.where(lane // 16 == x, roll(value, 16 * x, 1), packed)
-        edge[f] = packed
-    keep[1].start()
-    for copy in keep:
+            for f, value in ((2 * ex, own), (2 * ex + 1, other)):
+                core[f, 8 * x : 8 * x + 8] = value
+                packed[f] = jnp.where(strip == x, moved(value, x), packed[f])
+    for f in range(4):
+        edge[f] = packed[f]
+    kept.append(pltpu.make_async_copy(edge, edge_hbm, sems.at[5]))
+    kept.append(pltpu.make_async_copy(core.at[0:4], core_hbm.at[0:4], sems.at[6]))
+    kept[1].start()
+    kept[2].start()
+    for copy in kept:
         copy.wait()
 
 
@@ -88,8 +100,8 @@
 
 def by_side(axis, one, other, body):
     even = lax.axis_index(axis) % 2 == 0
-    pl.when(even)(lambda: body(((one, 1), (other, 0))))
-    pl.when(jnp.logical_not(even))(lambda: body(((one, 0), (other, 1))))
+    pl.when(even)(lambda: body(((one, 0), (other, 1))))
+    pl.when(jnp.logical_not(even))(lambda: body(((one, 1), (other, 0))))
 
 
 def y_kernel(core, from_one, from_other, beside_z, to_one, to_other):
@@ -107,9 +119,9 @@
                 for f in fields:
                     out[at : at + 8] = core[f, pl.ds(y, 8, stride=8), :]
                     at += 8
-            for d in range(3):
+            for d, fields in enumerate(FIELDS_Y):
                 y = 7 - d if side else d
-                for f in ALL:
+                for f in fields:
                     out[at : at + 1] = beside_z[f, y : y + 1]
                     at += 1
 
@@ -117,7 +129,8 @@
 
 
 def x_kernel(core, beside_z, from_one, from_other, beside_y, corner, to_one, to_other):
-    sub, lane = iota((8, 128), 0), iota((8, 128), 1)
+    lane = iota((8, 128), 1)
+    zero = jnp.zeros((8, 128), F32)
     beside_y[...] = jnp.zeros(beside_y.shape, F32)
     corner[...] = jnp.zeros(corner.shape, F32)
 
@@ -130,9 +143,9 @@
                     into = f ^ 1 if f < 4 else f
                     beside_y[into, pl.ds(row, 8, stride=8), :] = source[at : at + 8]
                     at += 8
-            for d in range(3):
+            for d, fields in enumerate(FIELDS_Y):
                 row = d if side else 7 - d
-                for f in ALL:
+                for f in fields:
                     into = f ^ 1 if f < 4 else f
                     corner[into, row : row + 1] = source[at : at + 1]
                     at += 1
@@ -147,18 +160,24 @@
                 for f in fields:
                     out[at : at + 8] = core[f, 8 * x : 8 * x + 8]
                     at += 8
-            first, second = (7, 6) if side else (0, 1)
+            for d, row, f in ROWS_XY:
+                from_row = 8 * (7 - d if side else d) + row
+                out[at : at + 1] = beside_y[f, from_row : from_row + 1]
+                at += 1
+            out[at : at + 2] = jnp.zeros((2, 128), F32)
+            at += 2
+            strips = []
             for f in ALL:
-                out[at : at + 8] = jnp.where(
-                    (sub == 2) | (sub == 3),
-                    roll(beside_y[f, 8 * second : 8 * second + 8], 3, 0),
-                    beside_y[f, 8 * first : 8 * first + 8],
-                )
-                at += 8
-            for f in ALL:
-                out[at : at + 8] = jnp.where(
-                    (lane >= 48) & (lane < 80), roll(corner[f], -48 if side else 48, 1), beside_z[f]
-                )
+                value = jnp.where((lane >= 48) & (lane < 80), roll(corner[f], -48 if side else 48, 1), beside_z[f])
+                strips.append(roll(value, 80 * f - 48 * side, 1))
+            for v in range(6):
+                value = zero
+                for f in ALL:
+                    start, stop = max(5 * f, 8 * v), min(5 * f + 5, 8 * v + 8)
+                    if start < stop:
+                        inside = (lane >= 16 * (start - 8 * v)) & (lane < 16 * (stop - 8 * v))
+                        value = jnp.where(inside, strips[f], value)
+                out[at : at + 8] = value
                 at += 8
 
     by_side("gx", to_one, to_other, send)
@@ -427,7 +446,7 @@
     outer = refs[18:29]
     outer_parts, sums, smoothed, sem = refs[29:]
     ext = outer[0]
-    sub = iota((8, 128), 0)
+    lane = iota((8, 128), 1)
     zero = jnp.zeros((8, 128), F32)
 
     def receive(pairs):
@@ -442,23 +461,27 @@
                         at += 8
                     else:
                         ext[into, plane, 0:8, 0:128] = zero
+            planes = (11, 12, 13) if side else (2, 1, 0)
+            for f in ALL:
+                for plane in planes:
+                    ext[f, plane, 8:16, 0:128] = zero
+            for d, row, f in ROWS_XY:
+                into = f ^ 2 if f < 4 else f
+                ext[into, planes[d], 8 + row : 9 + row, 0:128] = source[at : at + 1]
+                at += 1
+            at += 2
             for f in ALL:
                 into = f ^ 2 if f < 4 else f
-                rows = source[at : at + 8]
-                across = source[at + 72 : at + 80]
-                at += 8
-                lateral = roll(across, -48 if side else 48, 1)
+                first, last = 5 * f // 8, (5 * f + 4) // 8
+                value = source[at + 8 * first : at + 8 * first + 8]
+                if last > first:
+                    value = jnp.where(lane >= 16 * (5 * f % 8), value, source[at + 8 * last : at + 8 * last + 8])
+                value = roll(value, 48 * (1 - side) - 80 * f, 1)
+                lateral = roll(value, -48 if side else 48, 1)
                 for d in range(3):
-                    plane = 11 + d if side else 2 - d
                     slot = d if side else 7 - d
-                    ext[into, plane, 0:8, 128:256] = unpacked(across, slot)
-                    if d == 0:
-                        ext[into, plane, 8:16, 0:128] = jnp.where((sub < 2) | (sub > 5), rows, 0.0)
-                    elif d == 1:
-                        ext[into, plane, 8:16, 0:128] = jnp.where((sub < 1) | (sub > 6), roll(rows, -3, 0), 0.0)
-                    else:
-                        ext[into, plane, 8:16, 0:128] = zero
-                    ext[into, plane, 8:16, 128:256] = unpacked(lateral, slot) if d < 2 else zero
+                    ext[into, planes[d], 0:8, 128:256] = unpacked(value, slot)
+                    ext[into, planes[d], 8:16, 128:256] = unpacked(lateral, slot) if d < 2 else zero
 
     by_side("gx", from_one, from_other, receive)
     block = Block(arrays, outer)
@@ -531,10 +554,9 @@
 
 def exchange(axis, to_one, to_other):
     count = lax.axis_size(axis)
-    one = [(i, i ^ 1) for i in range(count)]
-    other = [(i, ((i + 1) ^ 1) - 1) for i in range(1, count - 1)]
-    from_other = lax.ppermute(to_other, axis, other)
-    return lax.ppermute(to_one, axis, one), from_other
+    one = [(i, ((i + 1) ^ 1) - 1) for i in range(1, count - 1)]
+    other = [(i, i ^ 1) for i in range(count)]
+    return lax.ppermute(to_one, axis, one), lax.ppermute(to_other, axis, other)
 
 
 def per_device(basis, perm, storage, layer):
@@ -555,15 +577,15 @@
             pltpu.VMEM(side, F32),
             pltpu.VMEM((27, 64, 128), F32),
             pltpu.VMEM((64, 128), jnp.int32),
-            pltpu.SemaphoreType.DMA((6,)),
+            pltpu.SemaphoreType.DMA((7,)),
         ],
     )
-    one, other = exchange("gz", edge, edge)
+    other, one = exchange("gz", edge, edge)
     (core,) = call(load_kernel, (block,), core)
-    rows = (ROWS_Y + 32, 128)
+    rows = (ROWS_Y + ROWS_Y // 8, 128)
     beside_z, to_one, to_other = call(y_kernel, (side, rows, rows), core, one, other)
     one, other = exchange("gy", to_one, to_other)
-    rows = (ROWS_X + 144, 128)
+    rows = (ROWS_X + 96, 128)
     beside_y, corner, to_one, to_other = call(x_kernel, (block, side, rows, rows), core, beside_z, one, other)
     one, other = exchange("gx", to_one, to_other)
 

time: 41.3 us -> 38.7 us (0.937)
  the two profiles are of different devices: /device:TPU:18 before, /device:TPU:438 now
where the time goes in v4:
time: 38.7 us; the launch traced here: 38.4 us
  starting transfers between devices  21.7 us (56%)
  Pallas kernels  7.82 us (20%)
  waiting for transfers between devices  7.24 us (19%)
  local copies, waits for them, and re-layouts  0.96 us (2%)
  between operations  0.73 us (2%)
    ppermute x3, starting transfers between devices, exchange(): lax.ppermute(to_one, axis, one)  11.3 us
    ppermute x3, starting transfers between devices, exchange(): lax.ppermute(to_other, axis, other)  10.3 us
    pallas_call x6, Pallas kernels, call(): pl.pallas_call(kernel, out_shape=[jax.ShapeDtypeStruct(shape, F32) for sh...  7.82 us
    ppermute x3, waiting for transfers between devices, exchange(): lax.ppermute(to_other, axis, other)  5.36 us
    ppermute x3, waiting for transfers between devices, exchange(): lax.ppermute(to_one, axis, one)  1.87 us
    unnamed x2, local copies, waits for them, and re-layouts  0.96 us
  transfers between devices with their start and end apart: 6, of which 4 were waited for; matrix products, arithmetic and copies ran while one was open for 0% of the time, Pallas kernels for 8%

profile of v4, /device:TPU:438, one launch (start us, length us, event | category | flops | bytes accessed | tf_op | source)
XLA Modules:
  0.0 38.4 jit_solution(12802381619883346473)
XLA Ops:
  0.6 2.2 %shard_map.59 = (f32[9,64,128]{2,1,0:T(8,128)}, f32[9,8,128]{2,1,0:T(8,128)}) custom-call(f32[27,64,128]{2,1,0:T(8,128)} %bitcast.7, f32[3,64,128]{2,1,0:T(8,128)} %bitcast.8, f32[64,128]{1,0:T(8,128)} %bitcast.9, s32[64,128]{1,0:T(8,128)} %bitcast.10), custom_call_target="tpu_custom_call" | custom-call | tf_op jit(solution)/shard_map/pallas_call | solution.py:544
  2.8 1.9 %collective-permute-start.1 = (f32[9,8,128]{2,1,0:T(8,128)}, f32[9,8,128]{2,1,0:T(8,128)S(1)}, u32[]{:S(2)}, u32[]{:S(2)}) collective-permute-start(f32[9,8,128]{2,1,0:T(8,128)} %get-tuple-element.30), channel_id=1, source_target_pairs={{1,2},{2,1},{3,4},{4,3},{5,6},{6,5},{7,8},{8,7},{9,10},{10,9},{11,... | collective-permute-start | bytes 110600 | tf_op jit(solution)/shard_map/ppermute | solution.py:559
  4.7 6.5 %collective-permute-start = (f32[9,8,128]{2,1,0:T(8,128)}, f32[9,8,128]{2,1,0:T(8,128)S(1)}, u32[]{:S(2)}, u32[]{:S(2)}) collective-permute-start(f32[9,8,128]{2,1,0:T(8,128)} %get-tuple-element.30), channel_id=1, source_target_pairs={{0,1},{1,0},{2,3},{3,2},{4,5},{5,4},{6,7},{7,6},{8,9},{9,8},{10,11... | collective-permute-start | bytes 110600 | tf_op jit(solution)/shard_map/ppermute | solution.py:559
  11.3 0.0 copy-start
  11.3 1.0 %copy-done = f32[9,64,128]{2,1,0:T(8,128)S(1)} copy-done((f32[9,64,128]{2,1,0:T(8,128)S(1)}, f32[9,64,128]{2,1,0:T(8,128)}, u32[]{:S(2)}) %copy-start) | copy-done | bytes 294936
  12.2 0.0 collective-permute-done.1.from_other
  12.3 0.1 collective-permute-done.from_one
  12.3 0.1 shard_map.61
  12.4 4.6 %collective-permute-start.2 = (f32[216,128]{1,0:T(8,128)S(1)}, f32[216,128]{1,0:T(8,128)S(1)}, u32[]{:S(2)}, u32[]{:S(2)}) collective-permute-start(f32[216,128]{1,0:T(8,128)S(1)} %get-tuple-element.32), channel_id=1, source_target_pairs={{16,32},{32,16},{48,64},{64,48},{80,96},{96,80},{17,33},{33,17},{4... | collective-permute-start | bytes 331784 | tf_op jit(solution)/shard_map/ppermute | solution.py:559
  17.0 1.9 %collective-permute-start.3 = (f32[216,128]{1,0:T(8,128)S(1)}, f32[216,128]{1,0:T(8,128)S(1)}, u32[]{:S(2)}, u32[]{:S(2)}) collective-permute-start(f32[216,128]{1,0:T(8,128)S(1)} %get-tuple-element.33), channel_id=1, source_target_pairs={{0,16},{16,0},{32,48},{48,32},{64,80},{80,64},{96,112},{112,96},{1... | collective-permute-start | bytes 331784 | tf_op jit(solution)/shard_map/ppermute | solution.py:559
  18.9 1.9 %collective-permute-done.2.from_one = f32[216,128]{1,0:T(8,128)S(1)} collective-permute-done((f32[216,128]{1,0:T(8,128)S(1)}, f32[216,128]{1,0:T(8,128)S(1)}, u32[]{:S(2)}, u32[]{:S(2)}) %collective-permute-start.2) | collective-permute-done | bytes 110624 | tf_op jit(solution)/shard_map/ppermute | solution.py:559
  20.8 3.1 %collective-permute-done.3.from_other = f32[216,128]{1,0:T(8,128)S(1)} collective-permute-done((f32[216,128]{1,0:T(8,128)S(1)}, f32[216,128]{1,0:T(8,128)S(1)}, u32[]{:S(2)}, u32[]{:S(2)}) %collective-permute-start.3) | collective-permute-done | bytes 110624 | tf_op jit(solution)/shard_map/ppermute | solution.py:559
  23.9 0.3 shard_map.62
  24.2 4.8 %collective-permute-start.4 = (f32[288,128]{1,0:T(8,128)S(1)}, f32[288,128]{1,0:T(8,128)S(1)}, u32[]{:S(2)}, u32[]{:S(2)}) collective-permute-start(f32[288,128]{1,0:T(8,128)S(1)} %get-tuple-element.34), channel_id=1, source_target_pairs={{128,256},{256,128},{384,512},{512,384},{640,768},{768,640},{129,2... | collective-permute-start | bytes 442376 | tf_op jit(solution)/shard_map/ppermute | solution.py:559
  29.0 1.9 %collective-permute-start.5 = (f32[288,128]{1,0:T(8,128)S(1)}, f32[288,128]{1,0:T(8,128)S(1)}, u32[]{:S(2)}, u32[]{:S(2)}) collective-permute-start(f32[288,128]{1,0:T(8,128)S(1)} %get-tuple-element.35), channel_id=1, source_target_pairs={{0,128},{128,0},{256,384},{384,256},{512,640},{640,512},{768,896},... | collective-permute-start | bytes 442376 | tf_op jit(solution)/shard_map/ppermute | solution.py:559
  30.9 2.9 %shard_map.63 = (f32[9,8,16,256]{3,2,1,0:T(8,128)S(1)}, f32[8,16,256]{2,1,0:T(8,128)S(1)}, f32[8,16,256]{2,1,0:T(8,128)S(1)}, f32[8,16,256]{2,1,0:T(8,128)S(1)},...) custom-call(f32[9,64,128]{2,1,0:T(8,128)S(1)} %shard_map.60.core, ...), custom_call_target="tpu_custom_call" | custom-call | tf_op jit(solution)/shard_map/pallas_call | solution.py:544
  33.8 0.0 collective-permute-done.4.from_one
  33.8 2.2 %collective-permute-done.5.from_other = f32[288,128]{1,0:T(8,128)S(1)} collective-permute-done((f32[288,128]{1,0:T(8,128)S(1)}, f32[288,128]{1,0:T(8,128)S(1)}, u32[]{:S(2)}, u32[]{:S(2)}) %collective-permute-start.5) | collective-permute-done | bytes 147488 | tf_op jit(solution)/shard_map/ppermute | solution.py:559
  36.0 2.4 %shard_map.64 = (f32[27,8,8,128]{3,2,1,0:T(8,128)}, f32[16,27]{1,0:T(8,128)}) custom-call(f32[288,128]{1,0:T(8,128)S(1)} %collective-permute-done.4.from_one, f32[288,128]{1,0:T(8,128)S(1)} %collective-permute-done.5.from_other, f32[9,8,16,256]{3,2,1,0:T(8,128)S(1)} %get-tuple-element.38.refs_0_, ...), custom_call_target="tpu_custom_call", output_to_operand_aliasing={{0}: (17, {})} | custom-call | tf_op jit(solution)/shard_map/pallas_call | solution.py:544
  (1 shorter events, 0.0 us)
Async XLA Ops:
  2.8 9.4 %collective-permute-start.1 = (f32[9,8,128]{2,1,0:T(8,128)}, f32[9,8,128]{2,1,0:T(8,128)S(1)}, u32[]{:S(2)}, u32[]{:S(2)}) collective-permute-start(f32[9,8,128]{2,1,0:T(8,128)} %get-tuple-element.30), channel_id=1, source_target_pairs={{1,2},{2,1},{3,4},{4,3},{5,6},{6,5},{7,8},{8,7},{9,10},{10,9},{11,... | collective-permute-start | bytes 110600 | tf_op jit(solution)/shard_map/ppermute | solution.py:559
  4.7 7.6 %collective-permute-start = (f32[9,8,128]{2,1,0:T(8,128)}, f32[9,8,128]{2,1,0:T(8,128)S(1)}, u32[]{:S(2)}, u32[]{:S(2)}) collective-permute-start(f32[9,8,128]{2,1,0:T(8,128)} %get-tuple-element.30), channel_id=1, source_target_pairs={{0,1},{1,0},{2,3},{3,2},{4,5},{5,4},{6,7},{7,6},{8,9},{9,8},{10,11... | collective-permute-start | bytes 110600 | tf_op jit(solution)/shard_map/ppermute | solution.py:559
  11.3 1.0 %copy-start = (f32[9,64,128]{2,1,0:T(8,128)S(1)}, f32[9,64,128]{2,1,0:T(8,128)}, u32[]{:S(2)}) copy-start(f32[9,64,128]{2,1,0:T(8,128)} %get-tuple-element.29.core_hbm) | copy-start | bytes 884740
  12.4 8.4 %collective-permute-start.2 = (f32[216,128]{1,0:T(8,128)S(1)}, f32[216,128]{1,0:T(8,128)S(1)}, u32[]{:S(2)}, u32[]{:S(2)}) collective-permute-start(f32[216,128]{1,0:T(8,128)S(1)} %get-tuple-element.32), channel_id=1, source_target_pairs={{16,32},{32,16},{48,64},{64,48},{80,96},{96,80},{17,33},{33,17},{4... | collective-permute-start | bytes 331784 | tf_op jit(solution)/shard_map/ppermute | solution.py:559
  17.0 6.9 %collective-permute-start.3 = (f32[216,128]{1,0:T(8,128)S(1)}, f32[216,128]{1,0:T(8,128)S(1)}, u32[]{:S(2)}, u32[]{:S(2)}) collective-permute-start(f32[216,128]{1,0:T(8,128)S(1)} %get-tuple-element.33), channel_id=1, source_target_pairs={{0,16},{16,0},{32,48},{48,32},{64,80},{80,64},{96,112},{112,96},{1... | collective-permute-start | bytes 331784 | tf_op jit(solution)/shard_map/ppermute | solution.py:559
  24.2 9.7 %collective-permute-start.4 = (f32[288,128]{1,0:T(8,128)S(1)}, f32[288,128]{1,0:T(8,128)S(1)}, u32[]{:S(2)}, u32[]{:S(2)}) collective-permute-start(f32[288,128]{1,0:T(8,128)S(1)} %get-tuple-element.34), channel_id=1, source_target_pairs={{128,256},{256,128},{384,512},{512,384},{640,768},{768,640},{129,2... | collective-permute-start | bytes 442376 | tf_op jit(solution)/shard_map/ppermute | solution.py:559
  29.0 7.0 %collective-permute-start.5 = (f32[288,128]{1,0:T(8,128)S(1)}, f32[288,128]{1,0:T(8,128)S(1)}, u32[]{:S(2)}, u32[]{:S(2)}) collective-permute-start(f32[288,128]{1,0:T(8,128)S(1)} %get-tuple-element.35), channel_id=1, source_target_pairs={{0,128},{128,0},{256,384},{384,256},{512,640},{640,512},{768,896},... | collective-permute-start | bytes 442376 | tf_op jit(solution)/shard_map/ppermute | solution.py:559

commit v5 on v4

--- a/solution.py
+++ b/solution.py
@@ -1,3 +1,5 @@
+import functools
+
 import jax
 import jax.numpy as jnp
 from jax import lax
@@ -314,52 +316,54 @@
     def coarse_parts(self, planes, parts):
         row = self.row
         octet = self.octets()
-        in_block = row < 8
+        above, below = (row < 7) | (row == 15), (row > 0) & (row < 9)
         for p in planes:
             inside = 3 <= p <= 10
-            tall = 16 if inside else 8
-            ids = self.cells(LAYER, p, tall)
-            lifted = ids > octet[0:tall]
-            keep = in_block[0:tall]
+            ids = self.cells(LAYER, p)
+            up, own, down = (jnp.zeros((8, 256), F32) for _ in range(3))
             given = []
             if p >= 4:
-                given.append((self.side_x(self.face_x, p - 1, tall), self.cells(LAYER, p - 1, tall), keep))
+                given.append((self.side_x(self.face_x, p - 1, 8), self.side_x(self.near_x, p - 1, 8), self.cells(LAYER, p - 1, 8)))
             if p <= 9:
-                given.append((self.side_x(self.face_x, p, tall), self.cells(LAYER, p + 1, tall), keep))
-            total = [jnp.zeros((tall, 256), F32) for _ in range(3)]
+                given.append((self.side_x(self.face_x, p, 8), self.side_x(self.near_x, p, 8), self.cells(LAYER, p + 1, 8)))
             if inside:
-                face = read(self.face_y, p)
-                given.append((face, roll(ids, -1, 0), (row < 7) | (row == 15)))
-                given.append((roll(face, 1, 0), roll(ids, 1, 0), (row > 0) & (row < 9)))
-                face = read(self.face_z, p)
-                given.append((face, roll(ids, -1, 1), keep))
-                given.append((roll(face, 1, 1), roll(ids, 1, 1), keep))
-                own = read(self.rest, p)
-                if p >= 4:
-                    own = own + self.side_x(self.face_x, p - 1)
-                if p <= 9:
-                    own = own + self.side_x(self.face_x, p)
-                total[1] = jnp.where(keep, own, 0.0)
-            for face, beside, kept in given:
-                face = jnp.where(kept, face, 0.0)
-                step = beside - ids
-                total[0] = total[0] - jnp.where(step == 1.0, face, 0.0)
-                total[1] = total[1] - jnp.where(step == 0.0, face, 0.0)
-                total[2] = total[2] - jnp.where(step == -1.0, face, 0.0)
+                own = read(self.rest, p, None, 8)
+                for face, _, _ in given:
+                    own = own + face
+                face, near, top = read(self.face_z, p, None, 8), read(self.near_z, p, None, 8), ids[0:8]
+                given.append((face, near, roll(top, -1, 1)))
+                given.append((roll(face, 1, 1), roll(near, 1, 1), roll(top, 1, 1)))
+            for face, near, beside in given:
+                apart = face - near
+                higher = jnp.where(beside > ids[0:8], apart, 0.0)
+                up, own, down = up - higher, own - near, down - (apart - higher)
+            total = [up, own, down]
+            if inside:
+                up, own, down = (jnp.zeros((16, 256), F32) for _ in range(3))
+                face, near = read(self.face_y, p), read(self.near_y, p)
+                for shift, keep in ((0, above), (1, below)):
+                    apart, close = face - near, near
+                    beside = roll(ids, 1 if shift else -1, 0)
+                    if shift:
+                        apart, close = roll(apart, 1, 0), roll(close, 1, 0)
+                    apart, close = jnp.where(keep, apart, 0.0), jnp.where(keep, close, 0.0)
+                    higher = jnp.where(beside > ids, apart, 0.0)
+                    up, own, down = up - higher, own - close, down - (apart - higher)
+                total = [jnp.concatenate([t + y[0:8], y[8:16]], axis=0) for t, y in zip(total, (up, own, down))]
+            tall = 16 if inside else 8
+            lifted = ids[0:tall] > octet[0:tall]
             for oz in range(3):
                 upper = jnp.where(lifted, total[oz], 0.0)
                 ref, at = parts.at(p)
                 ref[oz, 0, at, 0:tall] = total[oz] - upper
                 ref[oz, 1, at, 0:tall] = upper
 
-    def coarse_outer_faces(self, parts, outer_parts):
-        row, octet = self.row, self.octets()
-        for p, face in ((3, 2), (10, 10)):
-            face = jnp.where(row < 8, self.side_x(self.face_x, face), 0.0)
-            upper = jnp.where(self.cells(LAYER, p) > octet, face, 0.0)
-            ref, at = parts.at(p)
-            outer_parts[1, 0, p] = ref[1, 0, at] + (face - upper)
-            outer_parts[1, 1, p] = ref[1, 1, at] + upper
+    def coarse_outer_face(self, p, face, parts, outer_parts):
+        face = jnp.where(self.row < 8, self.side_x(self.face_x, face), 0.0)
+        upper = jnp.where(self.cells(LAYER, p) > self.octets(), face, 0.0)
+        ref, at = parts.at(p)
+        outer_parts[1, 0, p] = ref[1, 0, at] + (face - upper)
+        outer_parts[1, 1, p] = ref[1, 1, at] + upper
 
     def octets(self):
         octet = (jnp.where(self.column < 192, self.column, self.column - 256) + 256) // BLOCK - 32
@@ -371,6 +375,8 @@
                 for f in range(4):
                     groups = (planes,) if f < 2 else ([p for p in planes if p < 7], [p for p in planes if p >= 7])
                     for i, group in enumerate(groups):
+                        if not group:
+                            continue
                         top = bottom = None
                         for p in group:
                             part, spot = parts.at(p)
@@ -440,100 +446,110 @@
     copy.wait()
 
 
-def outer_kernel(from_one, from_other, *refs):
-    arrays, (inner_sums, inner_parts, held_once, held_twice, _) = refs[:11], refs[11:16]
-    smoothed_hbm, coarse = refs[16:18]
-    outer = refs[18:29]
-    outer_parts, sums, smoothed, sem = refs[29:]
-    ext = outer[0]
+def receive_planes(source, side, ext):
     lane = iota((8, 128), 1)
     zero = jnp.zeros((8, 128), F32)
-
-    def receive(pairs):
-        for source, side in pairs:
-            at = 0
-            for d in range(3):
-                plane = 11 + d if side else 2 - d
-                for f in ALL:
-                    into = f ^ 2 if f < 4 else f
-                    if f in FIELDS_X[d]:
-                        ext[into, plane, 0:8, 0:128] = source[at : at + 8]
-                        at += 8
-                    else:
-                        ext[into, plane, 0:8, 0:128] = zero
-            planes = (11, 12, 13) if side else (2, 1, 0)
-            for f in ALL:
-                for plane in planes:
-                    ext[f, plane, 8:16, 0:128] = zero
-            for d, row, f in ROWS_XY:
-                into = f ^ 2 if f < 4 else f
-                ext[into, planes[d], 8 + row : 9 + row, 0:128] = source[at : at + 1]
-                at += 1
-            at += 2
-            for f in ALL:
-                into = f ^ 2 if f < 4 else f
-                first, last = 5 * f // 8, (5 * f + 4) // 8
-                value = source[at + 8 * first : at + 8 * first + 8]
-                if last > first:
-                    value = jnp.where(lane >= 16 * (5 * f % 8), value, source[at + 8 * last : at + 8 * last + 8])
-                value = roll(value, 48 * (1 - side) - 80 * f, 1)
-                lateral = roll(value, -48 if side else 48, 1)
-                for d in range(3):
-                    slot = d if side else 7 - d
-                    ext[into, planes[d], 0:8, 128:256] = unpacked(value, slot)
-                    ext[into, planes[d], 8:16, 128:256] = unpacked(lateral, slot) if d < 2 else zero
-
-    by_side("gx", from_one, from_other, receive)
+    planes = (11, 12, 13) if side else (2, 1, 0)
+    at = 0
+    for d in range(3):
+        for f in ALL:
+            into = f ^ 2 if f < 4 else f
+            if f in FIELDS_X[d]:
+                ext[into, planes[d], 0:8, 0:128] = source[at : at + 8]
+                at += 8
+            else:
+                ext[into, planes[d], 0:8, 0:128] = zero
+            ext[into, planes[d], 8:16, 0:128] = zero
+    for d, row, f in ROWS_XY:
+        into = f ^ 2 if f < 4 else f
+        ext[into, planes[d], 8 + row : 9 + row, 0:128] = source[at : at + 1]
+        at += 1
+    at += 2
+    for f in ALL:
+        into = f ^ 2 if f < 4 else f
+        first, last = 5 * f // 8, (5 * f + 4) // 8
+        value = source[at + 8 * first : at + 8 * first + 8]
+        if last > first:
+            value = jnp.where(lane >= 16 * (5 * f % 8), value, source[at + 8 * last : at + 8 * last + 8])
+        value = roll(value, 48 * (1 - side) - 80 * f, 1)
+        lateral = roll(value, -48 if side else 48, 1)
+        for d in range(3):
+            slot = d if side else 7 - d
+            ext[into, planes[d], 0:8, 128:256] = unpacked(value, slot)
+            ext[into, planes[d], 8:16, 128:256] = unpacked(lateral, slot) if d < 2 else zero
+
+
+def outer_kernel(last, source, *refs):
+    arrays, (inner_sums, inner_parts, held_once, held_twice, _), refs = refs[:11], refs[11:16], refs[16:]
+    if last:
+        (first_sums, smoothed_hbm, coarse), refs = refs[:3], refs[3:]
+    else:
+        (smoothed_hbm, sums), refs = refs[:2], refs[2:]
+    outer, refs = refs[:11], refs[11:]
+    outer_parts, smoothed, sem = refs[:3]
+    if last:
+        sums = refs[3]
     block = Block(arrays, outer)
-    block.faces_x((0, 1, 2, 10, 11, 12))
-    block.faces((1, 2, 11, 12))
-    block.weights((1, 2, 3, 10, 11, 12))
-    steps = (
-        (held_once, block.ext, block.once, (1, 2, 11, 12), (3, 10)),
-        (held_twice, block.once, block.twice, (2, 3, 10, 11), (4, 9)),
-    )
-    for held, source, target, whole, begun in steps:
-        block.sweep(whole, source, target)
-        for i, p in enumerate(begun):
-            totals = block.beside_x(p, source, [held[f, i] for f in range(4)], low=i == 0, high=i == 1)
-            block.relax(p, source, target, totals)
-    store_slots(block, (0, 1, 6, 7), smoothed)
-    copies = [
-        pltpu.make_async_copy(smoothed.at[:, 0:2], smoothed_hbm.at[:, 0:2], sem.at[0]),
-        pltpu.make_async_copy(smoothed.at[:, 2:4], smoothed_hbm.at[:, 6:8], sem.at[1]),
-    ]
-    for copy in copies:
+    parts = Planes(inner_parts, outer_parts, 3)
+    even = lax.axis_index("gx") % 2 == 0
+    high = even if last else jnp.logical_not(even)
+    copy = pltpu.make_async_copy(smoothed, smoothed_hbm.at[:, pl.ds(jnp.where(high, 6, 0), 2)], sem)
+    sums[...] = jnp.zeros(sums.shape, F32)
+
+    def add(side):
+        def plane(d):
+            return 10 + d if side else 3 - d
+
+        def face(d):
+            return 9 + d if side else 3 - d
+
+        receive_planes(source, side, outer[0])
+        block.faces_x([face(d) for d in (1, 2, 3)])
+        block.faces([plane(1), plane(2)])
+        block.weights([plane(0), plane(1), plane(2)])
+        steps = (
+            (held_once, block.ext, block.once, (2, 1), 0),
+            (held_twice, block.once, block.twice, (1, 0), -1),
+        )
+        for held, values, target, whole, begun in steps:
+            block.sweep([plane(d) for d in whole], values, target)
+            p = plane(begun)
+            totals = [held[f, side] for f in range(4)]
+            totals = block.beside_x(p, values, totals, low=not side, high=bool(side))
+            block.relax(p, values, target, totals)
+        store_slots(block, (6, 7) if side else (0, 1), smoothed)
         copy.start()
-
-    parts = Planes(inner_parts, outer_parts, 3)
-    block.coarse_parts((2, 11), parts)
-    block.coarse_outer_faces(parts, outer_parts)
-    block.coarse_sums([2, 3, 4, 9, 10, 11], parts, sums, outer_parts)
-    spot = iota((16, 256), 1)
-    place = (jnp.where(spot < 192, spot, spot - 256) + 256) // BLOCK - 32
-    for oz in range(3):
-        total = jnp.zeros((16, 16), F32)
-        for lift in range(2):
-            rows = []
-            for oy in range(3):
-                for ox in range(3):
-                    ey = 0 if oy == 1 else 1
-                    value = sums[oz, lift, ox, ey] + inner_sums[oz, lift, ox, ey]
-                    if oy != 1:
-                        value = value[0:4] if oy == 0 else value[4:8]
-                    rows.append(jnp.sum(value, axis=0, keepdims=True))
-            rows.append(jnp.zeros((7, 256), F32))
-            chosen = (place + lift - (oz - 1) == iota((16, 256), 0)).astype(F32)
-            total = total + lax.dot_general(
-                chosen,
-                jnp.concatenate(rows, axis=0),
-                (((1,), (1,)), ((), ())),
-                precision=lax.Precision.HIGHEST,
-                preferred_element_type=F32,
-            )
-        coarse[:, 9 * oz : 9 * oz + 9] = total[:, 0:9] * (1.0 / (BLOCK * BLOCK))
-    for copy in copies:
-        copy.wait()
+        block.coarse_parts([plane(1)], parts)
+        block.coarse_outer_face(plane(0), face(1), parts, outer_parts)
+        block.coarse_sums(sorted(plane(d) for d in (-1, 0, 1)), parts, sums, outer_parts)
+
+    pl.when(high)(lambda: add(1))
+    pl.when(jnp.logical_not(high))(lambda: add(0))
+    if last:
+        spot = iota((16, 256), 1)
+        place = (jnp.where(spot < 192, spot, spot - 256) + 256) // BLOCK - 32
+        for oz in range(3):
+            total = jnp.zeros((16, 16), F32)
+            for lift in range(2):
+                rows = []
+                for oy in range(3):
+                    for ox in range(3):
+                        ey = 0 if oy == 1 else 1
+                        value = inner_sums[oz, lift, ox, ey] + first_sums[oz, lift, ox, ey] + sums[oz, lift, ox, ey]
+                        if oy != 1:
+                            value = value[0:4] if oy == 0 else value[4:8]
+                        rows.append(jnp.sum(value, axis=0, keepdims=True))
+                rows.append(jnp.zeros((7, 256), F32))
+                chosen = (place + lift - (oz - 1) == iota((16, 256), 0)).astype(F32)
+                total = total + lax.dot_general(
+                    chosen,
+                    jnp.concatenate(rows, axis=0),
+                    (((1,), (1,)), ((), ())),
+                    precision=lax.Precision.HIGHEST,
+                    preferred_element_type=F32,
+                )
+            coarse[:, 9 * oz : 9 * oz + 9] = total[:, 0:9] * (1.0 / (BLOCK * BLOCK))
+    copy.wait()
 
 
 VMEM = pl.BlockSpec(memory_space=pltpu.VMEM)
@@ -619,17 +635,29 @@
         out_specs=[VMEM] * 15 + [HBM],
         scratch=[half, pltpu.SemaphoreType.DMA],
     )
+    scratch = [pltpu.VMEM(shape, F32) for shape in arrays(lambda first: 14)]
+    scratch += [pltpu.VMEM((3, 2, 14, 16, 256), F32), pltpu.VMEM((27, 2, 8, 128), F32), pltpu.SemaphoreType.DMA]
+    smoothed, first_sums = call(
+        functools.partial(outer_kernel, False),
+        (whole, sums),
+        one,
+        *inner,
+        in_specs=[VMEM] * 16 + [HBM],
+        out_specs=[HBM, VMEM],
+        scratch=scratch,
+        aliases={16: 0},
+    )
     smoothed, coarse = call(
-        outer_kernel,
+        functools.partial(outer_kernel, True),
         (whole, (16, 27)),
-        one,
         other,
-        *inner,
-        in_specs=[VMEM] * 17 + [HBM],
+        *inner[:-1],
+        smoothed,
+        first_sums,
+        in_specs=[VMEM] * 16 + [HBM, VMEM],
         out_specs=[HBM, VMEM],
-        scratch=[pltpu.VMEM(shape, F32) for shape in arrays(lambda first: 14)]
-        + [pltpu.VMEM((3, 2, 14, 16, 256), F32), pltpu.VMEM(sums, F32), half, pltpu.SemaphoreType.DMA((2,))],
-        aliases={17: 0},
+        scratch=scratch + [pltpu.VMEM(sums, F32)],
+        aliases={16: 0},
     )
     return smoothed, coarse.T.reshape(27, 1, 1, 16)
 

time: 38.7 us -> 38.8 us (level)
  the two profiles are of different devices: /device:TPU:438 before, /device:TPU:422 now
where the time goes in v5:
time: 38.8 us; the launch traced here: 38.5 us
  starting transfers between devices  23.4 us (60%)
  Pallas kernels  8.36 us (22%)
  waiting for transfers between devices  5.06 us (13%)
  local copies, waits for them, and re-layouts  0.96 us (2%)
  between operations  0.75 us (2%)
    ppermute x3, starting transfers between devices, exchange(): lax.ppermute(to_other, axis, other)  14.6 us
    ppermute x3, starting transfers between devices, exchange(): lax.ppermute(to_one, axis, one)  8.77 us
    pallas_call x7, Pallas kernels, call(): pl.pallas_call(kernel, out_shape=[jax.ShapeDtypeStruct(shape, F32) for sh...  8.36 us
    ppermute x3, waiting for transfers between devices, exchange(): lax.ppermute(to_other, axis, other)  3.18 us
    ppermute x3, waiting for transfers between devices, exchange(): lax.ppermute(to_one, axis, one)  1.87 us
    unnamed x2, local copies, waits for them, and re-layouts  0.96 us
  transfers between devices with their start and end apart: 6, of which 3 were waited for; matrix products, arithmetic and copies ran while one was open for 0% of the time, Pallas kernels for 11%

profile of v5, /device:TPU:422, one launch (start us, length us, event | category | flops | bytes accessed | tf_op | source)
XLA Modules:
  0.0 38.5 jit_solution(708697947264913017)
XLA Ops:
  0.6 2.2 %shard_map.59 = (f32[9,64,128]{2,1,0:T(8,128)}, f32[9,8,128]{2,1,0:T(8,128)}) custom-call(f32[27,64,128]{2,1,0:T(8,128)} %bitcast.7, f32[3,64,128]{2,1,0:T(8,128)} %bitcast.8, f32[64,128]{1,0:T(8,128)} %bitcast.9, s32[64,128]{1,0:T(8,128)} %bitcast.10), custom_call_target="tpu_custom_call" | custom-call | tf_op jit(solution)/shard_map/pallas_call | solution.py:560
  2.8 1.9 %collective-permute-start.1 = (f32[9,8,128]{2,1,0:T(8,128)}, f32[9,8,128]{2,1,0:T(8,128)S(1)}, u32[]{:S(2)}, u32[]{:S(2)}) collective-permute-start(f32[9,8,128]{2,1,0:T(8,128)} %get-tuple-element.32), channel_id=1, source_target_pairs={{1,2},{2,1},{3,4},{4,3},{5,6},{6,5},{7,8},{8,7},{9,10},{10,9},{11,... | collective-permute-start | bytes 110600 | tf_op jit(solution)/shard_map/ppermute | solution.py:575
  4.7 6.5 %collective-permute-start = (f32[9,8,128]{2,1,0:T(8,128)}, f32[9,8,128]{2,1,0:T(8,128)S(1)}, u32[]{:S(2)}, u32[]{:S(2)}) collective-permute-start(f32[9,8,128]{2,1,0:T(8,128)} %get-tuple-element.32), channel_id=1, source_target_pairs={{0,1},{1,0},{2,3},{3,2},{4,5},{5,4},{6,7},{7,6},{8,9},{9,8},{10,11... | collective-permute-start | bytes 110600 | tf_op jit(solution)/shard_map/ppermute | solution.py:575
  11.3 0.0 copy-start
  11.3 1.0 %copy-done = f32[9,64,128]{2,1,0:T(8,128)S(1)} copy-done((f32[9,64,128]{2,1,0:T(8,128)S(1)}, f32[9,64,128]{2,1,0:T(8,128)}, u32[]{:S(2)}) %copy-start) | copy-done | bytes 294936
  12.2 0.0 collective-permute-done.1.from_other
  12.3 0.1 collective-permute-done.from_one
  12.3 0.1 shard_map.61
  12.4 4.6 %collective-permute-start.2 = (f32[216,128]{1,0:T(8,128)S(1)}, f32[216,128]{1,0:T(8,128)S(1)}, u32[]{:S(2)}, u32[]{:S(2)}) collective-permute-start(f32[216,128]{1,0:T(8,128)S(1)} %get-tuple-element.34), channel_id=1, source_target_pairs={{16,32},{32,16},{48,64},{64,48},{80,96},{96,80},{17,33},{33,17},{4... | collective-permute-start | bytes 331784 | tf_op jit(solution)/shard_map/ppermute | solution.py:575
  17.0 1.9 %collective-permute-start.3 = (f32[216,128]{1,0:T(8,128)S(1)}, f32[216,128]{1,0:T(8,128)S(1)}, u32[]{:S(2)}, u32[]{:S(2)}) collective-permute-start(f32[216,128]{1,0:T(8,128)S(1)} %get-tuple-element.35), channel_id=1, source_target_pairs={{0,16},{16,0},{32,48},{48,32},{64,80},{80,64},{96,112},{112,96},{1... | collective-permute-start | bytes 331784 | tf_op jit(solution)/shard_map/ppermute | solution.py:575
  18.9 1.9 %collective-permute-done.2.from_one = f32[216,128]{1,0:T(8,128)S(1)} collective-permute-done((f32[216,128]{1,0:T(8,128)S(1)}, f32[216,128]{1,0:T(8,128)S(1)}, u32[]{:S(2)}, u32[]{:S(2)}) %collective-permute-start.2) | collective-permute-done | bytes 110624 | tf_op jit(solution)/shard_map/ppermute | solution.py:575
  20.8 3.1 %collective-permute-done.3.from_other = f32[216,128]{1,0:T(8,128)S(1)} collective-permute-done((f32[216,128]{1,0:T(8,128)S(1)}, f32[216,128]{1,0:T(8,128)S(1)}, u32[]{:S(2)}, u32[]{:S(2)}) %collective-permute-start.3) | collective-permute-done | bytes 110624 | tf_op jit(solution)/shard_map/ppermute | solution.py:575
  23.9 0.2 shard_map.62
  24.2 2.2 %collective-permute-start.5 = (f32[288,128]{1,0:T(8,128)S(1)}, f32[288,128]{1,0:T(8,128)S(1)}, u32[]{:S(2)}, u32[]{:S(2)}) collective-permute-start(f32[288,128]{1,0:T(8,128)S(1)} %get-tuple-element.54), channel_id=1, source_target_pairs={{128,256},{256,128},{384,512},{512,384},{640,768},{768,640},{129,2... | collective-permute-start | bytes 442376 | tf_op jit(solution)/shard_map/ppermute | solution.py:575
  26.4 6.2 %collective-permute-start.4 = (f32[288,128]{1,0:T(8,128)S(1)}, f32[288,128]{1,0:T(8,128)S(1)}, u32[]{:S(2)}, u32[]{:S(2)}) collective-permute-start(f32[288,128]{1,0:T(8,128)S(1)} %get-tuple-element.36), channel_id=1, source_target_pairs={{0,128},{128,0},{256,384},{384,256},{512,640},{640,512},{768,896},... | collective-permute-start | bytes 442376 | tf_op jit(solution)/shard_map/ppermute | solution.py:575
  32.6 2.7 %shard_map.63 = (f32[9,8,16,256]{3,2,1,0:T(8,128)S(1)}, f32[8,16,256]{2,1,0:T(8,128)S(1)}, f32[8,16,256]{2,1,0:T(8,128)S(1)}, f32[8,16,256]{2,1,0:T(8,128)S(1)},...) custom-call(f32[9,64,128]{2,1,0:T(8,128)S(1)} %shard_map.60.core, ...), custom_call_target="tpu_custom_call" | custom-call | tf_op jit(solution)/shard_map/pallas_call | solution.py:560
  35.3 0.0 collective-permute-done.5.source
  35.3 1.3 %shard_map.64 = (f32[27,8,8,128]{3,2,1,0:T(8,128)}, f32[3,2,3,2,8,256]{5,4,3,2,1,0:T(8,128)S(1)}) custom-call(f32[288,128]{1,0:T(8,128)S(1)} %collective-permute-done.5.source, f32[9,8,16,256]{3,2,1,0:T(8,128)S(1)} %get-tuple-element.39.refs_0_, f32[8,16,256]{2,1,0:T(8,128)S(1)} %get-tuple-element.40.refs_1_, ...), custom_call_target="tpu_custom_call", output_to_operand_aliasing={{0}: (16, {})} | custom-call | tf_op jit(solution)/shard_map/pallas_call | solution.py:560
  36.7 0.0 collective-permute-done.4.source
  36.7 1.8 %shard_map.65 = (f32[27,8,8,128]{3,2,1,0:T(8,128)}, f32[16,27]{1,0:T(8,128)}) custom-call(f32[288,128]{1,0:T(8,128)S(1)} %collective-permute-done.4.source, f32[9,8,16,256]{3,2,1,0:T(8,128)S(1)} %get-tuple-element.39.refs_0_, f32[8,16,256]{2,1,0:T(8,128)S(1)} %get-tuple-element.40.refs_1_, ...), custom_call_target="tpu_custom_call", output_to_operand_aliasing={{0}: (16, {})} | custom-call | tf_op jit(solution)/shard_map/pallas_call | solution.py:560
  (1 shorter events, 0.0 us)
Async XLA Ops:
  2.8 9.4 %collective-permute-start.1 = (f32[9,8,128]{2,1,0:T(8,128)}, f32[9,8,128]{2,1,0:T(8,128)S(1)}, u32[]{:S(2)}, u32[]{:S(2)}) collective-permute-start(f32[9,8,128]{2,1,0:T(8,128)} %get-tuple-element.32), channel_id=1, source_target_pairs={{1,2},{2,1},{3,4},{4,3},{5,6},{6,5},{7,8},{8,7},{9,10},{10,9},{11,... | collective-permute-start | bytes 110600 | tf_op jit(solution)/shard_map/ppermute | solution.py:575
  4.7 7.6 %collective-permute-start = (f32[9,8,128]{2,1,0:T(8,128)}, f32[9,8,128]{2,1,0:T(8,128)S(1)}, u32[]{:S(2)}, u32[]{:S(2)}) collective-permute-start(f32[9,8,128]{2,1,0:T(8,128)} %get-tuple-element.32), channel_id=1, source_target_pairs={{0,1},{1,0},{2,3},{3,2},{4,5},{5,4},{6,7},{7,6},{8,9},{9,8},{10,11... | collective-permute-start | bytes 110600 | tf_op jit(solution)/shard_map/ppermute | solution.py:575
  11.3 1.0 %copy-start = (f32[9,64,128]{2,1,0:T(8,128)S(1)}, f32[9,64,128]{2,1,0:T(8,128)}, u32[]{:S(2)}) copy-start(f32[9,64,128]{2,1,0:T(8,128)} %get-tuple-element.31.core_hbm) | copy-start | bytes 884740
  12.4 8.4 %collective-permute-start.2 = (f32[216,128]{1,0:T(8,128)S(1)}, f32[216,128]{1,0:T(8,128)S(1)}, u32[]{:S(2)}, u32[]{:S(2)}) collective-permute-start(f32[216,128]{1,0:T(8,128)S(1)} %get-tuple-element.34), channel_id=1, source_target_pairs={{16,32},{32,16},{48,64},{64,48},{80,96},{96,80},{17,33},{33,17},{4... | collective-permute-start | bytes 331784 | tf_op jit(solution)/shard_map/ppermute | solution.py:575
  17.0 6.9 %collective-permute-start.3 = (f32[216,128]{1,0:T(8,128)S(1)}, f32[216,128]{1,0:T(8,128)S(1)}, u32[]{:S(2)}, u32[]{:S(2)}) collective-permute-start(f32[216,128]{1,0:T(8,128)S(1)} %get-tuple-element.35), channel_id=1, source_target_pairs={{0,16},{16,0},{32,48},{48,32},{64,80},{80,64},{96,112},{112,96},{1... | collective-permute-start | bytes 331784 | tf_op jit(solution)/shard_map/ppermute | solution.py:575
  24.2 11.1 %collective-permute-start.5 = (f32[288,128]{1,0:T(8,128)S(1)}, f32[288,128]{1,0:T(8,128)S(1)}, u32[]{:S(2)}, u32[]{:S(2)}) collective-permute-start(f32[288,128]{1,0:T(8,128)S(1)} %get-tuple-element.54), channel_id=1, source_target_pairs={{128,256},{256,128},{384,512},{512,384},{640,768},{768,640},{129,2... | collective-permute-start | bytes 442376 | tf_op jit(solution)/shard_map/ppermute | solution.py:575
  26.4 10.2 %collective-permute-start.4 = (f32[288,128]{1,0:T(8,128)S(1)}, f32[288,128]{1,0:T(8,128)S(1)}, u32[]{:S(2)}, u32[]{:S(2)}) collective-permute-start(f32[288,128]{1,0:T(8,128)S(1)} %get-tuple-element.36), channel_id=1, source_target_pairs={{0,128},{128,0},{256,384},{384,256},{512,640},{640,512},{768,896},... | collective-permute-start | bytes 442376 | tf_op jit(solution)/shard_map/ppermute | solution.py:575

commit v6 on v5

--- a/solution.py
+++ b/solution.py
@@ -130,7 +130,7 @@
     by_side("gy", to_one, to_other, send)
 
 
-def x_kernel(core, beside_z, from_one, from_other, beside_y, corner, to_one, to_other):
+def x_kernel(core, beside_z, from_one, from_other, _, beside_y, corner, to_one, to_other):
     lane = iota((8, 128), 1)
     zero = jnp.zeros((8, 128), F32)
     beside_y[...] = jnp.zeros(beside_y.shape, F32)
@@ -208,6 +208,9 @@
 
 def read(planes, p, f=None, tall=16, shift=0):
     ref, p = planes.at(p, shift)
+    if isinstance(ref, tuple):
+        halves = [half[p] if f is None else half[f, p] for half in ref[: tall // 8]]
+        return halves[0] if tall == 8 else jnp.concatenate(halves, axis=0)
     return ref[p, 0:tall] if f is None else ref[f, p, 0:tall]
 
 
@@ -221,7 +224,10 @@
 
 
 class Block:
-    def __init__(self, inner, outer):
+    def __init__(self, inner, outer, tops):
+        inner = list(inner[:11])
+        for i, top in zip((0, 1, 2, 4, 6), tops):
+            inner[i] = (top, inner[i])
         names = ("ext", "face_x", "near_x", "face_y", "face_z", "near_y", "near_z", "rest", "weight", "once", "twice")
         first = (3, 3, 3, 3, 3, 3, 3, 3, 4, 4, 5)
         for i, name in enumerate(names):
@@ -252,13 +258,24 @@
                 total = total + (face + roll(face, 1, axis))
             write(self.rest, total, p)
 
+    def inner_faces(self, planes):
+        for p in planes:
+            total = self.cells(STORAGE, p)
+            ids, across = self.cells(LAYER, p), self.cells(PY, p)
+            face = harmonic(across, roll(across, -1, 0))
+            write(self.face_y, face, p)
+            write(self.near_y, jnp.where(ids == roll(ids, -1, 0), face, 0.0), p)
+            total = total + (face + roll(face, 1, 0))
+            face = read(self.face_z, p)
+            write(self.rest, total + (face + roll(face, 1, 1)), p)
+
     def diagonal(self, p):
         return read(self.rest, p) + (self.side_x(self.face_x, p - 1) + self.side_x(self.face_x, p))
 
     def weights(self, planes):
         for p in planes:
             total = self.diagonal(p)
-            write(self.weight, (2.0 / 3.0) / jnp.where(total > 0.0, total, 1.0), p)
+            write(self.weight, 2.0 / jnp.where(total > 0.0, total, 1.0), p)
 
     def height(self, p, source):
         return 8 if p in ((1, 12) if source is self.ext else (2, 11)) else 16
@@ -303,7 +320,7 @@
             factor = scale_other if f & 1 else scale
             if f & 2:
                 factor = factor * x_valid
-            updated.append(read(source, p, f, tall) * (1.0 / 3.0) + factor * totals[f])
+            updated.append(read(source, p, f, tall) + factor * totals[f])
         total = (updated[0] + updated[1]) + (updated[2] + updated[3])
         inverse = 1.0 / jnp.where(total > 0.0, total, 1.0)
         for f in range(4):
@@ -369,7 +386,7 @@
         octet = (jnp.where(self.column < 192, self.column, self.column - 256) + 256) // BLOCK - 32
         return (octet + lax.axis_index("gz") * (128 // BLOCK)).astype(F32)
 
-    def coarse_sums(self, planes, parts, sums, changed=None):
+    def coarse_sums(self, planes, parts, sums, changed=None, before=None):
         for oz in range(3):
             for lift in range(2):
                 for f in range(4):
@@ -389,7 +406,10 @@
                                 value = part[oz, lift, spot, 8:16] * ref[f, at, 8:16]
                                 bottom = value if bottom is None else bottom + value
                         ox = 1 if f < 2 else 2 * i
-                        sums[oz, lift, ox, f & 1] = top + (roll(bottom, 4, 0) if f & 1 else bottom)
+                        total = top + (roll(bottom, 4, 0) if f & 1 else bottom)
+                        if before is not None:
+                            total = total + before[oz, lift, ox, f & 1]
+                        sums[oz, lift, ox, f & 1] = total
 
 
 def store_slots(block, planes, smoothed):
@@ -417,20 +437,39 @@
                 smoothed[9 * rz + 3 * ry + rx_none, i] = zero
 
 
-def inner_kernel(core, beside_z, beside_y, corner, *refs):
-    arrays, (sums, parts_ref, held_once, held_twice, smoothed_hbm) = refs[:11], refs[11:16]
-    smoothed, sem = refs[16:]
+def half_faces(ext, face_x, near_x, face_z, near_z):
+    for p in range(8):
+        ids = ext[LAYER, p]
+        if p < 7:
+            face = harmonic(ext[PX, p], ext[PX, p + 1])
+            face_x[p] = face
+            near_x[p] = jnp.where(ids == ext[LAYER, p + 1], face, 0.0)
+        across = ext[PZ, p]
+        face = harmonic(across, roll(across, -1, 1))
+        face_z[p] = face
+        near_z[p] = jnp.where(ids == roll(ids, -1, 1), face, 0.0)
+
+
+def early_kernel(core, beside_z, ext, *faces):
+    for f in ALL:
+        for x in range(8):
+            ext[f, x, :, 0:128] = core[f, 8 * x : 8 * x + 8]
+            ext[f, x, :, 128:256] = unpacked(beside_z[f], x)
+    half_faces(ext, *faces)
+
+
+def inner_kernel(beside_y, corner, *refs):
+    tops, arrays, (sums, parts_ref, held_once, held_twice, smoothed_hbm) = refs[:5], refs[5:16], refs[16:21]
+    smoothed, sem = refs[21:]
     ext = arrays[0]
     for f in ALL:
         for x in range(8):
-            ext[f, x, 0:8, 0:128] = core[f, 8 * x : 8 * x + 8]
-            ext[f, x, 8:16, 0:128] = beside_y[f, 8 * x : 8 * x + 8]
-            ext[f, x, 0:8, 128:256] = unpacked(beside_z[f], x)
-            ext[f, x, 8:16, 128:256] = unpacked(corner[f], x)
-    block = Block(arrays, None)
+            ext[f, x, :, 0:128] = beside_y[f, 8 * x : 8 * x + 8]
+            ext[f, x, :, 128:256] = unpacked(corner[f], x)
+    half_faces(ext, arrays[1], arrays[2], arrays[4], arrays[6])
+    block = Block(arrays, None, tops)
     parts = Planes(parts_ref, None, 3)
-    block.faces_x(range(3, 10))
-    block.faces(range(3, 11))
+    block.inner_faces(range(3, 11))
     block.weights(range(4, 10))
     block.sweep(range(4, 10), block.ext, block.once)
     block.sweep(range(5, 9), block.once, block.twice)
@@ -480,7 +519,7 @@
 
 
 def outer_kernel(last, source, *refs):
-    arrays, (inner_sums, inner_parts, held_once, held_twice, _), refs = refs[:11], refs[11:16], refs[16:]
+    tops, arrays, (inner_sums, inner_parts, held_once, held_twice, _), refs = refs[:5], refs[5:16], refs[16:21], refs[21:]
     if last:
         (first_sums, smoothed_hbm, coarse), refs = refs[:3], refs[3:]
     else:
@@ -489,12 +528,12 @@
     outer_parts, smoothed, sem = refs[:3]
     if last:
         sums = refs[3]
-    block = Block(arrays, outer)
+    block = Block(arrays, outer, tops)
     parts = Planes(inner_parts, outer_parts, 3)
     even = lax.axis_index("gx") % 2 == 0
     high = even if last else jnp.logical_not(even)
     copy = pltpu.make_async_copy(smoothed, smoothed_hbm.at[:, pl.ds(jnp.where(high, 6, 0), 2)], sem)
-    sums[...] = jnp.zeros(sums.shape, F32)
+    before = first_sums if last else inner_sums
 
     def add(side):
         def plane(d):
@@ -521,29 +560,41 @@
         copy.start()
         block.coarse_parts([plane(1)], parts)
         block.coarse_outer_face(plane(0), face(1), parts, outer_parts)
-        block.coarse_sums(sorted(plane(d) for d in (-1, 0, 1)), parts, sums, outer_parts)
+        block.coarse_sums(sorted(plane(d) for d in (-1, 0, 1)), parts, sums, outer_parts, before)
+        for oz in range(3):
+            for lift in range(2):
+                ox = 0 if side else 2
+                sums[oz, lift, ox] = before[oz, lift, ox]
 
     pl.when(high)(lambda: add(1))
     pl.when(jnp.logical_not(high))(lambda: add(0))
     if last:
         spot = iota((16, 256), 1)
         place = (jnp.where(spot < 192, spot, spot - 256) + 256) // BLOCK - 32
+        row = iota((8, 256), 0)
         for oz in range(3):
             total = jnp.zeros((16, 16), F32)
             for lift in range(2):
-                rows = []
-                for oy in range(3):
-                    for ox in range(3):
-                        ey = 0 if oy == 1 else 1
-                        value = inner_sums[oz, lift, ox, ey] + first_sums[oz, lift, ox, ey] + sums[oz, lift, ox, ey]
-                        if oy != 1:
-                            value = value[0:4] if oy == 0 else value[4:8]
-                        rows.append(jnp.sum(value, axis=0, keepdims=True))
-                rows.append(jnp.zeros((7, 256), F32))
+                first = second = jnp.zeros((8, 256), F32)
+                for ox in range(3):
+                    sides = sums[oz, lift, ox, 1]
+                    sides = sides + roll(sides, 1, 0)
+                    sides = sides + roll(sides, 2, 0)
+                    middle = sums[oz, lift, ox, 0]
+                    middle = middle + roll(middle, 4, 0)
+                    middle = middle + roll(middle, 2, 0)
+                    middle = middle + roll(middle, 1, 0)
+                    first = jnp.where(row == ox, roll(sides, ox - 3, 0), first)
+                    first = jnp.where(row == 3 + ox, middle, first)
+                    high = roll(sides, 6 + ox - 7, 0)
+                    if ox < 2:
+                        first = jnp.where(row == 6 + ox, high, first)
+                    else:
+                        second = jnp.where(row == 0, high, second)
                 chosen = (place + lift - (oz - 1) == iota((16, 256), 0)).astype(F32)
                 total = total + lax.dot_general(
                     chosen,
-                    jnp.concatenate(rows, axis=0),
+                    jnp.concatenate([first, second], axis=0),
                     (((1,), (1,)), ((), ())),
                     precision=lax.Precision.HIGHEST,
                     preferred_element_type=F32,
@@ -601,8 +652,10 @@
     rows = (ROWS_Y + ROWS_Y // 8, 128)
     beside_z, to_one, to_other = call(y_kernel, (side, rows, rows), core, one, other)
     one, other = exchange("gy", to_one, to_other)
+    faces = [(7, 8, 256), (7, 8, 256), (8, 8, 256), (8, 8, 256)]
+    tops = call(early_kernel, [(FIELDS, 8, 8, 256)] + faces, core, beside_z)
     rows = (ROWS_X + 96, 128)
-    beside_y, corner, to_one, to_other = call(x_kernel, (block, side, rows, rows), core, beside_z, one, other)
+    beside_y, corner, to_one, to_other = call(x_kernel, (block, side, rows, rows), core, beside_z, one, other, tops[4])
     one, other = exchange("gx", to_one, to_other)
 
     def arrays(planes):
@@ -624,14 +677,16 @@
     whole = (27, 8, 8, 128)
     half = pltpu.VMEM((27, 4, 8, 128), F32)
     held = (4, 2, 16, 256)
-    outs = arrays(lambda first: 14 - 2 * first) + [sums, (3, 2, 8, 16, 256), held, held, whole]
+    halves = arrays(lambda first: 14 - 2 * first)
+    for i, shape in zip((0, 1, 2, 4, 6), [(FIELDS, 8, 8, 256)] + faces):
+        halves[i] = shape
+    outs = halves + [sums, (3, 2, 8, 16, 256), held, held, whole]
     inner = call(
         inner_kernel,
         outs,
-        core,
-        beside_z,
         beside_y,
         corner,
+        *tops,
         out_specs=[VMEM] * 15 + [HBM],
         scratch=[half, pltpu.SemaphoreType.DMA],
     )
@@ -641,23 +696,25 @@
         functools.partial(outer_kernel, False),
         (whole, sums),
         one,
+        *tops,
         *inner,
-        in_specs=[VMEM] * 16 + [HBM],
+        in_specs=[VMEM] * 21 + [HBM],
         out_specs=[HBM, VMEM],
         scratch=scratch,
-        aliases={16: 0},
+        aliases={21: 0},
     )
     smoothed, coarse = call(
         functools.partial(outer_kernel, True),
         (whole, (16, 27)),
         other,
+        *tops,
         *inner[:-1],
         smoothed,
         first_sums,
-        in_specs=[VMEM] * 16 + [HBM, VMEM],
+        in_specs=[VMEM] * 21 + [HBM, VMEM],
         out_specs=[HBM, VMEM],
         scratch=scratch + [pltpu.VMEM(sums, F32)],
-        aliases={16: 0},
+        aliases={21: 0},
     )
     return smoothed, coarse.T.reshape(27, 1, 1, 16)
 

time: 38.8 us -> 38.4 us (0.990)
  waiting for transfers between devices: 5.06 us -> 4.6 us
    ppermute x3, waiting for transfers between devices: 1.87 us -> 1.41 us  [exchange(): lax.ppermute(to_one, axis, one)]
    pallas_call x7 -> x8, Pallas kernels: 8.36 us -> 8.47 us  [call(): pl.pallas_call(kernel, out_shape=[jax.ShapeDtypeStruct(shape, F32) for sh...]
where the time goes in v6:
time: 38.4 us; the launch traced here: 38.1 us
  starting transfers between devices  23.4 us (61%)
  Pallas kernels  8.47 us (22%)
  waiting for transfers between devices  4.6 us (12%)
  local copies, waits for them, and re-layouts  0.96 us (2%)
  between operations  0.76 us (2%)
    ppermute x3, starting transfers between devices, exchange(): lax.ppermute(to_other, axis, other)  14.6 us
    ppermute x3, starting transfers between devices, exchange(): lax.ppermute(to_one, axis, one)  8.77 us
    pallas_call x8, Pallas kernels, call(): pl.pallas_call(kernel, out_shape=[jax.ShapeDtypeStruct(shape, F32) for sh...  8.47 us
    ppermute x3, waiting for transfers between devices, exchange(): lax.ppermute(to_other, axis, other)  3.18 us
    ppermute x3, waiting for transfers between devices, exchange(): lax.ppermute(to_one, axis, one)  1.41 us
    unnamed x2, local copies, waits for them, and re-layouts  0.96 us
  transfers between devices with their start and end apart: 6, of which 3 were waited for; matrix products, arithmetic and copies ran while one was open for 0% of the time, Pallas kernels for 11%

profile of v6, /device:TPU:422, one launch (start us, length us, event | category | flops | bytes accessed | tf_op | source)
XLA Modules:
  0.0 38.1 jit_solution(10751016758039608174)
XLA Ops:
  0.6 2.2 %shard_map.59 = (f32[9,64,128]{2,1,0:T(8,128)}, f32[9,8,128]{2,1,0:T(8,128)}) custom-call(f32[27,64,128]{2,1,0:T(8,128)} %bitcast.7, f32[3,64,128]{2,1,0:T(8,128)} %bitcast.8, f32[64,128]{1,0:T(8,128)} %bitcast.9, s32[64,128]{1,0:T(8,128)} %bitcast.10), custom_call_target="tpu_custom_call" | custom-call | tf_op jit(solution)/shard_map/pallas_call | solution.py:611
  2.8 1.9 %collective-permute-start.1 = (f32[9,8,128]{2,1,0:T(8,128)}, f32[9,8,128]{2,1,0:T(8,128)S(1)}, u32[]{:S(2)}, u32[]{:S(2)}) collective-permute-start(f32[9,8,128]{2,1,0:T(8,128)} %get-tuple-element.37), channel_id=1, source_target_pairs={{1,2},{2,1},{3,4},{4,3},{5,6},{6,5},{7,8},{8,7},{9,10},{10,9},{11,... | collective-permute-start | bytes 110600 | tf_op jit(solution)/shard_map/ppermute | solution.py:626
  4.7 6.5 %collective-permute-start = (f32[9,8,128]{2,1,0:T(8,128)}, f32[9,8,128]{2,1,0:T(8,128)S(1)}, u32[]{:S(2)}, u32[]{:S(2)}) collective-permute-start(f32[9,8,128]{2,1,0:T(8,128)} %get-tuple-element.37), channel_id=1, source_target_pairs={{0,1},{1,0},{2,3},{3,2},{4,5},{5,4},{6,7},{7,6},{8,9},{9,8},{10,11... | collective-permute-start | bytes 110600 | tf_op jit(solution)/shard_map/ppermute | solution.py:626
  11.3 0.0 copy-start
  11.3 1.0 %copy-done = f32[9,64,128]{2,1,0:T(8,128)S(1)} copy-done((f32[9,64,128]{2,1,0:T(8,128)S(1)}, f32[9,64,128]{2,1,0:T(8,128)}, u32[]{:S(2)}) %copy-start) | copy-done | bytes 294936
  12.2 0.0 collective-permute-done.1.from_other
  12.3 0.1 collective-permute-done.from_one
  12.3 0.1 shard_map.61
  12.4 4.6 %collective-permute-start.2 = (f32[216,128]{1,0:T(8,128)S(1)}, f32[216,128]{1,0:T(8,128)S(1)}, u32[]{:S(2)}, u32[]{:S(2)}) collective-permute-start(f32[216,128]{1,0:T(8,128)S(1)} %get-tuple-element.39), channel_id=1, source_target_pairs={{16,32},{32,16},{48,64},{64,48},{80,96},{96,80},{17,33},{33,17},{4... | collective-permute-start | bytes 331784 | tf_op jit(solution)/shard_map/ppermute | solution.py:626
  17.0 1.9 %collective-permute-start.3 = (f32[216,128]{1,0:T(8,128)S(1)}, f32[216,128]{1,0:T(8,128)S(1)}, u32[]{:S(2)}, u32[]{:S(2)}) collective-permute-start(f32[216,128]{1,0:T(8,128)S(1)} %get-tuple-element.40), channel_id=1, source_target_pairs={{0,16},{16,0},{32,48},{48,32},{64,80},{80,64},{96,112},{112,96},{1... | collective-permute-start | bytes 331784 | tf_op jit(solution)/shard_map/ppermute | solution.py:626
  18.9 0.5 %shard_map.62 = (f32[9,8,8,256]{3,2,1,0:T(8,128)S(1)}, f32[7,8,256]{2,1,0:T(8,128)S(1)}, f32[7,8,256]{2,1,0:T(8,128)S(1)}, f32[8,8,256]{2,1,0:T(8,128)S(1)}, f32[8,8,256]{2,1,0:T(8,128)S(1)}) custom-call(f32[9,64,128]{2,1,0:T(8,128)S(1)} %shard_map.60.core, f32[9,8,128]{2,1,0:T(8,128)S(1)} %get-tuple-element.38.beside_z), custom_call_target="tpu_custom_call" | custom-call | tf_op jit(solution)/shard_map/pallas_call | solution.py:611
  19.4 1.4 %collective-permute-done.2.from_one = f32[216,128]{1,0:T(8,128)S(1)} collective-permute-done((f32[216,128]{1,0:T(8,128)S(1)}, f32[216,128]{1,0:T(8,128)S(1)}, u32[]{:S(2)}, u32[]{:S(2)}) %collective-permute-start.2) | collective-permute-done | bytes 110624 | tf_op jit(solution)/shard_map/ppermute | solution.py:626
  20.8 3.1 %collective-permute-done.3.from_other = f32[216,128]{1,0:T(8,128)S(1)} collective-permute-done((f32[216,128]{1,0:T(8,128)S(1)}, f32[216,128]{1,0:T(8,128)S(1)}, u32[]{:S(2)}, u32[]{:S(2)}) %collective-permute-start.3) | collective-permute-done | bytes 110624 | tf_op jit(solution)/shard_map/ppermute | solution.py:626
  23.9 0.2 shard_map.63
  24.2 2.2 %collective-permute-start.5 = (f32[288,128]{1,0:T(8,128)S(1)}, f32[288,128]{1,0:T(8,128)S(1)}, u32[]{:S(2)}, u32[]{:S(2)}) collective-permute-start(f32[288,128]{1,0:T(8,128)S(1)} %get-tuple-element.64), channel_id=1, source_target_pairs={{128,256},{256,128},{384,512},{512,384},{640,768},{768,640},{129,2... | collective-permute-start | bytes 442376 | tf_op jit(solution)/shard_map/ppermute | solution.py:626
  26.4 6.2 %collective-permute-start.4 = (f32[288,128]{1,0:T(8,128)S(1)}, f32[288,128]{1,0:T(8,128)S(1)}, u32[]{:S(2)}, u32[]{:S(2)}) collective-permute-start(f32[288,128]{1,0:T(8,128)S(1)} %get-tuple-element.42), channel_id=1, source_target_pairs={{0,128},{128,0},{256,384},{384,256},{512,640},{640,512},{768,896},... | collective-permute-start | bytes 442376 | tf_op jit(solution)/shard_map/ppermute | solution.py:626
  32.6 2.4 %shard_map.64 = (f32[9,8,8,256]{3,2,1,0:T(8,128)S(1)}, f32[7,8,256]{2,1,0:T(8,128)S(1)}, f32[7,8,256]{2,1,0:T(8,128)S(1)}, f32[8,16,256]{2,1,0:T(8,128)S(1)}, f3...) custom-call(f32[9,64,128]{2,1,0:T(8,128)S(1)} %get-tuple-element.47., ...), custom_call_target="tpu_custom_call" | custom-call | tf_op jit(solution)/shard_map/pallas_call | solution.py:611
  35.0 0.0 collective-permute-done.5.source
  35.1 1.3 %shard_map.65 = (f32[27,8,8,128]{3,2,1,0:T(8,128)}, f32[3,2,3,2,8,256]{5,4,3,2,1,0:T(8,128)S(1)}) custom-call(f32[288,128]{1,0:T(8,128)S(1)} %collective-permute-done.5.source, f32[9,8,8,256]{3,2,1,0:T(8,128)S(1)} %get-tuple-element.43.refs_0_, f32[7,8,256]{2,1,0:T(8,128)S(1)} %get-tuple-element.44.refs_1_, ...), custom_call_target="tpu_custom_call", output_to_operand_aliasing={{0}: (21, {})} | custom-call | tf_op jit(solution)/shard_map/pallas_call | solution.py:611
  36.4 0.0 collective-permute-done.4.source
  36.4 1.8 %shard_map.66 = (f32[27,8,8,128]{3,2,1,0:T(8,128)}, f32[16,27]{1,0:T(8,128)}) custom-call(f32[288,128]{1,0:T(8,128)S(1)} %collective-permute-done.4.source, f32[9,8,8,256]{3,2,1,0:T(8,128)S(1)} %get-tuple-element.43.refs_0_, f32[7,8,256]{2,1,0:T(8,128)S(1)} %get-tuple-element.44.refs_1_, ...), custom_call_target="tpu_custom_call", output_to_operand_aliasing={{0}: (21, {})} | custom-call | tf_op jit(solution)/shard_map/pallas_call | solution.py:611
  (1 shorter events, 0.0 us)
Async XLA Ops:
  2.8 9.4 %collective-permute-start.1 = (f32[9,8,128]{2,1,0:T(8,128)}, f32[9,8,128]{2,1,0:T(8,128)S(1)}, u32[]{:S(2)}, u32[]{:S(2)}) collective-permute-start(f32[9,8,128]{2,1,0:T(8,128)} %get-tuple-element.37), channel_id=1, source_target_pairs={{1,2},{2,1},{3,4},{4,3},{5,6},{6,5},{7,8},{8,7},{9,10},{10,9},{11,... | collective-permute-start | bytes 110600 | tf_op jit(solution)/shard_map/ppermute | solution.py:626
  4.7 7.6 %collective-permute-start = (f32[9,8,128]{2,1,0:T(8,128)}, f32[9,8,128]{2,1,0:T(8,128)S(1)}, u32[]{:S(2)}, u32[]{:S(2)}) collective-permute-start(f32[9,8,128]{2,1,0:T(8,128)} %get-tuple-element.37), channel_id=1, source_target_pairs={{0,1},{1,0},{2,3},{3,2},{4,5},{5,4},{6,7},{7,6},{8,9},{9,8},{10,11... | collective-permute-start | bytes 110600 | tf_op jit(solution)/shard_map/ppermute | solution.py:626
  11.3 1.0 %copy-start = (f32[9,64,128]{2,1,0:T(8,128)S(1)}, f32[9,64,128]{2,1,0:T(8,128)}, u32[]{:S(2)}) copy-start(f32[9,64,128]{2,1,0:T(8,128)} %get-tuple-element.36.core_hbm) | copy-start | bytes 884740
  12.4 8.4 %collective-permute-start.2 = (f32[216,128]{1,0:T(8,128)S(1)}, f32[216,128]{1,0:T(8,128)S(1)}, u32[]{:S(2)}, u32[]{:S(2)}) collective-permute-start(f32[216,128]{1,0:T(8,128)S(1)} %get-tuple-element.39), channel_id=1, source_target_pairs={{16,32},{32,16},{48,64},{64,48},{80,96},{96,80},{17,33},{33,17},{4... | collective-permute-start | bytes 331784 | tf_op jit(solution)/shard_map/ppermute | solution.py:626
  17.0 6.9 %collective-permute-start.3 = (f32[216,128]{1,0:T(8,128)S(1)}, f32[216,128]{1,0:T(8,128)S(1)}, u32[]{:S(2)}, u32[]{:S(2)}) collective-permute-start(f32[216,128]{1,0:T(8,128)S(1)} %get-tuple-element.40), channel_id=1, source_target_pairs={{0,16},{16,0},{32,48},{48,32},{64,80},{80,64},{96,112},{112,96},{1... | collective-permute-start | bytes 331784 | tf_op jit(solution)/shard_map/ppermute | solution.py:626
  24.2 10.9 %collective-permute-start.5 = (f32[288,128]{1,0:T(8,128)S(1)}, f32[288,128]{1,0:T(8,128)S(1)}, u32[]{:S(2)}, u32[]{:S(2)}) collective-permute-start(f32[288,128]{1,0:T(8,128)S(1)} %get-tuple-element.64), channel_id=1, source_target_pairs={{128,256},{256,128},{384,512},{512,384},{640,768},{768,640},{129,2... | collective-permute-start | bytes 442376 | tf_op jit(solution)/shard_map/ppermute | solution.py:626
  26.4 9.9 %collective-permute-start.4 = (f32[288,128]{1,0:T(8,128)S(1)}, f32[288,128]{1,0:T(8,128)S(1)}, u32[]{:S(2)}, u32[]{:S(2)}) collective-permute-start(f32[288,128]{1,0:T(8,128)S(1)} %get-tuple-element.42), channel_id=1, source_target_pairs={{0,128},{128,0},{256,384},{384,256},{512,640},{640,512},{768,896},... | collective-permute-start | bytes 442376 | tf_op jit(solution)/shard_map/ppermute | solution.py:626

commit v7 on v6

--- a/solution.py
+++ b/solution.py
@@ -21,6 +21,8 @@
     + [(0, row, f) for row in (6, 1) for f in FIELDS_XY]
     + [(1, row, f) for row in (7, 0) for f in FIELDS_XY]
 )
+STRIPS = [(2 if f in (PY, PZ, STORAGE) else 3, 1 if f in (PZ, STORAGE) else 2) for f in ALL]
+STARTS = [sum(planes + corners for planes, corners in STRIPS[:f]) for f in range(FIELDS + 1)]
 F32 = jnp.float32
 
 
@@ -170,12 +172,17 @@
             at += 2
             strips = []
             for f in ALL:
-                value = jnp.where((lane >= 48) & (lane < 80), roll(corner[f], -48 if side else 48, 1), beside_z[f])
-                strips.append(roll(value, 80 * f - 48 * side, 1))
-            for v in range(6):
+                planes, corners = STRIPS[f]
+                if side:
+                    start, stop, turn = 128 - 16 * (planes + corners), 128 - 16 * planes, -16 * planes
+                else:
+                    start, stop, turn = 16 * planes, 16 * (planes + corners), 16 * planes
+                value = jnp.where((lane >= start) & (lane < stop), roll(corner[f], turn, 1), beside_z[f])
+                strips.append(roll(value, 16 * STARTS[f + side], 1))
+            for v in range(STARTS[-1] // 8):
                 value = zero
                 for f in ALL:
-                    start, stop = max(5 * f, 8 * v), min(5 * f + 5, 8 * v + 8)
+                    start, stop = max(STARTS[f], 8 * v), min(STARTS[f + 1], 8 * v + 8)
                     if start < stop:
                         inside = (lane >= 16 * (start - 8 * v)) & (lane < 16 * (stop - 8 * v))
                         value = jnp.where(inside, strips[f], value)
@@ -506,16 +513,17 @@
     at += 2
     for f in ALL:
         into = f ^ 2 if f < 4 else f
-        first, last = 5 * f // 8, (5 * f + 4) // 8
+        count, corners = STRIPS[f]
+        first, last = STARTS[f] // 8, (STARTS[f + 1] - 1) // 8
         value = source[at + 8 * first : at + 8 * first + 8]
         if last > first:
-            value = jnp.where(lane >= 16 * (5 * f % 8), value, source[at + 8 * last : at + 8 * last + 8])
-        value = roll(value, 48 * (1 - side) - 80 * f, 1)
-        lateral = roll(value, -48 if side else 48, 1)
+            value = jnp.where(lane >= 16 * (STARTS[f] % 8), value, source[at + 8 * last : at + 8 * last + 8])
+        value = roll(value, -16 * STARTS[f if side else f + 1], 1)
+        lateral = roll(value, -16 * count if side else 16 * count, 1)
         for d in range(3):
             slot = d if side else 7 - d
-            ext[into, planes[d], 0:8, 128:256] = unpacked(value, slot)
-            ext[into, planes[d], 8:16, 128:256] = unpacked(lateral, slot) if d < 2 else zero
+            ext[into, planes[d], 0:8, 128:256] = unpacked(value, slot) if d < count else zero
+            ext[into, planes[d], 8:16, 128:256] = unpacked(lateral, slot) if d < corners else zero
 
 
 def outer_kernel(last, source, *refs):
@@ -654,7 +662,7 @@
     one, other = exchange("gy", to_one, to_other)
     faces = [(7, 8, 256), (7, 8, 256), (8, 8, 256), (8, 8, 256)]
     tops = call(early_kernel, [(FIELDS, 8, 8, 256)] + faces, core, beside_z)
-    rows = (ROWS_X + 96, 128)
+    rows = (ROWS_X + 48 + STARTS[-1], 128)
     beside_y, corner, to_one, to_other = call(x_kernel, (block, side, rows, rows), core, beside_z, one, other, tops[4])
     one, other = exchange("gx", to_one, to_other)
 

time: 38.4 us -> 38.4 us (level)
  no operation moved by 1% of the time
where the time goes in v7:
time: 38.4 us; the launch traced here: 38.1 us
  starting transfers between devices  23.4 us (61%)
  Pallas kernels  8.46 us (22%)
  waiting for transfers between devices  4.6 us (12%)
  local copies, waits for them, and re-layouts  0.96 us (2%)
  between operations  0.76 us (2%)
    ppermute x3, starting transfers between devices, exchange(): lax.ppermute(to_other, axis, other)  14.6 us
    ppermute x3, starting transfers between devices, exchange(): lax.ppermute(to_one, axis, one)  8.77 us
    pallas_call x8, Pallas kernels, call(): pl.pallas_call(kernel, out_shape=[jax.ShapeDtypeStruct(shape, F32) for sh...  8.46 us
    ppermute x3, waiting for transfers between devices, exchange(): lax.ppermute(to_other, axis, other)  3.18 us
    ppermute x3, waiting for transfers between devices, exchange(): lax.ppermute(to_one, axis, one)  1.41 us
    unnamed x2, local copies, waits for them, and re-layouts  0.96 us
  transfers between devices with their start and end apart: 6, of which 3 were waited for; matrix products, arithmetic and copies ran while one was open for 0% of the time, Pallas kernels for 11%

profile of v7, /device:TPU:422, one launch (start us, length us, event | category | flops | bytes accessed | tf_op | source)
XLA Modules:
  0.0 38.1 jit_solution(11692120009392953979)
XLA Ops:
  0.6 2.2 %shard_map.59 = (f32[9,64,128]{2,1,0:T(8,128)}, f32[9,8,128]{2,1,0:T(8,128)}) custom-call(f32[27,64,128]{2,1,0:T(8,128)} %bitcast.7, f32[3,64,128]{2,1,0:T(8,128)} %bitcast.8, f32[64,128]{1,0:T(8,128)} %bitcast.9, s32[64,128]{1,0:T(8,128)} %bitcast.10), custom_call_target="tpu_custom_call" | custom-call | tf_op jit(solution)/shard_map/pallas_call | solution.py:619
  2.8 1.9 %collective-permute-start.1 = (f32[9,8,128]{2,1,0:T(8,128)}, f32[9,8,128]{2,1,0:T(8,128)S(1)}, u32[]{:S(2)}, u32[]{:S(2)}) collective-permute-start(f32[9,8,128]{2,1,0:T(8,128)} %get-tuple-element.37), channel_id=1, source_target_pairs={{1,2},{2,1},{3,4},{4,3},{5,6},{6,5},{7,8},{8,7},{9,10},{10,9},{11,... | collective-permute-start | bytes 110600 | tf_op jit(solution)/shard_map/ppermute | solution.py:634
  4.7 6.5 %collective-permute-start = (f32[9,8,128]{2,1,0:T(8,128)}, f32[9,8,128]{2,1,0:T(8,128)S(1)}, u32[]{:S(2)}, u32[]{:S(2)}) collective-permute-start(f32[9,8,128]{2,1,0:T(8,128)} %get-tuple-element.37), channel_id=1, source_target_pairs={{0,1},{1,0},{2,3},{3,2},{4,5},{5,4},{6,7},{7,6},{8,9},{9,8},{10,11... | collective-permute-start | bytes 110600 | tf_op jit(solution)/shard_map/ppermute | solution.py:634
  11.3 0.0 copy-start
  11.3 1.0 %copy-done = f32[9,64,128]{2,1,0:T(8,128)S(1)} copy-done((f32[9,64,128]{2,1,0:T(8,128)S(1)}, f32[9,64,128]{2,1,0:T(8,128)}, u32[]{:S(2)}) %copy-start) | copy-done | bytes 294936
  12.2 0.0 collective-permute-done.1.from_other
  12.3 0.1 collective-permute-done.from_one
  12.3 0.1 shard_map.61
  12.4 4.6 %collective-permute-start.2 = (f32[216,128]{1,0:T(8,128)S(1)}, f32[216,128]{1,0:T(8,128)S(1)}, u32[]{:S(2)}, u32[]{:S(2)}) collective-permute-start(f32[216,128]{1,0:T(8,128)S(1)} %get-tuple-element.39), channel_id=1, source_target_pairs={{16,32},{32,16},{48,64},{64,48},{80,96},{96,80},{17,33},{33,17},{4... | collective-permute-start | bytes 331784 | tf_op jit(solution)/shard_map/ppermute | solution.py:634
  17.0 1.9 %collective-permute-start.3 = (f32[216,128]{1,0:T(8,128)S(1)}, f32[216,128]{1,0:T(8,128)S(1)}, u32[]{:S(2)}, u32[]{:S(2)}) collective-permute-start(f32[216,128]{1,0:T(8,128)S(1)} %get-tuple-element.40), channel_id=1, source_target_pairs={{0,16},{16,0},{32,48},{48,32},{64,80},{80,64},{96,112},{112,96},{1... | collective-permute-start | bytes 331784 | tf_op jit(solution)/shard_map/ppermute | solution.py:634
  18.9 0.5 %shard_map.62 = (f32[9,8,8,256]{3,2,1,0:T(8,128)S(1)}, f32[7,8,256]{2,1,0:T(8,128)S(1)}, f32[7,8,256]{2,1,0:T(8,128)S(1)}, f32[8,8,256]{2,1,0:T(8,128)S(1)}, f32[8,8,256]{2,1,0:T(8,128)S(1)}) custom-call(f32[9,64,128]{2,1,0:T(8,128)S(1)} %shard_map.60.core, f32[9,8,128]{2,1,0:T(8,128)S(1)} %get-tuple-element.38.beside_z), custom_call_target="tpu_custom_call" | custom-call | tf_op jit(solution)/shard_map/pallas_call | solution.py:619
  19.4 1.4 %collective-permute-done.2.from_one = f32[216,128]{1,0:T(8,128)S(1)} collective-permute-done((f32[216,128]{1,0:T(8,128)S(1)}, f32[216,128]{1,0:T(8,128)S(1)}, u32[]{:S(2)}, u32[]{:S(2)}) %collective-permute-start.2) | collective-permute-done | bytes 110624 | tf_op jit(solution)/shard_map/ppermute | solution.py:634
  20.8 3.1 %collective-permute-done.3.from_other = f32[216,128]{1,0:T(8,128)S(1)} collective-permute-done((f32[216,128]{1,0:T(8,128)S(1)}, f32[216,128]{1,0:T(8,128)S(1)}, u32[]{:S(2)}, u32[]{:S(2)}) %collective-permute-start.3) | collective-permute-done | bytes 110624 | tf_op jit(solution)/shard_map/ppermute | solution.py:634
  23.9 0.2 shard_map.63
  24.2 2.2 %collective-permute-start.5 = (f32[280,128]{1,0:T(8,128)S(1)}, f32[280,128]{1,0:T(8,128)S(1)}, u32[]{:S(2)}, u32[]{:S(2)}) collective-permute-start(f32[280,128]{1,0:T(8,128)S(1)} %get-tuple-element.64), channel_id=1, source_target_pairs={{128,256},{256,128},{384,512},{512,384},{640,768},{768,640},{129,2... | collective-permute-start | bytes 430088 | tf_op jit(solution)/shard_map/ppermute | solution.py:634
  26.4 6.2 %collective-permute-start.4 = (f32[280,128]{1,0:T(8,128)S(1)}, f32[280,128]{1,0:T(8,128)S(1)}, u32[]{:S(2)}, u32[]{:S(2)}) collective-permute-start(f32[280,128]{1,0:T(8,128)S(1)} %get-tuple-element.42), channel_id=1, source_target_pairs={{0,128},{128,0},{256,384},{384,256},{512,640},{640,512},{768,896},... | collective-permute-start | bytes 430088 | tf_op jit(solution)/shard_map/ppermute | solution.py:634
  32.6 2.5 %shard_map.64 = (f32[9,8,8,256]{3,2,1,0:T(8,128)S(1)}, f32[7,8,256]{2,1,0:T(8,128)S(1)}, f32[7,8,256]{2,1,0:T(8,128)S(1)}, f32[8,16,256]{2,1,0:T(8,128)S(1)}, f3...) custom-call(f32[9,64,128]{2,1,0:T(8,128)S(1)} %get-tuple-element.47., ...), custom_call_target="tpu_custom_call" | custom-call | tf_op jit(solution)/shard_map/pallas_call | solution.py:619
  35.1 0.0 collective-permute-done.5.source
  35.1 1.2 %shard_map.65 = (f32[27,8,8,128]{3,2,1,0:T(8,128)}, f32[3,2,3,2,8,256]{5,4,3,2,1,0:T(8,128)S(1)}) custom-call(f32[280,128]{1,0:T(8,128)S(1)} %collective-permute-done.5.source, f32[9,8,8,256]{3,2,1,0:T(8,128)S(1)} %get-tuple-element.43.refs_0_, f32[7,8,256]{2,1,0:T(8,128)S(1)} %get-tuple-element.44.refs_1_, ...), custom_call_target="tpu_custom_call", output_to_operand_aliasing={{0}: (21, {})} | custom-call | tf_op jit(solution)/shard_map/pallas_call | solution.py:619
  36.3 0.0 collective-permute-done.4.source
  36.3 1.8 %shard_map.66 = (f32[27,8,8,128]{3,2,1,0:T(8,128)}, f32[16,27]{1,0:T(8,128)}) custom-call(f32[280,128]{1,0:T(8,128)S(1)} %collective-permute-done.4.source, f32[9,8,8,256]{3,2,1,0:T(8,128)S(1)} %get-tuple-element.43.refs_0_, f32[7,8,256]{2,1,0:T(8,128)S(1)} %get-tuple-element.44.refs_1_, ...), custom_call_target="tpu_custom_call", output_to_operand_aliasing={{0}: (21, {})} | custom-call | tf_op jit(solution)/shard_map/pallas_call | solution.py:619
  (1 shorter events, 0.0 us)
Async XLA Ops:
  2.8 9.4 %collective-permute-start.1 = (f32[9,8,128]{2,1,0:T(8,128)}, f32[9,8,128]{2,1,0:T(8,128)S(1)}, u32[]{:S(2)}, u32[]{:S(2)}) collective-permute-start(f32[9,8,128]{2,1,0:T(8,128)} %get-tuple-element.37), channel_id=1, source_target_pairs={{1,2},{2,1},{3,4},{4,3},{5,6},{6,5},{7,8},{8,7},{9,10},{10,9},{11,... | collective-permute-start | bytes 110600 | tf_op jit(solution)/shard_map/ppermute | solution.py:634
  4.7 7.6 %collective-permute-start = (f32[9,8,128]{2,1,0:T(8,128)}, f32[9,8,128]{2,1,0:T(8,128)S(1)}, u32[]{:S(2)}, u32[]{:S(2)}) collective-permute-start(f32[9,8,128]{2,1,0:T(8,128)} %get-tuple-element.37), channel_id=1, source_target_pairs={{0,1},{1,0},{2,3},{3,2},{4,5},{5,4},{6,7},{7,6},{8,9},{9,8},{10,11... | collective-permute-start | bytes 110600 | tf_op jit(solution)/shard_map/ppermute | solution.py:634
  11.3 1.0 %copy-start = (f32[9,64,128]{2,1,0:T(8,128)S(1)}, f32[9,64,128]{2,1,0:T(8,128)}, u32[]{:S(2)}) copy-start(f32[9,64,128]{2,1,0:T(8,128)} %get-tuple-element.36.core_hbm) | copy-start | bytes 884740
  12.4 8.4 %collective-permute-start.2 = (f32[216,128]{1,0:T(8,128)S(1)}, f32[216,128]{1,0:T(8,128)S(1)}, u32[]{:S(2)}, u32[]{:S(2)}) collective-permute-start(f32[216,128]{1,0:T(8,128)S(1)} %get-tuple-element.39), channel_id=1, source_target_pairs={{16,32},{32,16},{48,64},{64,48},{80,96},{96,80},{17,33},{33,17},{4... | collective-permute-start | bytes 331784 | tf_op jit(solution)/shard_map/ppermute | solution.py:634
  17.0 6.9 %collective-permute-start.3 = (f32[216,128]{1,0:T(8,128)S(1)}, f32[216,128]{1,0:T(8,128)S(1)}, u32[]{:S(2)}, u32[]{:S(2)}) collective-permute-start(f32[216,128]{1,0:T(8,128)S(1)} %get-tuple-element.40), channel_id=1, source_target_pairs={{0,16},{16,0},{32,48},{48,32},{64,80},{80,64},{96,112},{112,96},{1... | collective-permute-start | bytes 331784 | tf_op jit(solution)/shard_map/ppermute | solution.py:634
  24.2 10.9 %collective-permute-start.5 = (f32[280,128]{1,0:T(8,128)S(1)}, f32[280,128]{1,0:T(8,128)S(1)}, u32[]{:S(2)}, u32[]{:S(2)}) collective-permute-start(f32[280,128]{1,0:T(8,128)S(1)} %get-tuple-element.64), channel_id=1, source_target_pairs={{128,256},{256,128},{384,512},{512,384},{640,768},{768,640},{129,2... | collective-permute-start | bytes 430088 | tf_op jit(solution)/shard_map/ppermute | solution.py:634
  26.4 9.9 %collective-permute-start.4 = (f32[280,128]{1,0:T(8,128)S(1)}, f32[280,128]{1,0:T(8,128)S(1)}, u32[]{:S(2)}, u32[]{:S(2)}) collective-permute-start(f32[280,128]{1,0:T(8,128)S(1)} %get-tuple-element.42), channel_id=1, source_target_pairs={{0,128},{128,0},{256,384},{384,256},{512,640},{640,512},{768,896},... | collective-permute-start | bytes 430088 | tf_op jit(solution)/shard_map/ppermute | solution.py:634
